TPU v7x, 32 devices: a whole 2x2x4 slice. The times are simulated.
32 devices in a mesh: joined: 4 (over z), view: 8 (over y, x, core).
Axes of the slice: x: 2, y: 2, z: 4, core: 2. Of those that a mesh axis runs over, the one named last changes fastest.
Arguments:
- estimate: float32 [8, 512, 2048], P('view', 'joined'), may hold values from 0.5 to 2
- views: float32 [8, 4, 512, 2048], P('view', None, 'joined'), may hold values from 0.25 to 4
- psf: float32 [4, 2, 65], replicated, may hold values from 0.2 to 2
- offsets: int32 [4, 2], replicated, may hold values from -16 to 16, as said below
- lengths: int32 [4, 2], replicated, may hold values from 1 to 4, as said below
Outputs:
- deconvolved: float32 [8, 512, 2048], P('view', 'joined')
Inputs may be any that keep to these rules, and one draw needn't show every extreme that they name: `offsets`: offsets along each lateral dimension reach both -16 and 16 in every draw. `lengths`: in every depth block some view has all 4 planes.
All inputs are finite; a program needn't handle non-finite values.
Results may differ from a plain program's by a relative error of at most 0.0001.
Values sent between devices are 32-bit elements; how exact they have to be, the bound alone decides.
No kernel may reach another device: no remote copies, remote signals or barrier semaphores. Data moves between devices by JAX's collectives and lax.ppermute only.
A program may use at most 128 MiB of HBM per device.

v0:
```python
import jax
import jax.numpy as jnp
from jax import lax
from jax.sharding import PartitionSpec as P

MAXD = 16
BLOCKS = 2
YBLOCK = 128


def padded_2(value, sides, width):
    for axis, dim in sides:
        peers, length = (lax.axis_size(axis), value.shape[dim])
        up = [(i, (i + 1) % peers) for i in range(peers)]
        down = [(j, i) for i, j in up]
        last = lax.slice_in_dim(value, length - width, length, axis=dim)
        first = lax.slice_in_dim(value, 0, width, axis=dim)
        before = lax.ppermute(last, axis, up)
        after = lax.ppermute(first, axis, down)
        value = jnp.concatenate([before, value, after], axis=dim)
    return value


def spread_taps(offset, kernel):
    tap_range = jnp.arange(kernel.shape[0], dtype=jnp.int32)
    onehot = (offset[:, :, None] == tap_range[None, None, :]).astype(jnp.float32)
    return jnp.einsum("ijt,t->ij", onehot, kernel, precision=lax.Precision.HIGHEST)


def blur_lateral(field, shift, band, radius, margin):
    depth_rows = field.shape[0]
    tile_rows = field.shape[1]
    lateral_cols = field.shape[2]
    block_cols = band.shape[1]
    block_total = lateral_cols // block_cols
    wrapped = jnp.concatenate(
        [field[:, :, lateral_cols - margin :], field, field[:, :, :margin]], axis=2
    )
    window = lax.dynamic_slice_in_dim(
        wrapped, margin + shift - radius, lateral_cols + 2 * radius, 2
    )
    leading = window[:, :, :lateral_cols].reshape(depth_rows, tile_rows, block_total, block_cols)
    trailing = jnp.concatenate(
        [
            window[:, :, block_cols:],
            jnp.zeros((depth_rows, tile_rows, block_cols - 2 * radius), jnp.float32),
        ],
        axis=2,
    )
    trailing = trailing.reshape(depth_rows, tile_rows, block_total, block_cols)[
        :, :, :, : 2 * radius
    ]
    stacked = jnp.concatenate([leading, trailing], axis=3)
    result = jnp.einsum("zxje,et->zxjt", stacked, band, precision=lax.Precision.HIGHEST)
    return result.reshape(depth_rows, tile_rows, lateral_cols)


def per_device(estimate, views, psf, offsets, lengths):
    owned_rows = estimate.shape[0]
    position = lax.axis_index("view")
    member = position // BLOCKS
    block = position % BLOCKS
    radius = (psf.shape[2] - 1) // 2
    margin = radius + MAXD
    plane_count = views.shape[1]
    tile_cols = views.shape[2]
    lateral_cols = views.shape[3]
    extended = tile_cols + 2 * radius
    widened = YBLOCK + 2 * radius
    highest = lax.Precision.HIGHEST
    kernels = lax.dynamic_index_in_dim(psf, member, 0, keepdims=False)
    kernels = kernels / jnp.sum(kernels, axis=1, keepdims=True)
    shifts = lax.dynamic_index_in_dim(offsets, member, 0, keepdims=False)
    shift_x = shifts[0]
    shift_y = shifts[1]
    member_lengths = lax.dynamic_index_in_dim(lengths, member, 0, keepdims=False)
    own_length = lax.dynamic_index_in_dim(member_lengths, block, 0, keepdims=False)
    band_diff = lax.broadcasted_iota(jnp.int32, (extended, tile_cols), 0) - lax.broadcasted_iota(
        jnp.int32, (extended, tile_cols), 1
    )
    band_forward = spread_taps(band_diff, kernels[0])
    band_back = spread_taps(band_diff, kernels[0][::-1])
    block_diff = lax.broadcasted_iota(jnp.int32, (widened, YBLOCK), 0) - lax.broadcasted_iota(
        jnp.int32, (widened, YBLOCK), 1
    )
    lateral_forward = spread_taps(block_diff, kernels[1])
    lateral_back = spread_taps(block_diff, kernels[1][::-1])
    planes = jnp.arange(plane_count, dtype=jnp.int32)
    live = (planes < own_length).astype(jnp.float32)[:, None, None]
    observed = views[0] * live
    owned_planes = position * owned_rows + jnp.arange(owned_rows, dtype=jnp.int32)
    plane_block = owned_planes // plane_count
    plane_row = owned_planes % plane_count
    block_select = (plane_block[None, :] == jnp.arange(BLOCKS, dtype=jnp.int32)[:, None]).astype(
        jnp.float32
    )
    reached = (plane_row[None, None, :] < lengths[:, :, None]).astype(jnp.float32)
    counts = jnp.sum(reached * block_select[None, :, :], axis=(0, 1))
    current = estimate
    whole = lax.all_gather(current, "view", axis=0, tiled=True)
    mine = lax.dynamic_slice_in_dim(whole, block * plane_count, plane_count, 0)
    padded = padded_2(mine, (("joined", 1),), margin)
    window = lax.dynamic_slice_in_dim(padded, margin + shift_x - radius, extended, 1)
    blurred = jnp.einsum("zey,et->zty", window, band_forward, precision=highest)
    image = blur_lateral(blurred, shift_y, lateral_forward, radius, margin)
    ratio = observed / image
    ratio_padded = padded_2(ratio, (("joined", 1),), margin)
    window = lax.dynamic_slice_in_dim(ratio_padded, margin - shift_x - radius, extended, 1)
    spread_x = jnp.einsum("zey,et->zty", window, band_back, precision=highest)
    correction = blur_lateral(spread_x, -shift_y, lateral_back, radius, margin)
    selector = (jnp.arange(BLOCKS, dtype=jnp.int32) == block).astype(jnp.float32)[
        :, None, None, None
    ]
    placed = (selector * correction[None]).reshape(BLOCKS * plane_count, tile_cols, lateral_cols)
    total = lax.psum_scatter(placed, "view", scatter_dimension=0, tiled=True)
    current = current * total / counts[:, None, None]
    return current


def solution(mesh):
    return jax.shard_map(
        per_device,
        mesh=mesh,
        in_specs=(P("view", "joined", None), P("view", None, "joined", None), P(), P(), P()),
        out_specs=P("view", "joined", None),
        check_vma=False,
    )
```

profile of v0, /device:TPU:0, one launch (start us, length us, event | category | flops | bytes accessed | tf_op | source)
XLA Modules:
  0.0 410.7 jit_solution(5155069206493155227)
XLA Ops:
  6.5 0.7 all-gather.2.cloned.1.call-update
  7.3 0.0 reduce-scatter.2.cloned.1.call-start
  7.3 1.3 dynamic_slice.29
  8.7 0.0 copy-done
  8.7 0.1 constant_dynamic-slice_fusion.6
  8.8 0.6 fusion.48
  9.3 57.1 %all-gather.2.cloned.1.call-done = f32[8,128,2048]{2,1,0:T(8,128)} async-done(((f32[1,128,2048]{2,1,0:T(8,128)}), f32[8,128,2048]{2,1,0:T(8,128)}) %all-gather.2.cloned.1.call-update) | async-done | bytes 8388624 | tf_op jit(solution)/shard_map/all_gather | solution.py:100
  66.4 2.1 constant_dynamic-slice_fusion
  68.5 1.5 collective-permute-start
  70.0 2.3 collective-permute-start.1
  72.3 0.6 compare_convert_fusion.1
  73.0 0.1 fusion.34
  75.6 0.1 bitcast_divide_fusion
  75.7 0.8 iota_compare_fusion
  76.5 2.9 fusion.27
  79.5 0.0 copy-done.10
  79.5 2.9 fusion.25
  82.4 0.3 constant_dynamic-slice_fusion.7
  82.7 25.0 %collective-permute-done = f32[4,48,2048]{2,1,0:T(8,128)} collective-permute-done((f32[4,48,2048]{2,1,0:T(8,128)S(1)}, f32[4,48,2048]{2,1,0:T(8,128)}, u32[]{:S(2)}, u32[]{:S(2)}) %collective-permute-start) | collective-permute-done | bytes 1572896 | tf_op jit(solution)/shard_map/ppermute | solution.py:18
  107.7 32.4 %collective-permute-done.1 = f32[4,48,2048]{2,1,0:T(8,128)} collective-permute-done((f32[4,48,2048]{2,1,0:T(8,128)S(1)}, f32[4,48,2048]{2,1,0:T(8,128)}, u32[]{:S(2)}, u32[]{:S(2)}) %collective-permute-start.1) | collective-permute-done | bytes 1572896 | tf_op jit(solution)/shard_map/ppermute | solution.py:19
  140.1 7.3 %fusion.17 = f32[4,128,2048]{2,1,0:T(8,128)S(1)} fusion(f32[192,128,1]{1,0,2:T(8,128)S(1)} %bitcast.79, s32[]{:T(128)S(6)} %select_n.59, f32[4,48,2048]{2,1,0:T(8,128)} %collective-permute-done, f32[4,128,2048]{2,1,0:T(8,128)S(1)} %constant_dynamic-slice_fusion.7, f32[4,48,2048]{2,1,0:T(8,128)} %collective-permute-done.1), kind=kOutput, calls=%fused_computation.24 | convolution fusion | flops 2419064832 | bytes 11632644 | tf_op jit(solution)/shard_map/zey,et->zty/dot_general | solution.py:104
  147.4 0.0 copy-start.7
  147.4 2.0 copy-done.7
  149.4 0.1 fusion.47
  149.5 6.5 %concatenate.25 = f32[4,128,2144]{2,1,0:T(8,128)} concatenate(f32[4,128,48]{2,1,0:T(8,128)S(1)} %get-tuple-element.12, f32[4,128,2048]{2,1,0:T(8,128)} %copy-done.7, f32[4,128,48]{2,1,0:T(8,128)S(1)} %get-tuple-element.11), dimensions={2} | concatenate | bytes 8781824 | tf_op jit(solution)/shard_map/concatenate | solution.py:36
  156.0 5.6 %constant_dynamic-slice_fusion.5 = f32[4,128,2048]{2,1,0:T(8,128)} fusion(f32[4,128,2144]{2,1,0:T(8,128)} %concatenate.25, s32[]{:T(128)S(6)} %select_n.60), kind=kLoop, calls=%fused_computation.43 | loop fusion | bytes 8388612 | tf_op jit(solution)/shard_map/slice | solution.py:42
  161.6 3.2 constant_dynamic-slice_fusion.4
  164.7 5.3 %copy.35 = f32[4,128,1984]{1,2,0:T(8,128)} copy(f32[4,128,1984]{2,1,0:T(8,128)} %constant_dynamic-slice_fusion.4) | data formatting | bytes 8126464
  170.0 2.5 concatenate.26.clone
  172.5 0.2 slice.78
  172.7 5.3 %copy.31 = f32[4,128,2048]{1,2,0:T(8,128)} copy(f32[4,128,2048]{2,1,0:T(8,128)} %constant_dynamic-slice_fusion.5) | data formatting | bytes 8388608 | tf_op jit(solution)/shard_map/reshape | solution.py:42
  178.1 8.6 %fusion.8 = f32[4,128,16,128]{1,3,2,0:T(8,128)} fusion(f32[192,128,1,1]{1,0,3,2:T(8,128)S(1)} %bitcast.76, f32[4,128,16,64]{1,3,2,0:T(8,128)S(1)} %slice.78, f32[4,128,16,128]{1,3,2,0:T(8,128)} %bitcast.70), kind=kOutput, calls=%fused_computation.14 | convolution fusion | flops 2417491968 | bytes 10584064 | tf_op jit(solution)/shard_map/zxje,et->zxjt/dot_general | solution.py:54
  186.7 5.6 %copy.20 = f32[4,128,2048]{2,1,0:T(8,128)} copy(f32[4,128,2048]{1,2,0:T(8,128)} %bitcast.71) | data formatting | bytes 8388608 | tf_op jit(solution)/shard_map/reshape | solution.py:55
  192.3 4.4 %fusion.16 = f32[4,128,2048]{2,1,0:T(8,128)S(1)} fusion(f32[4,128,2048]{2,1,0:T(8,128)} %copy.20, f32[1,4,128,2048]{3,2,1,0:T(8,128)} %param.6, f32[4]{0:T(128)S(1)} %compare_convert_fusion.1), kind=kLoop, calls=%fused_computation.23 | loop fusion | flops 2097152 | bytes 12582928 | tf_op jit(solution)/shard_map/div | solution.py:106
  196.7 2.0 copy-done.4
  198.7 1.4 fusion.46
  200.0 1.2 collective-permute-start.2
  201.2 2.7 collective-permute-start.3
  205.8 0.1 rev.6
  205.9 0.1 rev.7
  206.0 0.1 mul.44
  206.0 0.1 mul.45
  206.1 2.9 fusion.29
  209.1 2.9 fusion.23
  212.0 27.5 %collective-permute-done.2 = f32[4,48,2048]{2,1,0:T(8,128)} collective-permute-done((f32[4,48,2048]{2,1,0:T(8,128)}, f32[4,48,2048]{2,1,0:T(8,128)}, u32[]{:S(2)}, u32[]{:S(2)}) %collective-permute-start.2) | collective-permute-done | bytes 1572896 | tf_op jit(solution)/shard_map/ppermute | solution.py:18
  239.5 31.6 %collective-permute-done.3 = f32[4,48,2048]{2,1,0:T(8,128)} collective-permute-done((f32[4,48,2048]{2,1,0:T(8,128)S(1)}, f32[4,48,2048]{2,1,0:T(8,128)}, u32[]{:S(2)}, u32[]{:S(2)}) %collective-permute-start.3) | collective-permute-done | bytes 1572896 | tf_op jit(solution)/shard_map/ppermute | solution.py:19
  271.0 7.4 %fusion.20 = f32[4,128,2048]{2,1,0:T(8,128)S(1)} fusion(f32[192,128,1]{1,0,2:T(8,128)S(1)} %bitcast.78, s32[]{:T(128)S(6)} %select_n.61, f32[4,48,2048]{2,1,0:T(8,128)} %collective-permute-done.2, f32[4,128,2048]{2,1,0:T(8,128)S(1)} %copy-done.5, f32[4,48,2048]{2,1,0:T(8,128)} %collective-permute-done.3), kind=kOutput, calls=%fused_computation.25 | convolution fusion | flops 2419064832 | bytes 11632644 | tf_op jit(solution)/shard_map/zey,et->zty/dot_general | solution.py:109
  278.4 1.9 copy-done.8
  280.4 0.1 fusion.45
  280.5 6.6 %concatenate.29 = f32[4,128,2144]{2,1,0:T(8,128)} concatenate(f32[4,128,48]{2,1,0:T(8,128)S(1)} %get-tuple-element.8, f32[4,128,2048]{2,1,0:T(8,128)} %copy-done.8, f32[4,128,48]{2,1,0:T(8,128)S(1)} %get-tuple-element.7), dimensions={2} | concatenate | bytes 8781824 | tf_op jit(solution)/shard_map/concatenate | solution.py:36
  287.1 5.5 %constant_dynamic-slice_fusion.3 = f32[4,128,2048]{2,1,0:T(8,128)} fusion(f32[4,128,2144]{2,1,0:T(8,128)} %concatenate.29, s32[]{:T(128)S(6)} %select_n.62), kind=kLoop, calls=%fused_computation.41 | loop fusion | bytes 8388612 | tf_op jit(solution)/shard_map/slice | solution.py:42
  292.6 3.1 constant_dynamic-slice_fusion.2
  295.7 5.3 %copy.36 = f32[4,128,1984]{1,2,0:T(8,128)} copy(f32[4,128,1984]{2,1,0:T(8,128)} %constant_dynamic-slice_fusion.2) | data formatting | bytes 8126464
  301.0 2.5 concatenate.30.clone
  303.5 0.2 slice.83
  303.7 5.4 %copy.33 = f32[4,128,2048]{1,2,0:T(8,128)} copy(f32[4,128,2048]{2,1,0:T(8,128)} %constant_dynamic-slice_fusion.3) | data formatting | bytes 8388608 | tf_op jit(solution)/shard_map/reshape | solution.py:42
  309.1 8.5 %fusion.12 = f32[4,128,16,128]{1,3,2,0:T(8,128)} fusion(f32[192,128,1,1]{1,0,3,2:T(8,128)S(1)} %bitcast.77, f32[4,128,16,64]{1,3,2,0:T(8,128)S(1)} %slice.83, f32[4,128,16,128]{1,3,2,0:T(8,128)} %bitcast.72), kind=kOutput, calls=%fused_computation.18 | convolution fusion | flops 2417491968 | bytes 10584064 | tf_op jit(solution)/shard_map/zxje,et->zxjt/dot_general | solution.py:54
  317.7 5.4 %copy.23 = f32[4,128,2048]{2,1,0:T(8,128)} copy(f32[4,128,2048]{1,2,0:T(8,128)} %bitcast.73) | data formatting | bytes 8388608 | tf_op jit(solution)/shard_map/mul | solution.py:114
  323.1 6.8 %bitcast_multiply_fusion = f32[8,128,2048]{2,1,0:T(8,128)} fusion(f32[4,128,2048]{2,1,0:T(8,128)} %copy.23, f32[8]{0:T(128)S(1)} %mul.45), kind=kLoop, calls=%fused_computation | loop fusion | flops 2097152 | bytes 12582944 | tf_op jit(solution)/shard_map/mul | solution.py:114
  329.9 0.0 reduce-scatter.2.cloned.1.call-update
  330.0 0.6 copy-done.12
  330.6 0.7 fusion.33
  331.3 69.0 %reduce-scatter.2.cloned.1.call-done = f32[1,128,2048]{2,1,0:T(8,128)} async-done(((f32[8,128,2048]{2,1,0:T(8,128)}), f32[1,128,2048]{2,1,0:T(8,128)}) %reduce-scatter.2.cloned.1.call-update) | async-done | bytes 1048592 | tf_op jit(solution)/shard_map/reduce_scatter | solution.py:115
  400.4 3.0 multiply_divide_fusion
  (26 shorter events, 0.1 us)
Async XLA Ops:
  6.5 2.1 copy-start
  6.5 66.4 %copy-start.13 = (f32[4,2,65]{2,1,0:T(2,128)S(1)}, f32[4,2,65]{2,1,0:T(2,128)}, u32[]{:S(2)}) copy-start(f32[4,2,65]{2,1,0:T(2,128)} %param.7) | copy-start | bytes 6244
  6.5 59.8 %all-gather.2.cloned.1.call-start = ((), (), s32[]{:S(2)}) async-start(), calls=%async_computation.1 | async-start | bytes 9437184 | tf_op jit(solution)/shard_map/all_gather | solution.py:100
  7.3 393.1 %reduce-scatter.2.cloned.1.call-start = ((), (), s32[]{:S(2)}) async-start(), calls=%async_computation.2 | async-start | bytes 9437184 | tf_op jit(solution)/shard_map/reduce_scatter | solution.py:115
  68.5 39.2 %collective-permute-start = (f32[4,48,2048]{2,1,0:T(8,128)S(1)}, f32[4,48,2048]{2,1,0:T(8,128)}, u32[]{:S(2)}, u32[]{:S(2)}) collective-permute-start(f32[4,48,2048]{2,1,0:T(8,128)S(1)} %get-tuple-element.6), channel_id=1, source_target_pairs={{0,8},{8,16},{16,24},{24,0},{1,9},{9,17},{17,25},{25,1},{2,10},{10... | collective-permute-start | bytes 4718600 | tf_op jit(solution)/shard_map/ppermute | solution.py:18
  70.0 70.1 %collective-permute-start.1 = (f32[4,48,2048]{2,1,0:T(8,128)S(1)}, f32[4,48,2048]{2,1,0:T(8,128)}, u32[]{:S(2)}, u32[]{:S(2)}) collective-permute-start(f32[4,48,2048]{2,1,0:T(8,128)S(1)} %get-tuple-element.5), channel_id=1, source_target_pairs={{8,0},{16,8},{24,16},{0,24},{9,1},{17,9},{25,17},{1,25},{10,2},{18... | collective-permute-start | bytes 4718600 | tf_op jit(solution)/shard_map/ppermute | solution.py:19
  76.5 3.0 copy-start.10
  76.5 5.9 %copy-start.6 = (f32[8,128,2048]{2,1,0:T(8,128)S(1)}, f32[8,128,2048]{2,1,0:T(8,128)}, u32[]{:S(2)}) copy-start(f32[8,128,2048]{2,1,0:T(8,128)} %all-gather.2.cloned.1.call-done) | copy-start | bytes 25165828
  147.4 2.0 copy-start.7
  156.0 5.6 %copy-start.2 = (f32[4,128,2144]{2,1,0:T(8,128)S(1)}, f32[4,128,2144]{2,1,0:T(8,128)}, u32[]{:S(2)}) copy-start(f32[4,128,2144]{2,1,0:T(8,128)} %concatenate.25) | copy-start | bytes 13172740
  196.7 2.0 copy-start.4
  198.7 7.5 %copy-start.11 = (pred[192,128,65]{1,0,2:T(32,128)(4,1)S(1)}, pred[192,128,65]{1,0,2:T(32,128)(4,1)}, u32[]{:S(2)}) copy-start(pred[192,128,65]{1,0,2:T(32,128)(4,1)} %copy-done.10) | copy-start | bytes 4792324
  200.0 39.4 %collective-permute-start.2 = (f32[4,48,2048]{2,1,0:T(8,128)}, f32[4,48,2048]{2,1,0:T(8,128)}, u32[]{:S(2)}, u32[]{:S(2)}) collective-permute-start(f32[4,48,2048]{2,1,0:T(8,128)} %get-tuple-element.10), channel_id=1, source_target_pairs={{0,8},{8,16},{16,24},{24,0},{1,9},{9,17},{17,25},{25,1},{2,10},{10... | collective-permute-start | bytes 4718600 | tf_op jit(solution)/shard_map/ppermute | solution.py:18
  201.2 69.9 %collective-permute-start.3 = (f32[4,48,2048]{2,1,0:T(8,128)S(1)}, f32[4,48,2048]{2,1,0:T(8,128)}, u32[]{:S(2)}, u32[]{:S(2)}) collective-permute-start(f32[4,48,2048]{2,1,0:T(8,128)S(1)} %get-tuple-element.9), channel_id=1, source_target_pairs={{8,0},{16,8},{24,16},{0,24},{9,1},{17,9},{25,17},{1,25},{10,2},{18... | collective-permute-start | bytes 4718600 | tf_op jit(solution)/shard_map/ppermute | solution.py:19
  206.1 64.9 %copy-start.5 = (f32[4,128,2048]{2,1,0:T(8,128)S(1)}, f32[4,128,2048]{2,1,0:T(8,128)}, u32[]{:S(2)}) copy-start(f32[4,128,2048]{2,1,0:T(8,128)} %copy-done.4) | copy-start | bytes 12582916
  278.4 1.9 copy-start.8
  287.1 5.5 %copy-start.3 = (f32[4,128,2144]{2,1,0:T(8,128)S(1)}, f32[4,128,2144]{2,1,0:T(8,128)}, u32[]{:S(2)}) copy-start(f32[4,128,2144]{2,1,0:T(8,128)} %concatenate.29) | copy-start | bytes 13172740
  329.9 73.4 %copy-start.1 = (s32[4,2]{0,1:T(2,128)S(1)}, s32[4,2]{0,1:T(2,128)}, u32[]{:S(2)}) copy-start(s32[4,2]{0,1:T(2,128)} %param.8) | copy-start | bytes 100
  329.9 0.7 copy-start.12
  329.9 70.4 %copy-start.9 = (f32[1,128,2048]{2,1,0:T(8,128)S(1)}, f32[1,128,2048]{2,1,0:T(8,128)}, u32[]{:S(2)}) copy-start(f32[1,128,2048]{2,1,0:T(8,128)} %param.5) | copy-start | bytes 3145732
Sparse Core Ops, SparseCore 0:
  9.2 57.0 all-gather.1
  330.1 70.2 reduce-scatter.1
where the time goes:
time: 417 us; the launch traced here: 411 us
  waiting for transfers between devices  243 us (58%)
  local copies, waits for them, and re-layouts  81.1 us (19%)
  matrix products  43.5 us (10%)
  between operations  18.5 us (4%)
  other arithmetic  16.6 us (4%)
  starting transfers between devices  7.74 us (2%)
    reduce_scatter x1, waiting for transfers between devices, per_device(): total = lax.psum_scatter(placed, 'view', scatter_dimension=0, tiled=True)  69 us
    ppermute x2, waiting for transfers between devices, padded_2(): after = lax.ppermute(first, axis, down)  64 us
    all_gather x1, waiting for transfers between devices, per_device(): whole = lax.all_gather(current, 'view', axis=0, tiled=True)  57.1 us
    ppermute x2, waiting for transfers between devices, padded_2(): before = lax.ppermute(last, axis, up)  52.5 us
    unnamed x30, local copies, waits for them, and re-layouts  17.2 us
    dot_general x2, matrix products, blur_lateral(): jnp.einsum('zxje,et->zxjt', stacked, band, precision=lax.Precision.HIGHEST)  17.1 us
    concatenate x2, local copies, waits for them, and re-layouts, blur_lateral(): jnp.concatenate([field[:, :, lateral_cols - margin:], field, field[:, :,...  13.1 us
    dot_general x4, matrix products, spread_taps(): jnp.einsum('ijt,t->ij', onehot, kernel, precision=lax.Precision.HIGHEST)  11.7 us
  transfers between devices with their start and end apart: 6, of which 6 were waited for; matrix products, arithmetic and copies ran while one was open for 4% of the time, Pallas kernels for 0%

commit v1 on v0

v1 whole, which is shorter than its diff:
```python
import functools

import jax
import jax.numpy as jnp
from jax import lax
from jax.experimental import pallas as pl
from jax.experimental.pallas import tpu as pltpu
from jax.sharding import PartitionSpec as P

MAXD = 16
BLOCKS = 2
LANES = 128
F32 = jnp.float32
BF16 = jnp.bfloat16
VMEM_LIMIT = 48 * 1024 * 1024


def split(x):
    hi = x.astype(BF16)
    return hi, (x - hi.astype(F32)).astype(BF16)


def mm(a, b):
    return jnp.dot(a, b, preferred_element_type=F32)


def toeplitz(row, rows, shift, width):
    turned = pltpu.roll(jnp.broadcast_to(row, (8, width)), lax.rem(shift + 4 * width, width), 1)
    wide = jnp.broadcast_to(turned[0:1], (rows, width))
    return pltpu.roll(wide, 0, 1, stride=1, stride_axis=0)


def lateral_factors(row, shift):
    width = row.shape[1]
    left = toeplitz(row, LANES, shift, width)[:, :LANES]
    right = toeplitz(row, LANES, shift + LANES, width)[:, :LANES]
    hi, lo = split(jnp.concatenate([left, right], axis=1))
    return jnp.concatenate([hi, hi], axis=0), lo


def forward_kernel(radius, cut, scal, taps, est, above, below, *rest):
    outs, scratch = rest[:-4], rest[-4:]
    e_hi, e_lo, lhs, _ = scratch
    slot = pl.program_id(0)
    slots = scal.shape[1]
    margin = radius + MAXD
    tile, cols = est.shape
    extended = tile + 2 * margin
    blocks = cols // LANES

    @pl.when(slot == 0)
    def _():
        for piece, at in ((above, 0), (est, margin), (below, margin + tile)):
            rolled = pltpu.roll(piece[...], margin, 1)
            hi, lo = split(rolled)
            e_hi[at : at + piece.shape[0], :] = hi
            e_lo[at : at + piece.shape[0], :] = lo

    dx, dy = scal[0, slot], scal[1, slot]
    live = scal[2, slot].astype(F32)
    width = taps.shape[2]
    gx, gyr = taps[0, 0:1, :], taps[0, 3:4, :]
    band = toeplitz(gx, tile, dx + MAXD, width)[:, :extended]
    b_hi, b_lo = split(band)
    both = mm(jnp.concatenate([b_hi, b_lo], axis=0), e_hi[...])
    blurred = both[:tile] + both[tile:] + mm(b_hi, e_lo[...])
    hi, lo = split(blurred)
    for j in range(blocks):
        at = slice(j * LANES, (j + 1) * LANES)
        lhs[j * tile : (j + 1) * tile, :LANES] = hi[:, at]
        lhs[j * tile : (j + 1) * tile, LANES:] = lo[:, at]
    first, second = lateral_factors(gyr, -dy - MAXD - 2 * radius)
    part = mm(lhs[...], first) + mm(lhs[:, :LANES], second)
    for j in range(blocks):
        n = (j + 1) % blocks
        image = part[j * tile : (j + 1) * tile, :LANES] + part[n * tile : (n + 1) * tile, LANES:]
        value = live / image
        for out, (c0, c1) in zip(outs[:-1], cut):
            if c0 <= j < c1:
                at = slice((j - c0) * LANES, (j - c0 + 1) * LANES)
                out[0, :margin, at] = value[:margin]
                out[0, margin:, at] = value[tile - margin :]
        outs[-1][0, :, j * LANES : (j + 1) * LANES] = value[margin : tile - margin]


def ratio_blurred(slot, value, lhs, taps, dy, radius):
    rows, cols = value.shape
    hi, lo = split(value)
    blocks = cols // LANES
    for j in range(blocks):
        at = slice(j * LANES, (j + 1) * LANES)
        lhs[j * rows : (j + 1) * rows, :LANES] = hi[:, at]
        lhs[j * rows : (j + 1) * rows, LANES:] = lo[:, at]
    first, second = lateral_factors(taps[slot, 2:3, :], dy + MAXD - LANES)
    part = mm(lhs[...], first) + mm(lhs[:, :LANES], second)
    return [part[j * rows : (j + 1) * rows] for j in range(blocks)]


def slot_values(slot, half, kept, sib):
    return kept[slot][0] if slot < half else sib[slot - half]


def edge_kernel(radius, tile, is_first, is_last, half, scal, taps, rim, sib, *rest):
    kept, rest = rest[:half], rest[half:]
    if not is_first:
        (carry_left, *rest) = rest
    if is_last and not is_first:
        (carry_right, *rest) = rest
    main, up, down = rest[:3]
    rest = rest[3:]
    if not is_last:
        (next_left, *rest) = rest
    if is_first and not is_last:
        (next_right, *rest) = rest
    lhs, s_hi, s_lo = rest
    slots = 2 * half
    margin = radius + MAXD
    extended = tile + 2 * margin
    width = taps.shape[2]
    bands = []
    for slot in range(slots):
        dx, dy = scal[0, slot], scal[1, slot]
        value = slot_values(slot, half, kept, sib) * rim[slot]
        parts = ratio_blurred(slot, value, lhs, taps, dy, radius)
        lefts = [x[:, :LANES] for x in parts]
        rights = [x[:, LANES:] for x in parts]
        if not is_first:
            lefts = [carry_left[slot]] + lefts
        else:
            if is_last:
                closing = rights[0]
            else:
                next_right[slot] = rights[0]
            rights = rights[1:]
        if is_last:
            rights = rights + [closing if is_first else carry_right[slot]]
        else:
            next_left[slot] = lefts[-1]
            lefts = lefts[:-1]
        base = slot * tile
        for j, (left, right) in enumerate(zip(lefts, rights)):
            at = slice(j * LANES, (j + 1) * LANES)
            hi, lo = split(left + right)
            for ref, piece in ((s_hi, hi), (s_lo, lo)):
                ref[base : base + margin, at] = piece[:margin]
                ref[base + margin : base + tile - margin, at] = jnp.zeros((tile - 2 * margin, LANES), BF16)
                ref[base + tile - margin : base + tile, at] = piece[margin:]
        gxr = taps[slot, 1:2, :]
        bands.append(toeplitz(gxr, extended, -dx - MAXD - 2 * radius, width)[:, :tile])
    b_hi, b_lo = split(jnp.concatenate(bands, axis=1))
    both = mm(jnp.concatenate([b_hi, b_lo], axis=0), s_hi[...])
    total = both[:extended] + both[extended:] + mm(b_hi, s_lo[...])
    up[...] = total[:margin]
    main[...] = total[margin : margin + tile]
    down[...] = total[margin + tile :]


def final_kernel(radius, tile, half, nchunks, scal, inv, taps, rim, sib, est, *rest):
    kept, rest = rest[:half], rest[half:]
    chunks, rest = rest[: 3 * nchunks], rest[3 * nchunks :]
    out, lhs, s_hi, s_lo, total = rest
    slots = 2 * half
    margin = radius + MAXD
    mid = tile - 2 * margin
    cols = est.shape[1]
    blocks = cols // LANES
    wide = 2 * LANES * max(1, slots * mid // LANES)
    lane = lax.broadcasted_iota(jnp.int32, (tile, wide), 1)
    band = jnp.zeros((tile, wide), F32)
    for slot in range(slots):
        dx, dy = scal[0, slot], scal[1, slot]
        value = slot_values(slot, half, kept, sib) * rim[slot]
        parts = ratio_blurred(slot, value, lhs, taps, dy, radius)
        base = slot * mid
        for j in range(1, blocks + 1):
            at = slice((j - 1) * LANES, j * LANES)
            hi, lo = split(parts[j - 1][:, :LANES] + parts[j % blocks][:, LANES:])
            s_hi[base : base + mid, at] = hi
            s_lo[base : base + mid, at] = lo
        gxr = taps[slot, 1:2, :]
        if wide > gxr.shape[1]:
            gxr = jnp.concatenate([gxr, jnp.zeros((1, wide - gxr.shape[1]), F32)], axis=1)
        line = toeplitz(gxr, tile, base - dx - MAXD - 2 * radius, wide)
        band = jnp.where((lane >= base) & (lane < base + mid), line, band)
    b_hi, b_lo = split(band[:, : slots * mid])
    both = mm(jnp.concatenate([b_hi, b_lo], axis=0), s_hi[...])
    total[...] = both[:tile] + both[tile:] + mm(b_hi, s_lo[...])
    at = 0
    for c in range(nchunks):
        main, above, below = chunks[3 * c : 3 * c + 3]
        w = main.shape[1]
        total[:, at : at + w] += main[...]
        total[:margin, at : at + w] += above[...]
        total[tile - margin :, at : at + w] += below[...]
        at += w
    turned = pltpu.roll(total[...], LANES - margin, 1)
    out[...] = est[...] * turned * inv[0]


def whole_spec(shape):
    return pl.BlockSpec(shape, lambda i, *_: (0,) * len(shape))


def params():
    return pltpu.CompilerParams(vmem_limit_bytes=VMEM_LIMIT, dimension_semantics=("arbitrary",))


def forward(radius, cut, scal, taps, est, above, below):
    slots = taps.shape[0]
    tile, cols = est.shape
    margin = radius + MAXD
    widths = [(c1 - c0) * LANES for c0, c1 in cut]
    shapes = [(slots, 2 * margin, w) for w in widths] + [(slots, tile - 2 * margin, cols)]
    extended = tile + 2 * margin
    return pl.pallas_call(
        functools.partial(forward_kernel, radius, cut),
        grid_spec=pltpu.PrefetchScalarGridSpec(
            num_scalar_prefetch=1,
            grid=(slots,),
            in_specs=[
                pl.BlockSpec((1,) + taps.shape[1:], lambda i, *_: (i, 0, 0)),
                whole_spec(est.shape),
                whole_spec(above.shape),
                whole_spec(below.shape),
            ],
            out_specs=[pl.BlockSpec((1,) + s[1:], lambda i, *_: (i, 0, 0)) for s in shapes],
            scratch_shapes=[
                pltpu.VMEM((extended, cols), BF16),
                pltpu.VMEM((extended, cols), BF16),
                pltpu.VMEM((tile * cols // LANES, 2 * LANES), BF16),
                pltpu.SMEM((1,), jnp.int32),
            ],
        ),
        out_shape=[jax.ShapeDtypeStruct(s, F32) for s in shapes],
        compiler_params=params(),
        name="forward",
    )(scal, taps, est, above, below)


def kept_spec(array):
    shape = (1,) + array.shape[1:]
    return pl.BlockSpec(shape, lambda i, scal, *_: (scal[3, 0], 0, 0))


def edges(radius, tile, is_first, is_last, scal, taps, rim, sib, kept, carries):
    half = len(kept)
    slots = 2 * half
    margin = radius + MAXD
    blocks = rim.shape[2] // LANES
    made = (blocks - (1 if is_first else 0) + (1 if is_last else 0)) * LANES
    shapes = [(tile, made), (margin, made), (margin, made)]
    carried = (slots, 2 * margin, LANES)
    if not is_last:
        shapes.append(carried)
        if is_first:
            shapes.append(carried)
    operands = [taps, rim, sib]
    return pl.pallas_call(
        functools.partial(edge_kernel, radius, tile, is_first, is_last, half),
        grid_spec=pltpu.PrefetchScalarGridSpec(
            num_scalar_prefetch=1,
            grid=(1,),
            in_specs=[whole_spec(x.shape) for x in operands]
            + [kept_spec(x) for x in kept]
            + [whole_spec(x.shape) for x in carries],
            out_specs=[whole_spec(s) for s in shapes],
            scratch_shapes=[
                pltpu.VMEM((blocks * 2 * margin, 2 * LANES), BF16),
                pltpu.VMEM((slots * tile, made), BF16),
                pltpu.VMEM((slots * tile, made), BF16),
            ],
        ),
        out_shape=[jax.ShapeDtypeStruct(s, F32) for s in shapes],
        compiler_params=params(),
        name="edges",
    )(scal, *operands, *kept, *carries)


def finish(radius, scal, inv, taps, rim, sib, est, kept, chunks):
    half = len(kept)
    slots = 2 * half
    margin = radius + MAXD
    tile, cols = est.shape
    mid = tile - 2 * margin
    operands = [taps, rim, sib, est]
    flat = [x for chunk in chunks for x in chunk]
    return pl.pallas_call(
        functools.partial(final_kernel, radius, tile, half, len(chunks)),
        grid_spec=pltpu.PrefetchScalarGridSpec(
            num_scalar_prefetch=2,
            grid=(1,),
            in_specs=[whole_spec(x.shape) for x in operands]
            + [kept_spec(x) for x in kept]
            + [whole_spec(x.shape) for x in flat],
            out_specs=whole_spec(est.shape),
            scratch_shapes=[
                pltpu.VMEM((cols // LANES * mid, 2 * LANES), BF16),
                pltpu.VMEM((slots * mid, cols), BF16),
                pltpu.VMEM((slots * mid, cols), BF16),
                pltpu.VMEM((tile, cols), F32),
            ],
        ),
        out_shape=jax.ShapeDtypeStruct(est.shape, F32),
        compiler_params=params(),
        name="finish",
    )(scal, inv, *operands, *kept, *flat)


def per_device(estimate, views, psf, offsets, lengths):
    size = lax.axis_size("view")
    joined = lax.axis_size("joined")
    position = lax.axis_index("view")
    members = size // BLOCKS
    half = members // 2
    member, block = position // BLOCKS, position % BLOCKS
    planes, tile, cols = views.shape[1:]
    radius = (psf.shape[2] - 1) // 2
    margin = radius + MAXD
    stack = views[0]
    est = estimate[0]
    total_blocks = cols // LANES

    up = [(i, (i + 1) % joined) for i in range(joined)]
    down = [(j, i) for i, j in up]
    above = lax.ppermute(est[tile - margin :], "joined", up)
    below = lax.ppermute(est[:margin], "joined", down)

    pair, core = position // 2, position % 2
    owned_block, place = pair // half, pair % half
    row = position % planes

    def slot_view(c, s):
        return c * half + (place - s - (c == owned_block).astype(jnp.int32)) % half

    order = [slot_view(core, s) for s in range(half)] + [slot_view(1 - core, s) for s in range(half)]
    order = jnp.stack(order).astype(jnp.int32)
    weights = psf / jnp.sum(psf, axis=2, keepdims=True)
    taps = jnp.stack(
        [weights[:, 0], weights[:, 0, ::-1], weights[:, 1], weights[:, 1, ::-1]], axis=1
    )
    taps = jnp.pad(taps, ((0, 0), (0, 0), (0, 2 * LANES - taps.shape[2])))
    taps = taps[order]
    shifts = offsets[order]
    reach = lax.dynamic_index_in_dim(lengths, owned_block, 1, keepdims=False)
    live = (row < reach).astype(jnp.int32)
    inv = (1.0 / jnp.sum(live).astype(F32)).reshape(1)
    scal = jnp.stack(
        [shifts[:, 0], shifts[:, 1], live[order], jnp.full((members,), core, jnp.int32)]
    ).astype(jnp.int32)

    def target(p, s):
        k, b = p // BLOCKS, p % BLOCKS
        t = (k % half + s + (1 if k // half == b else 0)) % half
        return 2 * (b * half + t) + k // half

    def exchange(cut_rows):
        kept = []
        for s in range(half):
            t = (member % half + s + (member // half == block).astype(jnp.int32)) % half
            payload = cut_rows(lax.dynamic_slice_in_dim(stack, 2 * t, 2, 0))
            kept.append(lax.ppermute(payload, "view", [(p, target(p, s)) for p in range(size)]))
        other = jnp.concatenate(
            [lax.dynamic_slice_in_dim(x, 1 - core, 1, 0) for x in kept], axis=0
        )
        return kept, lax.ppermute(other, "view", [(p, p ^ 1) for p in range(size)])

    first = total_blocks * 5 // 8
    cut = ((0, first), (first, total_blocks))

    def edge_rows(c0, c1):
        def take(x):
            x = x[:, :, c0 * LANES : c1 * LANES]
            return jnp.concatenate([x[:, :margin], x[:, tile - margin :]], axis=1)

        return take

    received = [exchange(edge_rows(c0, c1)) for c0, c1 in cut]
    middle = exchange(lambda x: x[:, margin : tile - margin])

    rims = forward(radius, cut, scal, taps, est, above, below)

    chunks, carries, closing = [], [], None
    for i, (kept, sib) in enumerate(received):
        is_first, is_last = i == 0, i == len(cut) - 1
        given = [] if is_first else [carries] + ([closing] if is_last else [])
        result = edges(radius, tile, is_first, is_last, scal, taps, rims[i], sib, kept, given)
        main, upper, lower = result[:3]
        if not is_last:
            carries = result[3]
            if is_first:
                closing = result[4]
        from_above = lax.ppermute(lower, "joined", up)
        from_below = lax.ppermute(upper, "joined", down)
        chunks.append((main, from_above, from_below))
    kept, sib = middle
    out = finish(radius, scal, inv, taps, rims[-1], sib, est, kept, chunks)
    return out[None]


def solution(mesh):
    return jax.shard_map(
        per_device,
        mesh=mesh,
        in_specs=(P("view", "joined", None), P("view", None, "joined", None), P(), P(), P()),
        out_specs=P("view", "joined", None),
        check_vma=False,
    )
```

time: 417 us -> 110 us (0.26); the launches traced: 411 us -> 110 us
  waiting for transfers between devices: 243 us -> 35.4 us
  local copies, waits for them, and re-layouts: 81.1 us -> 18.9 us
  matrix products: 43.5 us -> 0 us
  starting transfers between devices: 7.74 us -> 30.7 us
  Pallas kernels: 0 us -> 20.6 us
  between operations: 18.5 us -> 1.1 us
  other arithmetic: 16.6 us -> 3.16 us
    ppermute x4 -> x15, waiting for transfers between devices: 116 us -> 35.4 us  [the longest x6 28.4 us: exchange(): lax.ppermute(payload, 'view', [(p, target(p, s)) for p in range(size)])]
    reduce_scatter x1 -> x0, waiting for transfers between devices: 69 us -> none  [per_device(): total = lax.psum_scatter(placed, 'view', scatter_dimension=0, tiled=True)]
    all_gather x1 -> x0, waiting for transfers between devices: 57.1 us -> none  [per_device(): whole = lax.all_gather(current, 'view', axis=0, tiled=True)]
    dot_general x8 -> x0, matrix products: 43.5 us -> none  [the longest x2 17.1 us: blur_lateral(): jnp.einsum('zxje,et->zxjt', stacked, band, precision=lax.Precision.HIGHEST)]
    ppermute x4 -> x15, starting transfers between devices: 7.7 us -> 30.7 us  [the longest x3 9.75 us: exchange(): lax.ppermute(other, 'view', [(p, p ^ 1) for p in range(size)])]
    pallas_call x0 -> x4, Pallas kernels: none -> 20.6 us  [the longest x2 8.75 us: edges(): pl.pallas_call(functools.partial(edge_kernel, radius, tile, is_first, is_...]
    concatenate x4 -> x0, local copies, waits for them, and re-layouts: 18 us -> none  [the longest x2 13.1 us: blur_lateral(): jnp.concatenate([field[:, :, lateral_cols - margin:], field, field[:, :,...]
    reshape x3 -> x0, local copies, waits for them, and re-layouts: 16.3 us -> none  [the longest x2 10.7 us: blur_lateral(): window[:, :, :lateral_cols]]
  transfers between devices with their start and end apart: 6 -> 15, of which waited for: 6 -> 5; matrix products, arithmetic and copies ran while one was open for 4% -> 13% of each run, Pallas kernels for 0% -> 15%
where the time goes in v1:
time: 110 us
  waiting for transfers between devices  35.4 us (32%)
  starting transfers between devices  30.7 us (28%)
  Pallas kernels  20.6 us (19%)
  local copies, waits for them, and re-layouts  18.9 us (17%)
  other arithmetic  3.16 us (3%)
  between operations  1.1 us (1%)
    ppermute x6, waiting for transfers between devices, exchange(): lax.ppermute(payload, 'view', [(p, target(p, s)) for p in range(size)])  28.4 us
    ppermute x3, starting transfers between devices, exchange(): lax.ppermute(other, 'view', [(p, p ^ 1) for p in range(size)])  9.75 us
    pallas_call x2, Pallas kernels, edges(): pl.pallas_call(functools.partial(edge_kernel, radius, tile, is_first, is_...  8.75 us
    ppermute x6, starting transfers between devices, exchange(): lax.ppermute(payload, 'view', [(p, target(p, s)) for p in range(size)])  8.01 us
    ppermute x2, starting transfers between devices, per_device(): from_below = lax.ppermute(upper, 'joined', down)  7.71 us
    pallas_call x1, Pallas kernels, forward(): pl.pallas_call(functools.partial(forward_kernel, radius, cut), grid_spec=...  7.37 us
    unnamed x45, local copies, waits for them, and re-layouts  5.95 us
    ppermute x2, waiting for transfers between devices, per_device(): from_above = lax.ppermute(lower, 'joined', up)  5.62 us
  transfers between devices with their start and end apart: 15, of which 5 were waited for; matrix products, arithmetic and copies ran while one was open for 13% of the time, Pallas kernels for 15%

profile of v1, /device:TPU:0, one launch (start us, length us, event | category | flops | bytes accessed | tf_op | source)
XLA Modules:
  0.0 109.9 jit_solution(2766171312810003948)
XLA Ops:
  0.0 2.1 %slice_bitcast_fusion = (f32[48,2048]{1,0:T(8,128)}, f32[48,2048]{1,0:T(8,128)}) fusion(f32[1,128,2048]{2,1,0:T(8,128)} %param.5), kind=kLoop, calls=%fused_computation.12 | loop fusion | bytes 1572864 | tf_op jit(solution)/shard_map/slice | solution.py:326
  2.1 5.0 %collective-permute-start.1 = (f32[48,2048]{1,0:T(8,128)}, f32[48,2048]{1,0:T(8,128)}, u32[]{:S(2)}, u32[]{:S(2)}) collective-permute-start(f32[48,2048]{1,0:T(8,128)} %get-tuple-element.39), channel_id=1, source_target_pairs={{8,0},{16,8},{24,16},{0,24},{9,1},{17,9},{25,17},{1,25},{10,2},{18... | collective-permute-start | bytes 1179656 | tf_op jit(solution)/shard_map/ppermute | solution.py:326
  7.1 0.0 collective-permute-start
  7.1 2.5 %dynamic-slice_bitcast_fusion.1 = (f32[2,128,2048]{2,1,0:T(8,128)S(1)}, f32[2,128,2048]{2,1,0:T(8,128)S(1)}) fusion(f32[1,4,128,2048]{3,2,1,0:T(8,128)} %param.6, s32[]{:T(128)S(6)} %select_n.121, s32[]{:T(128)S(6)} %select_n.124), kind=kLoop, calls=%fused_computation.4 | loop fusion | bytes 8388616 | tf_op jit(solution)/shard_map/dynamic_slice | solution.py:360
  9.6 0.9 slice.95
  10.6 1.7 %collective-permute-start.3 = (f32[2,32,2048]{2,1,0:T(8,128)}, f32[2,32,2048]{2,1,0:T(8,128)S(1)}, u32[]{:S(2)}, u32[]{:S(2)}) collective-permute-start(f32[2,32,2048]{2,1,0:T(8,128)} %slice.95), channel_id=1, source_target_pairs={{0,0},{1,6},{2,2},{3,4},{4,3},{5,5},{6,1},{7,7},{8,8},{9,14},{10,1... | collective-permute-start | bytes 1572872 | tf_op jit(solution)/shard_map/ppermute | solution.py:361
  12.2 0.2 fusion.5
  12.4 0.0 copy-start.16
  12.4 0.0 copy-start.19
  12.4 1.0 pad_maximum_fusion.1
  13.5 2.0 %collective-permute-start.6 = (f32[2,96,1280]{2,1,0:T(8,128)}, f32[2,96,1280]{2,1,0:T(8,128)S(1)}, u32[]{:S(2)}, u32[]{:S(2)}) collective-permute-start(f32[2,96,1280]{2,1,0:T(8,128)} %pad_maximum_fusion.1), channel_id=1, source_target_pairs={{0,0},{1,6},{2,2},{3,4},{4,3},{5,5},{6,1},{7,7},{8,8},{9,14},{10,1... | collective-permute-start | bytes 2949128 | tf_op jit(solution)/shard_map/ppermute | solution.py:361
  15.4 0.1 pad_maximum_fusion
  15.5 1.6 %collective-permute-start.5 = (f32[2,96,1280]{2,1,0:T(8,128)S(1)}, f32[2,96,1280]{2,1,0:T(8,128)S(1)}, u32[]{:S(2)}, u32[]{:S(2)}) collective-permute-start(f32[2,96,1280]{2,1,0:T(8,128)S(1)} %pad_maximum_fusion), channel_id=1, source_target_pairs={{0,2},{1,4},{2,0},{3,6},{4,1},{5,7},{6,3},{7,5},{8,10},{9,12},{10,... | collective-permute-start | bytes 2949128 | tf_op jit(solution)/shard_map/ppermute | solution.py:361
  17.1 0.1 reduce_sum.19
  17.1 0.1 broadcast_divide_fusion
  17.2 0.1 fusion
  17.3 0.1 rev.6
  17.4 0.1 rev.7
  17.6 1.9 %slice.94 = f32[2,32,2048]{2,1,0:T(8,128)} slice(f32[2,128,2048]{2,1,0:T(8,128)} %copy-done.12), slice={[0:2], [48:80], [0:2048]} | slice | bytes 1048576 | tf_op jit(solution)/shard_map/slice | solution.py:378
  19.5 0.7 pad.24.clone
  20.2 0.1 copy.7
  20.3 0.6 gather_fusion.2
  20.8 1.2 %gather_fusion.1 = s32[4]{0:T(128)} fusion(s32[4]{0:T(128)S(1)} %fusion.2, s32[1024]{0:T(1024)S(1)} %pad_clamp_fusion), kind=kCustom, calls=%fused_computation.1 | custom fusion | bytes 48 | tf_op jit(solution)/shard_map/gather | solution.py:348
  22.0 1.1 %gather_fusion = s32[4,2]{1,0:T(4,128)} fusion(s32[4,2]{1,0:T(4,128)S(1)} %copy.7, s32[1024]{0:T(1024)S(1)} %pad_clamp_fusion), kind=kCustom, calls=%fused_computation | custom fusion | bytes 80 | tf_op jit(solution)/shard_map/gather | solution.py:343
  23.1 1.4 %fusion.3 = (f32[2,48,768]{2,1,0:T(8,128)S(1)}, f32[2,48,768]{2,1,0:T(8,128)S(1)}, f32[2,48,768]{2,1,0:T(8,128)S(1)}, f32[2,48,768]{2,1,0:T(8,128)S(1)}) fusion(f32[2,128,2048]{2,1,0:T(8,128)} %copy-done.12, f32[2,128,2048]{2,1,0:T(8,128)} %copy-done.13), kind=kLoop, calls=%fused_computation.32 | loop fusion | bytes 2359296 | tf_op jit(solution)/shard_map/slice | solution.py:373
  24.6 0.0 collective-permute-done.3.rest_1_
  24.6 0.6 collective-permute-start.2
  25.2 0.0 collective-permute-done.6.rest_1_
  25.3 0.7 collective-permute-start.11
  26.0 14.3 %collective-permute-done.5.rest_0_ = f32[2,96,1280]{2,1,0:T(8,128)S(1)} collective-permute-done((f32[2,96,1280]{2,1,0:T(8,128)S(1)}, f32[2,96,1280]{2,1,0:T(8,128)S(1)}, u32[]{:S(2)}, u32[]{:S(2)}) %collective-permute-start.5) | collective-permute-done | bytes 983072 | tf_op jit(solution)/shard_map/ppermute | solution.py:361
  40.3 1.5 %collective-permute-start.10 = (f32[2,96,768]{2,1,0:T(8,128)S(1)}, f32[2,96,768]{2,1,0:T(8,128)S(1)}, u32[]{:S(2)}, u32[]{:S(2)}) collective-permute-start(f32[2,96,768]{2,1,0:T(8,128)S(1)} %pad_maximum_fusion.3), channel_id=1, source_target_pairs={{0,2},{1,4},{2,0},{3,6},{4,1},{5,7},{6,3},{7,5},{8,10},{9,12},{10,... | collective-permute-start | bytes 1769480 | tf_op jit(solution)/shard_map/ppermute | solution.py:361
  41.8 0.1 pad_maximum_fusion.2
  41.9 0.0 copy-start
  41.9 7.0 %collective-permute-done.2.rest_0_ = f32[2,32,2048]{2,1,0:T(8,128)S(1)} collective-permute-done((f32[2,32,2048]{2,1,0:T(8,128)S(1)}, f32[2,32,2048]{2,1,0:T(8,128)S(1)}, u32[]{:S(2)}, u32[]{:S(2)}) %collective-permute-start.2) | collective-permute-done | bytes 524320 | tf_op jit(solution)/shard_map/ppermute | solution.py:361
  48.9 2.2 %collective-permute-start.7 = (f32[2,96,1280]{2,1,0:T(8,128)S(1)}, f32[2,96,1280]{2,1,0:T(8,128)S(1)}, u32[]{:S(2)}, u32[]{:S(2)}) collective-permute-start(f32[2,96,1280]{2,1,0:T(8,128)S(1)} %pad_maximum_fusion.2), channel_id=1, source_target_pairs={{0,1},{1,0},{2,3},{3,2},{4,5},{5,4},{6,7},{7,6},{8,9},{9,8},{10,11... | collective-permute-start | bytes 2949128 | tf_op jit(solution)/shard_map/ppermute | solution.py:365
  51.1 0.0 collective-permute-done.11.rest_1_
  51.1 7.2 %collective-permute-done.10.rest_0_ = f32[2,96,768]{2,1,0:T(8,128)S(1)} collective-permute-done((f32[2,96,768]{2,1,0:T(8,128)S(1)}, f32[2,96,768]{2,1,0:T(8,128)S(1)}, u32[]{:S(2)}, u32[]{:S(2)}) %collective-permute-start.10) | collective-permute-done | bytes 589856 | tf_op jit(solution)/shard_map/ppermute | solution.py:361
  58.4 7.6 %collective-permute-start.12 = (f32[2,96,768]{2,1,0:T(8,128)S(1)}, f32[2,96,768]{2,1,0:T(8,128)S(1)}, u32[]{:S(2)}, u32[]{:S(2)}) collective-permute-start(f32[2,96,768]{2,1,0:T(8,128)S(1)} %pad_maximum_fusion.5), channel_id=1, source_target_pairs={{0,1},{1,0},{2,3},{3,2},{4,5},{5,4},{6,7},{7,6},{8,9},{9,8},{10,11... | collective-permute-start | bytes 1769480 | tf_op jit(solution)/shard_map/ppermute | solution.py:365
  65.9 0.8 pad_maximum_fusion.6
  66.8 0.0 collective-permute-start.4
  66.8 0.2 slice_reduce_fusion.1
  67.0 0.1 add_add_fusion.scal
  67.1 0.0 collective-permute-done.1.below
  67.1 0.0 collective-permute-done.above
  67.1 7.4 %forward.1 = (f32[4,96,1280]{2,1,0:T(8,128)S(1)}, f32[4,96,768]{2,1,0:T(8,128)S(1)}, f32[4,32,2048]{2,1,0:T(8,128)S(1)}) custom-call(s32[4,4]{1,0:T(4,128)S(1)} %add_add_fusion.scal, f32[4,4,256]{2,1,0:T(4,128)S(1)} %gather.15.taps, f32[128,2048]{1,0:T(8,128)S(1)} %bitcast.23, f32[48,2048]{1,0:T(8,128)} %collective-permute-done.above, ...), custom_call_target="tpu_custom_call" | custom-call | tf_op jit(solution)/shard_map/forward/pallas_call | solution.py:215
  74.5 1.3 %copy-done.1 = f32[4,96,1280]{2,1,0:T(8,128)} copy-done((f32[4,96,1280]{2,1,0:T(8,128)}, f32[4,96,1280]{2,1,0:T(8,128)S(1)}, u32[]{:S(2)}) %copy-start.1) | copy-done | bytes 1966104
  75.8 1.0 copy-done.4
  76.7 0.0 collective-permute-done.7.sib
  76.7 5.5 %edges.2 = (f32[128,1152]{1,0:T(8,128)S(1)}, f32[48,1152]{1,0:T(8,128)}, f32[48,1152]{1,0:T(8,128)}, f32[4,96,128]{2,1,0:T(8,128)S(1)}, f32[4,96,128]{2,1,0:T(8,128)S(1)}) custom-call(s32[4,4]{1,0:T(4,128)S(1)} %add_add_fusion.scal, f32[4,4,256]{2,1,0:T(4,128)S(1)} %gather.15.taps, f32[4,96,1280]{2,1,0:T(8,128)} %copy-done.1, ...), custom_call_target="tpu_custom_call" | custom-call | tf_op jit(solution)/shard_map/edges/pallas_call | solution.py:258
  82.2 0.2 collective-permute-start.8
  82.4 3.9 %collective-permute-start.9 = (f32[48,1152]{1,0:T(8,128)}, f32[48,1152]{1,0:T(8,128)}, u32[]{:S(2)}, u32[]{:S(2)}) collective-permute-start(f32[48,1152]{1,0:T(8,128)} %get-tuple-element.20), channel_id=1, source_target_pairs={{8,0},{16,8},{24,16},{0,24},{9,1},{17,9},{25,17},{1,25},{10,2},{18... | collective-permute-start | bytes 663560 | tf_op jit(solution)/shard_map/ppermute | solution.py:393
  86.3 0.0 collective-permute-done.12.sib
  86.3 3.2 %edges.3 = (f32[128,896]{1,0:T(8,128)S(1)}, f32[48,896]{1,0:T(8,128)}, f32[48,896]{1,0:T(8,128)}) custom-call(s32[4,4]{1,0:T(4,128)S(1)} %add_add_fusion.scal, f32[4,4,256]{2,1,0:T(4,128)S(1)} %gather.15.taps, f32[4,96,768]{2,1,0:T(8,128)S(1)} %get-tuple-element.21.rim, f32[2,96,768]{2,1,0:T(8,128)S(1)} %collective-permute-done.12.sib, ...), custom_call_target="tpu_custom_call" | custom-call | tf_op jit(solution)/shard_map/edges/pallas_call | solution.py:258
  89.6 0.8 copy-done.8
  90.4 3.8 %collective-permute-start.14 = (f32[48,896]{1,0:T(8,128)}, f32[48,896]{1,0:T(8,128)}, u32[]{:S(2)}, u32[]{:S(2)}) collective-permute-start(f32[48,896]{1,0:T(8,128)} %get-tuple-element.26), channel_id=1, source_target_pairs={{8,0},{16,8},{24,16},{0,24},{9,1},{17,9},{25,17},{1,25},{10,2},{18... | collective-permute-start | bytes 516104 | tf_op jit(solution)/shard_map/ppermute | solution.py:393
  94.2 0.7 fusion.1
  95.6 0.0 collective-permute-done.4.sib
  95.6 5.6 %collective-permute-done.13.rest_6_ = f32[48,896]{1,0:T(8,128)S(1)} collective-permute-done((f32[48,896]{1,0:T(8,128)}, f32[48,896]{1,0:T(8,128)S(1)}, u32[]{:S(2)}, u32[]{:S(2)}) %collective-permute-start.13) | collective-permute-done | bytes 172064 | tf_op jit(solution)/shard_map/ppermute | solution.py:392
  101.3 1.4 %collective-permute-done.14.rest_7_ = f32[48,896]{1,0:T(8,128)} collective-permute-done((f32[48,896]{1,0:T(8,128)}, f32[48,896]{1,0:T(8,128)}, u32[]{:S(2)}, u32[]{:S(2)}) %collective-permute-start.14) | collective-permute-done | bytes 172064 | tf_op jit(solution)/shard_map/ppermute | solution.py:393
  102.6 0.0 collective-permute-done.8.rest_3_
  102.7 1.1 copy-done.7
  103.7 1.0 copy-done.9
  104.7 0.7 copy-done.11
  105.4 4.5 %finish.1 = f32[128,2048]{1,0:T(8,128)} custom-call(s32[4,4]{1,0:T(4,128)S(1)} %copy-done.11, f32[1]{0:T(128)} %bitcast.7.inv, f32[4,4,256]{2,1,0:T(4,128)S(1)} %gather.15.taps, f32[4,32,2048]{2,1,0:T(8,128)S(1)} %copy-done.5, f32[2,32,2048]{2,1,0:T(8,128)} %collective-permute-done.4.sib, f32[128,2048]{1,0:T(8,128)S(1)} %bitcast.24, ...), custom_call_target="tpu_custom_call" | custom-call | tf_op jit(solution)/shard_map/finish/pallas_call | solution.py:287
  (51 shorter events, 0.4 us)
Async XLA Ops:
  2.1 65.0 %collective-permute-start.1 = (f32[48,2048]{1,0:T(8,128)}, f32[48,2048]{1,0:T(8,128)}, u32[]{:S(2)}, u32[]{:S(2)}) collective-permute-start(f32[48,2048]{1,0:T(8,128)} %get-tuple-element.39), channel_id=1, source_target_pairs={{8,0},{16,8},{24,16},{0,24},{9,1},{17,9},{25,17},{1,25},{10,2},{18... | collective-permute-start | bytes 1179656 | tf_op jit(solution)/shard_map/ppermute | solution.py:326
  7.1 59.9 %collective-permute-start = (f32[48,2048]{1,0:T(8,128)}, f32[48,2048]{1,0:T(8,128)}, u32[]{:S(2)}, u32[]{:S(2)}) collective-permute-start(f32[48,2048]{1,0:T(8,128)} %get-tuple-element.40), channel_id=1, source_target_pairs={{0,8},{8,16},{16,24},{24,0},{1,9},{9,17},{17,25},{25,1},{2,10},{10... | collective-permute-start | bytes 1179656 | tf_op jit(solution)/shard_map/ppermute | solution.py:325
  9.6 2.8 %copy-start.12 = (f32[2,128,2048]{2,1,0:T(8,128)}, f32[2,128,2048]{2,1,0:T(8,128)S(1)}, u32[]{:S(2)}) copy-start(f32[2,128,2048]{2,1,0:T(8,128)S(1)} %get-tuple-element.29) | copy-start | bytes 6291460
  9.6 2.8 %copy-start.13 = (f32[2,128,2048]{2,1,0:T(8,128)}, f32[2,128,2048]{2,1,0:T(8,128)S(1)}, u32[]{:S(2)}) copy-start(f32[2,128,2048]{2,1,0:T(8,128)S(1)} %get-tuple-element.30) | copy-start | bytes 6291460
  10.6 14.0 %collective-permute-start.3 = (f32[2,32,2048]{2,1,0:T(8,128)}, f32[2,32,2048]{2,1,0:T(8,128)S(1)}, u32[]{:S(2)}, u32[]{:S(2)}) collective-permute-start(f32[2,32,2048]{2,1,0:T(8,128)} %slice.95), channel_id=1, source_target_pairs={{0,0},{1,6},{2,2},{3,4},{4,3},{5,5},{6,1},{7,7},{8,8},{9,14},{10,1... | collective-permute-start | bytes 1572872 | tf_op jit(solution)/shard_map/ppermute | solution.py:361
  12.4 4.6 %copy-start.16 = (f32[4,2,65]{2,1,0:T(2,128)S(1)}, f32[4,2,65]{2,1,0:T(2,128)}, u32[]{:S(2)}) copy-start(f32[4,2,65]{2,1,0:T(2,128)} %param.7) | copy-start | bytes 6244
  12.4 5.1 %copy-start.19 = (s32[4,2]{0,1:T(2,128)S(1)}, s32[4,2]{0,1:T(2,128)}, u32[]{:S(2)}) copy-start(s32[4,2]{0,1:T(2,128)} %param.9) | copy-start | bytes 100
  13.5 6.7 %copy-start.18 = (s32[4,2]{0,1:T(2,128)S(1)}, s32[4,2]{0,1:T(2,128)}, u32[]{:S(2)}) copy-start(s32[4,2]{0,1:T(2,128)} %param.8) | copy-start | bytes 100
  13.5 11.8 %collective-permute-start.6 = (f32[2,96,1280]{2,1,0:T(8,128)}, f32[2,96,1280]{2,1,0:T(8,128)S(1)}, u32[]{:S(2)}, u32[]{:S(2)}) collective-permute-start(f32[2,96,1280]{2,1,0:T(8,128)} %pad_maximum_fusion.1), channel_id=1, source_target_pairs={{0,0},{1,6},{2,2},{3,4},{4,3},{5,5},{6,1},{7,7},{8,8},{9,14},{10,1... | collective-permute-start | bytes 2949128 | tf_op jit(solution)/shard_map/ppermute | solution.py:361
  15.5 24.8 %collective-permute-start.5 = (f32[2,96,1280]{2,1,0:T(8,128)S(1)}, f32[2,96,1280]{2,1,0:T(8,128)S(1)}, u32[]{:S(2)}, u32[]{:S(2)}) collective-permute-start(f32[2,96,1280]{2,1,0:T(8,128)S(1)} %pad_maximum_fusion), channel_id=1, source_target_pairs={{0,2},{1,4},{2,0},{3,6},{4,1},{5,7},{6,3},{7,5},{8,10},{9,12},{10,... | collective-permute-start | bytes 2949128 | tf_op jit(solution)/shard_map/ppermute | solution.py:361
  23.1 1.5 %copy-start.14 = (f32[2,32,2048]{2,1,0:T(8,128)S(1)}, f32[2,32,2048]{2,1,0:T(8,128)}, u32[]{:S(2)}) copy-start(f32[2,32,2048]{2,1,0:T(8,128)} %slice.94) | copy-start | bytes 1572868
  24.6 24.3 %collective-permute-start.2 = (f32[2,32,2048]{2,1,0:T(8,128)S(1)}, f32[2,32,2048]{2,1,0:T(8,128)S(1)}, u32[]{:S(2)}, u32[]{:S(2)}) collective-permute-start(f32[2,32,2048]{2,1,0:T(8,128)S(1)} %copy-done.14), channel_id=1, source_target_pairs={{0,2},{1,4},{2,0},{3,6},{4,1},{5,7},{6,3},{7,5},{8,10},{9,12},{10,... | collective-permute-start | bytes 1572872 | tf_op jit(solution)/shard_map/ppermute | solution.py:361
  25.3 25.9 %collective-permute-start.11 = (f32[2,96,768]{2,1,0:T(8,128)S(1)}, f32[2,96,768]{2,1,0:T(8,128)S(1)}, u32[]{:S(2)}, u32[]{:S(2)}) collective-permute-start(f32[2,96,768]{2,1,0:T(8,128)S(1)} %pad_maximum_fusion.4), channel_id=1, source_target_pairs={{0,0},{1,6},{2,2},{3,4},{4,3},{5,5},{6,1},{7,7},{8,8},{9,14},{10,1... | collective-permute-start | bytes 1769480 | tf_op jit(solution)/shard_map/ppermute | solution.py:361
  40.3 18.0 %collective-permute-start.10 = (f32[2,96,768]{2,1,0:T(8,128)S(1)}, f32[2,96,768]{2,1,0:T(8,128)S(1)}, u32[]{:S(2)}, u32[]{:S(2)}) collective-permute-start(f32[2,96,768]{2,1,0:T(8,128)S(1)} %pad_maximum_fusion.3), channel_id=1, source_target_pairs={{0,2},{1,4},{2,0},{3,6},{4,1},{5,7},{6,3},{7,5},{8,10},{9,12},{10,... | collective-permute-start | bytes 1769480 | tf_op jit(solution)/shard_map/ppermute | solution.py:361
  41.9 24.9 %copy-start.15 = (s32[4,2]{1,0:T(4,128)S(1)}, s32[4,2]{1,0:T(4,128)}, u32[]{:S(2)}) copy-start(s32[4,2]{1,0:T(4,128)} %gather_fusion) | copy-start | bytes 100
  41.9 25.1 %copy-start.17 = (s32[4]{0:T(128)S(1)}, s32[4]{0:T(128)}, u32[]{:S(2)}) copy-start(s32[4]{0:T(128)} %gather_fusion.1) | copy-start | bytes 52
  41.9 25.1 %copy-start.21 = (s32[4]{0:T(128)S(1)}, s32[4]{0:T(128)}, u32[]{:S(2)}) copy-start(s32[4]{0:T(128)} %pad.24.clone) | copy-start | bytes 52
  41.9 25.2 %copy-start = (f32[1,128,2048]{2,1,0:T(8,128)S(1)}, f32[1,128,2048]{2,1,0:T(8,128)}, u32[]{:S(2)}) copy-start(f32[1,128,2048]{2,1,0:T(8,128)} %param.5) | copy-start | bytes 3145732
  48.9 25.6 %copy-start.2 = (f32[2,32,2048]{2,1,0:T(8,128)}, f32[2,32,2048]{2,1,0:T(8,128)S(1)}, u32[]{:S(2)}) copy-start(f32[2,32,2048]{2,1,0:T(8,128)S(1)} %collective-permute-done.2.rest_0_) | copy-start | bytes 1572868
  48.9 27.8 %collective-permute-start.7 = (f32[2,96,1280]{2,1,0:T(8,128)S(1)}, f32[2,96,1280]{2,1,0:T(8,128)S(1)}, u32[]{:S(2)}, u32[]{:S(2)}) collective-permute-start(f32[2,96,1280]{2,1,0:T(8,128)S(1)} %pad_maximum_fusion.2), channel_id=1, source_target_pairs={{0,1},{1,0},{2,3},{3,2},{4,5},{5,4},{6,7},{7,6},{8,9},{9,8},{10,11... | collective-permute-start | bytes 2949128 | tf_op jit(solution)/shard_map/ppermute | solution.py:365
  58.4 28.0 %collective-permute-start.12 = (f32[2,96,768]{2,1,0:T(8,128)S(1)}, f32[2,96,768]{2,1,0:T(8,128)S(1)}, u32[]{:S(2)}, u32[]{:S(2)}) collective-permute-start(f32[2,96,768]{2,1,0:T(8,128)S(1)} %pad_maximum_fusion.5), channel_id=1, source_target_pairs={{0,1},{1,0},{2,3},{3,2},{4,5},{5,4},{6,7},{7,6},{8,9},{9,8},{10,11... | collective-permute-start | bytes 1769480 | tf_op jit(solution)/shard_map/ppermute | solution.py:365
  66.8 28.9 %collective-permute-start.4 = (f32[2,32,2048]{2,1,0:T(8,128)}, f32[2,32,2048]{2,1,0:T(8,128)}, u32[]{:S(2)}, u32[]{:S(2)}) collective-permute-start(f32[2,32,2048]{2,1,0:T(8,128)} %pad_maximum_fusion.6), channel_id=1, source_target_pairs={{0,1},{1,0},{2,3},{3,2},{4,5},{5,4},{6,7},{7,6},{8,9},{9,8},{10,11... | collective-permute-start | bytes 1572872 | tf_op jit(solution)/shard_map/ppermute | solution.py:365
  67.0 19.3 %copy-start.10 = (s32[4,4]{1,0:T(4,128)}, s32[4,4]{1,0:T(4,128)S(1)}, u32[]{:S(2)}) copy-start(s32[4,4]{1,0:T(4,128)S(1)} %add_add_fusion.scal) | copy-start | bytes 196
  74.5 1.3 %copy-start.1 = (f32[4,96,1280]{2,1,0:T(8,128)}, f32[4,96,1280]{2,1,0:T(8,128)S(1)}, u32[]{:S(2)}) copy-start(f32[4,96,1280]{2,1,0:T(8,128)S(1)} %get-tuple-element.17.rim) | copy-start | bytes 5898244
  75.8 1.0 copy-start.4
  82.2 7.3 %copy-start.6 = (f32[128,1152]{1,0:T(8,128)}, f32[128,1152]{1,0:T(8,128)S(1)}, u32[]{:S(2)}) copy-start(f32[128,1152]{1,0:T(8,128)S(1)} %get-tuple-element.18.rest_2_) | copy-start | bytes 1769476
  82.2 12.0 %copy-start.20 = (s32[4,2]{0,1:T(2,128)S(1)}, s32[4,2]{0,1:T(2,128)}, u32[]{:S(2)}) copy-start(s32[4,2]{0,1:T(2,128)} %param.9) | copy-start | bytes 100
  82.2 20.4 %copy-start.3 = (f32[2,32,2048]{2,1,0:T(8,128)S(1)}, f32[2,32,2048]{2,1,0:T(8,128)}, u32[]{:S(2)}) copy-start(f32[2,32,2048]{2,1,0:T(8,128)} %copy-done.2) | copy-start | bytes 1572868
  82.2 20.4 %copy-start.5 = (f32[4,32,2048]{2,1,0:T(8,128)S(1)}, f32[4,32,2048]{2,1,0:T(8,128)}, u32[]{:S(2)}) copy-start(f32[4,32,2048]{2,1,0:T(8,128)} %copy-done.4) | copy-start | bytes 3145732
  82.2 20.4 %collective-permute-start.8 = (f32[48,1152]{1,0:T(8,128)}, f32[48,1152]{1,0:T(8,128)S(1)}, u32[]{:S(2)}, u32[]{:S(2)}) collective-permute-start(f32[48,1152]{1,0:T(8,128)} %get-tuple-element.19), channel_id=1, source_target_pairs={{0,8},{8,16},{16,24},{24,0},{1,9},{9,17},{17,25},{25,1},{2,10},{10... | collective-permute-start | bytes 663560 | tf_op jit(solution)/shard_map/ppermute | solution.py:392
  82.4 20.2 %collective-permute-start.9 = (f32[48,1152]{1,0:T(8,128)}, f32[48,1152]{1,0:T(8,128)}, u32[]{:S(2)}, u32[]{:S(2)}) collective-permute-start(f32[48,1152]{1,0:T(8,128)} %get-tuple-element.20), channel_id=1, source_target_pairs={{8,0},{16,8},{24,16},{0,24},{9,1},{17,9},{25,17},{1,25},{10,2},{18... | collective-permute-start | bytes 663560 | tf_op jit(solution)/shard_map/ppermute | solution.py:393
  89.6 0.8 copy-start.8
  90.4 10.9 %collective-permute-start.13 = (f32[48,896]{1,0:T(8,128)}, f32[48,896]{1,0:T(8,128)S(1)}, u32[]{:S(2)}, u32[]{:S(2)}) collective-permute-start(f32[48,896]{1,0:T(8,128)} %get-tuple-element.25), channel_id=1, source_target_pairs={{0,8},{8,16},{16,24},{24,0},{1,9},{9,17},{17,25},{25,1},{2,10},{10... | collective-permute-start | bytes 516104 | tf_op jit(solution)/shard_map/ppermute | solution.py:392
  90.4 12.3 %collective-permute-start.14 = (f32[48,896]{1,0:T(8,128)}, f32[48,896]{1,0:T(8,128)}, u32[]{:S(2)}, u32[]{:S(2)}) collective-permute-start(f32[48,896]{1,0:T(8,128)} %get-tuple-element.26), channel_id=1, source_target_pairs={{8,0},{16,8},{24,16},{0,24},{9,1},{17,9},{25,17},{1,25},{10,2},{18... | collective-permute-start | bytes 516104 | tf_op jit(solution)/shard_map/ppermute | solution.py:393
  102.7 1.1 copy-start.7
  103.7 1.0 copy-start.9
  104.7 0.7 copy-start.11

commit v2 on v1

--- a/solution.py
+++ b/solution.py
@@ -12,7 +12,7 @@
 LANES = 128
 F32 = jnp.float32
 BF16 = jnp.bfloat16
-VMEM_LIMIT = 48 * 1024 * 1024
+VMEM_LIMIT = 28 * 1024 * 1024
 
 
 def split(x):
@@ -38,11 +38,15 @@
     return jnp.concatenate([hi, hi], axis=0), lo
 
 
+def fetch(source, target, sem):
+    copy = pltpu.make_async_copy(source, target, sem)
+    copy.start()
+    return copy
+
+
 def forward_kernel(radius, cut, scal, taps, est, above, below, *rest):
-    outs, scratch = rest[:-4], rest[-4:]
-    e_hi, e_lo, lhs, _ = scratch
+    outs, (e_hi, e_lo, lhs, halo, sems) = rest[:-5], rest[-5:]
     slot = pl.program_id(0)
-    slots = scal.shape[1]
     margin = radius + MAXD
     tile, cols = est.shape
     extended = tile + 2 * margin
@@ -50,11 +54,17 @@
 
     @pl.when(slot == 0)
     def _():
-        for piece, at in ((above, 0), (est, margin), (below, margin + tile)):
-            rolled = pltpu.roll(piece[...], margin, 1)
-            hi, lo = split(rolled)
-            e_hi[at : at + piece.shape[0], :] = hi
-            e_lo[at : at + piece.shape[0], :] = lo
+        copies = [fetch(x, halo.at[i], sems.at[i]) for i, x in enumerate((above, below))]
+        for piece, at, copy in (
+            (est, margin, None),
+            (halo.at[0], 0, copies[0]),
+            (halo.at[1], margin + tile, copies[1]),
+        ):
+            if copy is not None:
+                copy.wait()
+            top, rest = split(pltpu.roll(piece[...], margin, 1))
+            e_hi[at : at + piece.shape[0], :] = top
+            e_lo[at : at + piece.shape[0], :] = rest
 
     dx, dy = scal[0, slot], scal[1, slot]
     live = scal[2, slot].astype(F32)
@@ -78,9 +88,9 @@
         for out, (c0, c1) in zip(outs[:-1], cut):
             if c0 <= j < c1:
                 at = slice((j - c0) * LANES, (j - c0 + 1) * LANES)
-                out[0, :margin, at] = value[:margin]
-                out[0, margin:, at] = value[tile - margin :]
-        outs[-1][0, :, j * LANES : (j + 1) * LANES] = value[margin : tile - margin]
+                out[slot, :margin, at] = value[:margin]
+                out[slot, margin:, at] = value[tile - margin :]
+        outs[-1][slot, :, j * LANES : (j + 1) * LANES] = value[margin : tile - margin]
 
 
 def ratio_blurred(slot, value, lhs, taps, dy, radius):
@@ -96,16 +106,65 @@
     return [part[j * rows : (j + 1) * rows] for j in range(blocks)]
 
 
-def slot_values(slot, half, kept, sib):
-    return kept[slot][0] if slot < half else sib[slot - half]
-
-
-def edge_kernel(radius, tile, is_first, is_last, half, scal, taps, rim, sib, *rest):
-    kept, rest = rest[:half], rest[half:]
+def runs_of(arrays, half, blocks):
+    total = half * blocks
+    marks = [round(total * i / arrays) for i in range(arrays + 1)]
+    result = []
+    for lo, hi in zip(marks, marks[1:]):
+        runs = []
+        for view in range(half):
+            c0, c1 = max(lo, view * blocks), min(hi, (view + 1) * blocks)
+            if c0 < c1:
+                runs.append((view, c0 - view * blocks, c1 - view * blocks))
+        result.append(runs)
+    return result
+
+
+def slot_values(slot, half, runs, mine, sib):
+    if slot < half:
+        return mine[slot][...]
+    parts = []
+    for ref, of_ref in zip(sib, runs):
+        at = 0
+        for view, c0, c1 in of_ref:
+            width = (c1 - c0) * LANES
+            if view == slot - half:
+                parts.append(ref[:, at : at + width])
+            at += width
+    return parts[0] if len(parts) == 1 else jnp.concatenate(parts, axis=1)
+
+
+def pair_kernel(half, runs, scal, *refs):
+    kept, own, refs = refs[:half], refs[half], refs[half + 1 :]
+    (buffer, sem), refs = refs[-2:], refs[:-2]
+    outs = refs[-(half + len(runs)) :]
+    away, inner = scal[half], scal[half + 1]
+
+    @pl.when(inner != 0)
+    def _():
+        copy = fetch(own, buffer, sem.at[0])
+        copy.wait()
+
+    @pl.when(inner == 0)
+    def _():
+        buffer[...] = kept[half - 1][...]
+
+    sources = [*kept[: half - 1], buffer]
+    for s in range(half):
+        outs[s][...] = sources[s][1 - away]
+    for out, of_out in zip(outs[half:], runs):
+        at = 0
+        for view, c0, c1 in of_out:
+            width = (c1 - c0) * LANES
+            out[:, at : at + width] = sources[view][away, :, c0 * LANES : c1 * LANES]
+            at += width
+
+
+def edge_kernel(radius, tile, is_first, is_last, half, runs, scal, taps, rim, *rest):
+    mine, sib, rest = rest[:half], rest[half : half + len(runs)], rest[half + len(runs) :]
+    carries = []
     if not is_first:
-        (carry_left, *rest) = rest
-    if is_last and not is_first:
-        (carry_right, *rest) = rest
+        carries, rest = rest[: 1 + is_last], rest[1 + is_last :]
     main, up, down = rest[:3]
     rest = rest[3:]
     if not is_last:
@@ -120,12 +179,12 @@
     bands = []
     for slot in range(slots):
         dx, dy = scal[0, slot], scal[1, slot]
-        value = slot_values(slot, half, kept, sib) * rim[slot]
+        value = slot_values(slot, half, runs, mine, sib) * rim[slot]
         parts = ratio_blurred(slot, value, lhs, taps, dy, radius)
         lefts = [x[:, :LANES] for x in parts]
         rights = [x[:, LANES:] for x in parts]
         if not is_first:
-            lefts = [carry_left[slot]] + lefts
+            lefts = [carries[0][slot]] + lefts
         else:
             if is_last:
                 closing = rights[0]
@@ -133,7 +192,7 @@
                 next_right[slot] = rights[0]
             rights = rights[1:]
         if is_last:
-            rights = rights + [closing if is_first else carry_right[slot]]
+            rights = rights + [closing if is_first else carries[1][slot]]
         else:
             next_left[slot] = lefts[-1]
             lefts = lefts[:-1]
@@ -155,10 +214,21 @@
     down[...] = total[margin + tile :]
 
 
-def final_kernel(radius, tile, half, nchunks, scal, inv, taps, rim, sib, est, *rest):
-    kept, rest = rest[:half], rest[half:]
+def final_kernel(radius, tile, half, runs, nchunks, scal, inv, taps, rim, est, *rest):
+    mine, sib, rest = rest[:half], rest[half : half + len(runs)], rest[half + len(runs) :]
     chunks, rest = rest[: 3 * nchunks], rest[3 * nchunks :]
-    out, lhs, s_hi, s_lo, total = rest
+    out, lhs, s_hi, s_lo, total, rbuf, field, part, edge, sems = rest
+    first = fetch(rim, rbuf, sems.at[0])
+    late = [fetch(est, field, sems.at[1])]
+    at = 0
+    for c in range(nchunks):
+        main, above, below = chunks[3 * c : 3 * c + 3]
+        w = main.shape[1]
+        late.append(fetch(main, part.at[:, at : at + w], sems.at[2 + 3 * c]))
+        late.append(fetch(above, edge.at[0, :, at : at + w], sems.at[3 + 3 * c]))
+        late.append(fetch(below, edge.at[1, :, at : at + w], sems.at[4 + 3 * c]))
+        at += w
+    first.wait()
     slots = 2 * half
     margin = radius + MAXD
     mid = tile - 2 * margin
@@ -169,7 +239,7 @@
     band = jnp.zeros((tile, wide), F32)
     for slot in range(slots):
         dx, dy = scal[0, slot], scal[1, slot]
-        value = slot_values(slot, half, kept, sib) * rim[slot]
+        value = slot_values(slot, half, runs, mine, sib) * rbuf[slot]
         parts = ratio_blurred(slot, value, lhs, taps, dy, radius)
         base = slot * mid
         for j in range(1, blocks + 1):
@@ -184,17 +254,87 @@
         band = jnp.where((lane >= base) & (lane < base + mid), line, band)
     b_hi, b_lo = split(band[:, : slots * mid])
     both = mm(jnp.concatenate([b_hi, b_lo], axis=0), s_hi[...])
-    total[...] = both[:tile] + both[tile:] + mm(b_hi, s_lo[...])
-    at = 0
-    for c in range(nchunks):
-        main, above, below = chunks[3 * c : 3 * c + 3]
-        w = main.shape[1]
-        total[:, at : at + w] += main[...]
-        total[:margin, at : at + w] += above[...]
-        total[tile - margin :, at : at + w] += below[...]
-        at += w
+    for copy in late:
+        copy.wait()
+    total[...] = both[:tile] + both[tile:] + mm(b_hi, s_lo[...]) + part[...]
+    total[:margin, :] += edge[0]
+    total[tile - margin :, :] += edge[1]
     turned = pltpu.roll(total[...], LANES - margin, 1)
-    out[...] = est[...] * turned * inv[0]
+    out[...] = field[...] * turned * inv[0]
+
+
+def light():
+    return pl.CostEstimate(flops=0, bytes_accessed=1024, transcendentals=0)
+
+
+def pack_kernel(starts, pieces, n_in, *refs):
+    scal, refs = refs[0], refs[1:]
+    ins, outs, sem = refs[:n_in], refs[n_in:-1], refs[-1]
+    copies = []
+    for i, (src, dst, start, src_at, dst_at) in enumerate(pieces):
+        ref = ins[src] if start is None else ins[src].at[pl.ds(scal[start], starts[start])]
+        copies.append(fetch(ref.at[src_at], outs[dst].at[dst_at], sem.at[i]))
+    for copy in copies:
+        copy.wait()
+
+
+def in_vmem():
+    return pl.BlockSpec(memory_space=pltpu.VMEM)
+
+
+def in_hbm():
+    return pl.BlockSpec(memory_space=pltpu.HBM)
+
+
+def anywhere():
+    return pl.BlockSpec(memory_space=pl.ANY)
+
+
+def from_vmem(operands):
+    return [pltpu.with_memory_space_constraint(x, pltpu.VMEM) for x in operands]
+
+
+def from_hbm(operands):
+    return [pltpu.with_memory_space_constraint(x, pltpu.HBM) for x in operands]
+
+
+def pack(scal, starts, ins, after, shapes, pieces, name):
+    return pl.pallas_call(
+        functools.partial(pack_kernel, starts, pieces, len(ins) + len(after)),
+        grid_spec=pltpu.PrefetchScalarGridSpec(
+            num_scalar_prefetch=1,
+            grid=(1,),
+            in_specs=[in_hbm()] * len(ins) + [anywhere()] * len(after),
+            out_specs=[in_vmem()] * len(shapes),
+            scratch_shapes=[pltpu.SemaphoreType.DMA((len(pieces),))],
+        ),
+        out_shape=[jax.ShapeDtypeStruct(s, F32) for s in shapes],
+        compiler_params=params(),
+        cost_estimate=light(),
+        name=name,
+    )(scal, *from_hbm(ins), *after)
+
+
+def part_pair(scal, runs, kept, own, after):
+    half = len(kept)
+    rows, cols = own.shape[1:]
+    shapes = [(rows, cols)] * half
+    shapes += [(rows, sum(c1 - c0 for _, c0, c1 in of) * LANES) for of in runs]
+    out = pl.pallas_call(
+        functools.partial(pair_kernel, half, runs),
+        grid_spec=pltpu.PrefetchScalarGridSpec(
+            num_scalar_prefetch=1,
+            grid=(1,),
+            in_specs=[in_vmem()] * half + [in_hbm()] + [anywhere()] * len(after),
+            out_specs=[in_vmem()] * len(shapes),
+            scratch_shapes=[pltpu.VMEM(own.shape, F32), pltpu.SemaphoreType.DMA((1,))],
+        ),
+        out_shape=[jax.ShapeDtypeStruct(s, F32) for s in shapes],
+        compiler_params=params(),
+        cost_estimate=light(),
+        name="pair",
+    )(scal, *from_vmem(kept), *from_hbm([own]), *after)
+    return out[:half], out[half:]
 
 
 def whole_spec(shape):
@@ -217,33 +357,26 @@
         grid_spec=pltpu.PrefetchScalarGridSpec(
             num_scalar_prefetch=1,
             grid=(slots,),
-            in_specs=[
-                pl.BlockSpec((1,) + taps.shape[1:], lambda i, *_: (i, 0, 0)),
-                whole_spec(est.shape),
-                whole_spec(above.shape),
-                whole_spec(below.shape),
-            ],
-            out_specs=[pl.BlockSpec((1,) + s[1:], lambda i, *_: (i, 0, 0)) for s in shapes],
+            in_specs=[pl.BlockSpec((1,) + taps.shape[1:], lambda i, *_: (i, 0, 0))]
+            + [in_vmem(), in_hbm(), in_hbm()],
+            out_specs=[in_vmem()] * len(shapes),
             scratch_shapes=[
                 pltpu.VMEM((extended, cols), BF16),
                 pltpu.VMEM((extended, cols), BF16),
                 pltpu.VMEM((tile * cols // LANES, 2 * LANES), BF16),
-                pltpu.SMEM((1,), jnp.int32),
+                pltpu.VMEM((2, margin, cols), F32),
+                pltpu.SemaphoreType.DMA((2,)),
             ],
         ),
         out_shape=[jax.ShapeDtypeStruct(s, F32) for s in shapes],
         compiler_params=params(),
+        cost_estimate=light(),
         name="forward",
-    )(scal, taps, est, above, below)
-
-
-def kept_spec(array):
-    shape = (1,) + array.shape[1:]
-    return pl.BlockSpec(shape, lambda i, scal, *_: (scal[3, 0], 0, 0))
-
-
-def edges(radius, tile, is_first, is_last, scal, taps, rim, sib, kept, carries):
-    half = len(kept)
+    )(scal, taps, *from_vmem([est]), *from_hbm([above, below]))
+
+
+def edges(radius, tile, is_first, is_last, runs, scal, taps, rim, mine, sib, carries):
+    half = len(mine)
     slots = 2 * half
     margin = radius + MAXD
     blocks = rim.shape[2] // LANES
@@ -254,16 +387,14 @@
         shapes.append(carried)
         if is_first:
             shapes.append(carried)
-    operands = [taps, rim, sib]
+    operands = [rim, *mine, *sib, *carries]
     return pl.pallas_call(
-        functools.partial(edge_kernel, radius, tile, is_first, is_last, half),
+        functools.partial(edge_kernel, radius, tile, is_first, is_last, half, runs),
         grid_spec=pltpu.PrefetchScalarGridSpec(
             num_scalar_prefetch=1,
             grid=(1,),
-            in_specs=[whole_spec(x.shape) for x in operands]
-            + [kept_spec(x) for x in kept]
-            + [whole_spec(x.shape) for x in carries],
-            out_specs=[whole_spec(s) for s in shapes],
+            in_specs=[whole_spec(taps.shape)] + [in_vmem()] * len(operands),
+            out_specs=[in_vmem()] * len(shapes),
             scratch_shapes=[
                 pltpu.VMEM((blocks * 2 * margin, 2 * LANES), BF16),
                 pltpu.VMEM((slots * tile, made), BF16),
@@ -272,38 +403,44 @@
         ),
         out_shape=[jax.ShapeDtypeStruct(s, F32) for s in shapes],
         compiler_params=params(),
+        cost_estimate=light(),
         name="edges",
-    )(scal, *operands, *kept, *carries)
-
-
-def finish(radius, scal, inv, taps, rim, sib, est, kept, chunks):
-    half = len(kept)
+    )(scal, taps, *from_vmem(operands))
+
+
+def finish(radius, runs, scal, inv, taps, rim, est, mine, sib, chunks):
+    half = len(mine)
     slots = 2 * half
     margin = radius + MAXD
     tile, cols = est.shape
     mid = tile - 2 * margin
-    operands = [taps, rim, sib, est]
     flat = [x for chunk in chunks for x in chunk]
     return pl.pallas_call(
-        functools.partial(final_kernel, radius, tile, half, len(chunks)),
+        functools.partial(final_kernel, radius, tile, half, runs, len(chunks)),
         grid_spec=pltpu.PrefetchScalarGridSpec(
             num_scalar_prefetch=2,
             grid=(1,),
-            in_specs=[whole_spec(x.shape) for x in operands]
-            + [kept_spec(x) for x in kept]
-            + [whole_spec(x.shape) for x in flat],
+            in_specs=[whole_spec(taps.shape), in_hbm(), in_hbm()]
+            + [in_vmem()] * (half + len(runs))
+            + [in_hbm()] * len(flat),
             out_specs=whole_spec(est.shape),
             scratch_shapes=[
                 pltpu.VMEM((cols // LANES * mid, 2 * LANES), BF16),
                 pltpu.VMEM((slots * mid, cols), BF16),
                 pltpu.VMEM((slots * mid, cols), BF16),
                 pltpu.VMEM((tile, cols), F32),
+                pltpu.VMEM(rim.shape, F32),
+                pltpu.VMEM((tile, cols), F32),
+                pltpu.VMEM((tile, cols), F32),
+                pltpu.VMEM((2, margin, cols), F32),
+                pltpu.SemaphoreType.DMA((2 + len(flat),)),
             ],
         ),
         out_shape=jax.ShapeDtypeStruct(est.shape, F32),
         compiler_params=params(),
+        cost_estimate=light(),
         name="finish",
-    )(scal, inv, *operands, *kept, *flat)
+    )(scal, inv, taps, *from_hbm([rim, est]), *from_vmem([*mine, *sib]), *from_hbm(flat))
 
 
 def per_device(estimate, views, psf, offsets, lengths):
@@ -322,8 +459,68 @@
 
     up = [(i, (i + 1) % joined) for i in range(joined)]
     down = [(j, i) for i, j in up]
-    above = lax.ppermute(est[tile - margin :], "joined", up)
-    below = lax.ppermute(est[:margin], "joined", down)
+
+    def target(p, s):
+        k, b = p // BLOCKS, p % BLOCKS
+        t = (k % half + s + (1 if k // half == b else 0)) % half
+        return 2 * (b * half + t) + k // half
+
+    first = total_blocks // 2
+    cut = ((0, first), (first, total_blocks))
+    away = [
+        2 * ((member % half + s + (member // half == block).astype(jnp.int32)) % half)
+        for s in range(half)
+    ]
+    inner = (member // half == block).astype(jnp.int32)
+    away = jnp.stack(away + [1 - position % 2, inner]).astype(jnp.int32)
+    starts = (2,) * half + (1,)
+    top, bottom = slice(0, margin), slice(tile - margin, tile)
+    low, high = slice(0, margin), slice(margin, 2 * margin)
+    every = slice(None)
+
+    def edge_pieces(c0, c1):
+        at = slice(c0 * LANES, c1 * LANES)
+        pieces = []
+        for s in range(half):
+            pieces.append((0, s, s, (every, top, at), (every, low)))
+            pieces.append((0, s, s, (every, bottom, at), (every, high)))
+        return pieces
+
+    def view_send(parts):
+        sent = []
+        for s, x in enumerate(parts):
+            pairs = [(p, target(p, s)) for p in range(size)]
+            sent.append(lax.ppermute(x, "view", [(p, q) for p, q in pairs if p != q]))
+        return sent
+
+    def pair_send(runs, kept, own, after):
+        mine, others = part_pair(away, runs, kept, own, after)
+        return mine, [lax.ppermute(x, "view", [(p, p ^ 1) for p in range(size)]) for x in others]
+
+    def edge_shape(c0, c1):
+        return (2, 2 * margin, (c1 - c0) * LANES)
+
+    packed_a = pack(
+        away, starts, [stack], [], [edge_shape(*cut[0])] * half, edge_pieces(*cut[0]), "pack_first"
+    )
+    kept_a = view_send(packed_a)
+    slab = pack(
+        away, starts, [est, psf], packed_a[:1], [(margin, cols)] * 2 + [psf.shape],
+        [
+            (0, 0, None, (bottom,), (every,)),
+            (0, 1, None, (top,), (every,)),
+            (1, 2, None, (every,), (every,)),
+        ],
+        "pack_slab",
+    )
+    above = lax.ppermute(slab[0], "joined", up)
+    below = lax.ppermute(slab[1], "joined", down)
+    psf = slab[2]
+    packed_b = pack(
+        away, starts, [stack], slab[:1], [edge_shape(*cut[1])] * half, edge_pieces(*cut[1]),
+        "pack_second",
+    )
+    kept_b = view_send(packed_b)
 
     pair, core = position // 2, position % 2
     owned_block, place = pair // half, pair % half
@@ -345,55 +542,34 @@
     live = (row < reach).astype(jnp.int32)
     inv = (1.0 / jnp.sum(live).astype(F32)).reshape(1)
     scal = jnp.stack(
-        [shifts[:, 0], shifts[:, 1], live[order], jnp.full((members,), core, jnp.int32)]
+        [shifts[:, 0], shifts[:, 1], live[order], jnp.where(jnp.arange(members) == 0, core, (core == owned_block).astype(jnp.int32))]
     ).astype(jnp.int32)
 
-    def target(p, s):
-        k, b = p // BLOCKS, p % BLOCKS
-        t = (k % half + s + (1 if k // half == b else 0)) % half
-        return 2 * (b * half + t) + k // half
-
-    def exchange(cut_rows):
-        kept = []
-        for s in range(half):
-            t = (member % half + s + (member // half == block).astype(jnp.int32)) % half
-            payload = cut_rows(lax.dynamic_slice_in_dim(stack, 2 * t, 2, 0))
-            kept.append(lax.ppermute(payload, "view", [(p, target(p, s)) for p in range(size)]))
-        other = jnp.concatenate(
-            [lax.dynamic_slice_in_dim(x, 1 - core, 1, 0) for x in kept], axis=0
+    rims = forward(radius, cut, scal, taps, est, above, below)
+    mid = slice(margin, tile - margin)
+    packed_c = pack(
+        away, starts, [stack], packed_b[:1], [(2, tile - 2 * margin, cols)] * half,
+        [(0, s, s, (every, slice(margin, tile - margin)), (every,)) for s in range(half)],
+        "pack_third",
+    )
+    kept_c = view_send(packed_c)
+
+    chunks, carries, main = [], [], None
+    for i, (kept, packed) in enumerate(((kept_a, packed_a), (kept_b, packed_b))):
+        runs = runs_of(half, half, cut[i][1] - cut[i][0])
+        mine, sib = pair_send(runs, kept, packed[-1], rims[-1:] if i == 0 else [main])
+        is_first, is_last = i == 0, i == len(cut) - 1
+        result = edges(
+            radius, tile, is_first, is_last, runs, scal, taps, rims[i], mine, sib, carries
         )
-        return kept, lax.ppermute(other, "view", [(p, p ^ 1) for p in range(size)])
-
-    first = total_blocks * 5 // 8
-    cut = ((0, first), (first, total_blocks))
-
-    def edge_rows(c0, c1):
-        def take(x):
-            x = x[:, :, c0 * LANES : c1 * LANES]
-            return jnp.concatenate([x[:, :margin], x[:, tile - margin :]], axis=1)
-
-        return take
-
-    received = [exchange(edge_rows(c0, c1)) for c0, c1 in cut]
-    middle = exchange(lambda x: x[:, margin : tile - margin])
-
-    rims = forward(radius, cut, scal, taps, est, above, below)
-
-    chunks, carries, closing = [], [], None
-    for i, (kept, sib) in enumerate(received):
-        is_first, is_last = i == 0, i == len(cut) - 1
-        given = [] if is_first else [carries] + ([closing] if is_last else [])
-        result = edges(radius, tile, is_first, is_last, scal, taps, rims[i], sib, kept, given)
         main, upper, lower = result[:3]
-        if not is_last:
-            carries = result[3]
-            if is_first:
-                closing = result[4]
+        carries = result[3:]
         from_above = lax.ppermute(lower, "joined", up)
         from_below = lax.ppermute(upper, "joined", down)
         chunks.append((main, from_above, from_below))
-    kept, sib = middle
-    out = finish(radius, scal, inv, taps, rims[-1], sib, est, kept, chunks)
+    runs = runs_of(3, half, total_blocks)
+    mine, sib = pair_send(runs, kept_c, packed_c[-1], [main, *chunks[0][1:]])
+    out = finish(radius, runs, scal, inv, taps, rims[-1], est, mine, sib, chunks)
     return out[None]
 
 

time: 110 us -> 82.3 us (0.75)
  waiting for transfers between devices: 35.4 us -> 15.3 us
  local copies, waits for them, and re-layouts: 18.9 us -> 2.96 us
  Pallas kernels: 20.6 us -> 34.9 us
  starting transfers between devices: 30.7 us -> 26.7 us
  other arithmetic: 3.16 us -> 1 us
    ppermute x11 -> x15, waiting for transfers between devices: 28.4 us -> 9.74 us  [the longest x1 4.44 us: per_device(): above = lax.ppermute(slab[0], 'joined', up)]
    pallas_call x1 -> x8, Pallas kernels: 4.48 us -> 22 us  [the longest x4 9.36 us: pack(): pl.pallas_call(functools.partial(pack_kernel, starts, pieces, len(ins) +...]
    slice x5 -> x0, local copies, waits for them, and re-layouts: 6.41 us -> none  [the longest x2 2.82 us: per_device(): middle = exchange(lambda x: x[:, margin:tile - margin])]
    ppermute x11 -> x15, starting transfers between devices: 22.8 us -> 17.1 us  [the longest x6 8.97 us: view_send(): sent.append(lax.ppermute(x, 'view', [(p, q) for p, q in pairs if p != q]))]
    unnamed x45 -> x25, local copies, waits for them, and re-layouts: 5.95 us -> 0.81 us
    pallas_call x2, Pallas kernels: 8.75 us -> 5.89 us  [edges(): pl.pallas_call(functools.partial(edge_kernel, radius, tile, is_first, is_...]
    dynamic_slice x7 -> x0, local copies, waits for them, and re-layouts: 2.65 us -> none  [the longest x1 2.49 us: exchange(): payload = cut_rows(lax.dynamic_slice_in_dim(stack, 2 * t, 2, 0))]
    ppermute x2, waiting for transfers between devices: 5.62 us -> 3.02 us  [per_device(): from_above = lax.ppermute(lower, 'joined', up)]
  transfers between devices with their start and end apart: 15 -> 19, of which waited for: 5 -> 6; matrix products, arithmetic and copies ran while one was open for 13% -> 4% of each run, Pallas kernels for 15% -> 29%
where the time goes in v2:
time: 82.3 us; the launch traced here: 81.9 us
  Pallas kernels  34.9 us (42%)
  starting transfers between devices  26.7 us (32%)
  waiting for transfers between devices  15.3 us (19%)
  local copies, waits for them, and re-layouts  2.96 us (4%)
  between operations  1.1 us (1%)
  other arithmetic  1 us (1%)
    pallas_call x4, Pallas kernels, pack(): pl.pallas_call(functools.partial(pack_kernel, starts, pieces, len(ins) +...  9.36 us
    ppermute x6, starting transfers between devices, view_send(): sent.append(lax.ppermute(x, 'view', [(p, q) for p, q in pairs if p != q]))  8.97 us
    ppermute x2, starting transfers between devices, per_device(): from_below = lax.ppermute(upper, 'joined', down)  8.82 us
    pallas_call x3, Pallas kernels, part_pair(): pl.pallas_call(functools.partial(pair_kernel, half, runs), grid_spec=pltp...  7.98 us
    pallas_call x1, Pallas kernels, forward(): pl.pallas_call(functools.partial(forward_kernel, radius, cut), grid_spec=...  7.04 us
    pallas_call x2, Pallas kernels, edges(): pl.pallas_call(functools.partial(edge_kernel, radius, tile, is_first, is_...  5.89 us
    pallas_call x1, Pallas kernels, finish(): pl.pallas_call(functools.partial(final_kernel, radius, tile, half, runs,...  4.63 us
    ppermute x1, waiting for transfers between devices, per_device(): above = lax.ppermute(slab[0], 'joined', up)  4.44 us
  transfers between devices with their start and end apart: 19, of which 6 were waited for; matrix products, arithmetic and copies ran while one was open for 4% of the time, Pallas kernels for 29%

profile of v2, /device:TPU:0, one launch (start us, length us, event | category | flops | bytes accessed | tf_op | source)
XLA Modules:
  0.0 81.9 jit_solution(755335874771153235)
XLA Ops:
  0.0 0.1 pad_add_fusion.1.refs_0_.scal
  0.1 3.1 %pack_first.1 = (f32[2,96,1024]{2,1,0:T(8,128)}, f32[2,96,1024]{2,1,0:T(8,128)}) custom-call(s32[4]{0:T(128)S(1)} %pad_add_fusion.1.refs_0_.scal, f32[4,128,2048]{2,1,0:T(8,128)} %bitcast.22), custom_call_target="tpu_custom_call" | custom-call | bytes 1024 | tf_op jit(solution)/shard_map/pack_first/pallas_call | solution.py:302
  3.2 3.0 %collective-permute-start.6 = (f32[2,96,1024]{2,1,0:T(8,128)}, f32[2,96,1024]{2,1,0:T(8,128)}, u32[]{:S(2)}, u32[]{:S(2)}) collective-permute-start(f32[2,96,1024]{2,1,0:T(8,128)} %get-tuple-element.38.refs_3_), channel_id=1, source_target_pairs={{0,2},{1,4},{2,0},{3,6},{4,1},{5,7},{6,3},{7,5},{8,10},{9,12},{10,... | collective-permute-start | bytes 2359304 | tf_op jit(solution)/shard_map/ppermute | solution.py:493
  6.2 1.7 %pack_slab.1 = (f32[48,2048]{1,0:T(8,128)S(1)}, f32[48,2048]{1,0:T(8,128)S(1)}, f32[4,2,65]{2,1,0:T(2,128)S(1)}) custom-call(s32[4]{0:T(128)S(1)} %pad_add_fusion.1.refs_0_.scal, f32[128,2048]{1,0:T(8,128)} %bitcast.19, f32[4,2,65]{2,1,0:T(2,128)} %refs_2_.1, f32[2,96,1024]{2,1,0:T(8,128)} %get-tuple-element.38.refs_3_), custom_call_target="tpu_custom_call" | custom-call | bytes 1024 | tf_op jit(solution)/shard_map/pack_slab/pallas_call | solution.py:302
  7.9 1.6 %collective-permute-start = (f32[48,2048]{1,0:T(8,128)S(1)}, f32[48,2048]{1,0:T(8,128)S(1)}, u32[]{:S(2)}, u32[]{:S(2)}) collective-permute-start(f32[48,2048]{1,0:T(8,128)S(1)} %get-tuple-element.40.refs_2_), channel_id=1, source_target_pairs={{0,8},{8,16},{16,24},{24,0},{1,9},{9,17},{17,25},{25,1},{2,10},{10... | collective-permute-start | bytes 1179656 | tf_op jit(solution)/shard_map/ppermute | solution.py:516
  9.5 2.2 %collective-permute-start.1 = (f32[48,2048]{1,0:T(8,128)S(1)}, f32[48,2048]{1,0:T(8,128)}, u32[]{:S(2)}, u32[]{:S(2)}) collective-permute-start(f32[48,2048]{1,0:T(8,128)S(1)} %get-tuple-element.41), channel_id=1, source_target_pairs={{8,0},{16,8},{24,16},{0,24},{9,1},{17,9},{25,17},{1,25},{10,2},{18... | collective-permute-start | bytes 1179656 | tf_op jit(solution)/shard_map/ppermute | solution.py:517
  11.7 1.7 %collective-permute-start.7 = (f32[2,96,1024]{2,1,0:T(8,128)}, f32[2,96,1024]{2,1,0:T(8,128)}, u32[]{:S(2)}, u32[]{:S(2)}) collective-permute-start(f32[2,96,1024]{2,1,0:T(8,128)} %get-tuple-element.49.refs_2_), channel_id=1, source_target_pairs={{1,6},{3,4},{4,3},{6,1},{9,14},{11,12},{12,11},{14,9},{17,22},{19,... | collective-permute-start | bytes 2359304 | tf_op jit(solution)/shard_map/ppermute | solution.py:493
  13.4 2.8 %pack_second.1 = (f32[2,96,1024]{2,1,0:T(8,128)S(1)}, f32[2,96,1024]{2,1,0:T(8,128)}) custom-call(s32[4]{0:T(128)S(1)} %pad_add_fusion.1.refs_0_.scal, f32[4,128,2048]{2,1,0:T(8,128)} %bitcast.23, f32[48,2048]{1,0:T(8,128)S(1)} %get-tuple-element.40.refs_2_), custom_call_target="tpu_custom_call" | custom-call | bytes 1024 | tf_op jit(solution)/shard_map/pack_second/pallas_call | solution.py:302
  16.3 0.4 collective-permute-start.4
  16.7 0.1 reduce_sum.19
  16.8 0.1 broadcast_divide_fusion
  17.0 0.1 rev.6
  17.1 0.1 rev.7
  17.2 0.1 fusion
  17.3 4.4 %collective-permute-done.above = f32[48,2048]{1,0:T(8,128)S(1)} collective-permute-done((f32[48,2048]{1,0:T(8,128)S(1)}, f32[48,2048]{1,0:T(8,128)S(1)}, u32[]{:S(2)}, u32[]{:S(2)}) %collective-permute-start) | collective-permute-done | bytes 393248 | tf_op jit(solution)/shard_map/ppermute | solution.py:516
  21.7 1.6 %collective-permute-start.5 = (f32[2,96,1024]{2,1,0:T(8,128)}, f32[2,96,1024]{2,1,0:T(8,128)}, u32[]{:S(2)}, u32[]{:S(2)}) collective-permute-start(f32[2,96,1024]{2,1,0:T(8,128)} %get-tuple-element.47.refs_2_), channel_id=1, source_target_pairs={{1,6},{3,4},{4,3},{6,1},{9,14},{11,12},{12,11},{14,9},{17,22},{19,... | collective-permute-start | bytes 2359304 | tf_op jit(solution)/shard_map/ppermute | solution.py:493
  23.3 0.0 copy-done.11
  23.3 0.6 gather_fusion.2
  23.9 0.1 copy.7
  24.0 0.6 gather_fusion
  24.6 0.6 gather_fusion.1
  25.2 0.2 slice_reduce_fusion.1
  25.4 3.5 %collective-permute-done.1.below = f32[48,2048]{1,0:T(8,128)} collective-permute-done((f32[48,2048]{1,0:T(8,128)S(1)}, f32[48,2048]{1,0:T(8,128)}, u32[]{:S(2)}, u32[]{:S(2)}) %collective-permute-start.1) | collective-permute-done | bytes 393248 | tf_op jit(solution)/shard_map/ppermute | solution.py:517
  28.9 7.0 %forward.1 = (f32[4,96,1024]{2,1,0:T(8,128)S(1)}, f32[4,96,1024]{2,1,0:T(8,128)S(1)}, f32[4,32,2048]{2,1,0:T(8,128)S(1)}) custom-call(s32[4,4]{1,0:T(4,128)S(1)} %pad_add_fusion.scal, f32[4,4,256]{2,1,0:T(4,128)S(1)} %gather.15.taps, f32[128,2048]{1,0:T(8,128)S(1)} %bitcast.21, f32[48,2048]{1,0:T(8,128)} %copy-done.7, f32[48,2048]{1,0:T(8,128)} %collective-permute-done.1.below), custom_call_target="tpu_custom_call" | custom-call | bytes 1024 | tf_op jit(solution)/shard_map/forward/pallas_call | solution.py:355
  36.0 0.0 collective-permute-done.6.refs_0_
  36.0 0.0 collective-permute-done.7.refs_1_
  36.0 3.2 %pair.3 = (f32[96,1024]{1,0:T(8,128)S(1)}, f32[96,1024]{1,0:T(8,128)S(1)}, f32[96,1024]{1,0:T(8,128)S(1)}, f32[96,1024]{1,0:T(8,128)S(1)}) custom-call(s32[4]{0:T(128)S(1)} %pad_add_fusion.1.refs_0_.scal, f32[2,96,1024]{2,1,0:T(8,128)} %collective-permute-done.6.refs_0_, f32[2,96,1024]{2,1,0:T(8,128)} %collective-permute-done.7.refs_1_, ...), custom_call_target="tpu_custom_call" | custom-call | bytes 1024 | tf_op jit(solution)/shard_map/pair/pallas_call | solution.py:323
  39.2 0.1 collective-permute-start.8
  39.2 0.5 collective-permute-start.9
  39.7 1.2 %collective-permute-done.8.rest_2_ = f32[96,1024]{1,0:T(8,128)S(1)} collective-permute-done((f32[96,1024]{1,0:T(8,128)S(1)}, f32[96,1024]{1,0:T(8,128)S(1)}, u32[]{:S(2)}, u32[]{:S(2)}) %collective-permute-start.8) | collective-permute-done | bytes 393248 | tf_op jit(solution)/shard_map/ppermute | solution.py:498
  41.0 0.6 collective-permute-done.9.rest_3_
  41.5 2.9 %edges.2 = (f32[128,896]{1,0:T(8,128)S(1)}, f32[48,896]{1,0:T(8,128)S(1)}, f32[48,896]{1,0:T(8,128)S(1)}, f32[4,96,128]{2,1,0:T(8,128)S(1)}, f32[4,96,128]{2,1,0:T(8,128)S(1)}) custom-call(s32[4,4]{1,0:T(4,128)S(1)} %pad_add_fusion.scal, f32[4,4,256]{2,1,0:T(4,128)S(1)} %gather.15.taps, f32[4,96,1024]{2,1,0:T(8,128)S(1)} %get-tuple-element.48.rim, ...), custom_call_target="tpu_custom_call" | custom-call | bytes 1024 | tf_op jit(solution)/shard_map/edges/pallas_call | solution.py:391
  44.4 0.0 collective-permute-done.4.refs_0_
  44.4 0.0 collective-permute-done.5.refs_1_
  44.4 3.2 %pair.4 = (f32[96,1024]{1,0:T(8,128)S(1)}, f32[96,1024]{1,0:T(8,128)S(1)}, f32[96,1024]{1,0:T(8,128)S(1)}, f32[96,1024]{1,0:T(8,128)S(1)}) custom-call(s32[4]{0:T(128)S(1)} %pad_add_fusion.1.refs_0_.scal, f32[2,96,1024]{2,1,0:T(8,128)} %collective-permute-done.4.refs_0_, f32[2,96,1024]{2,1,0:T(8,128)} %collective-permute-done.5.refs_1_, ...), custom_call_target="tpu_custom_call" | custom-call | bytes 1024 | tf_op jit(solution)/shard_map/pair/pallas_call | solution.py:323
  47.6 0.1 collective-permute-start.10
  47.7 1.8 %pack_third.1 = (f32[2,32,2048]{2,1,0:T(8,128)S(1)}, f32[2,32,2048]{2,1,0:T(8,128)S(1)}) custom-call(s32[4]{0:T(128)S(1)} %pad_add_fusion.1.refs_0_.scal, f32[4,128,2048]{2,1,0:T(8,128)} %bitcast.24, f32[2,96,1024]{2,1,0:T(8,128)S(1)} %get-tuple-element.43.refs_2_), custom_call_target="tpu_custom_call" | custom-call | bytes 1024 | tf_op jit(solution)/shard_map/pack_third/pallas_call | solution.py:302
  49.5 0.0 copy-start.6
  49.5 1.6 %collective-permute-start.2 = (f32[2,32,2048]{2,1,0:T(8,128)S(1)}, f32[2,32,2048]{2,1,0:T(8,128)S(1)}, u32[]{:S(2)}, u32[]{:S(2)}) collective-permute-start(f32[2,32,2048]{2,1,0:T(8,128)S(1)} %get-tuple-element.44), channel_id=1, source_target_pairs={{0,2},{1,4},{2,0},{3,6},{4,1},{5,7},{6,3},{7,5},{8,10},{9,12},{10,... | collective-permute-start | bytes 1572872 | tf_op jit(solution)/shard_map/ppermute | solution.py:493
  51.0 0.7 collective-permute-start.3
  51.7 3.0 %collective-permute-start.11 = (f32[96,1024]{1,0:T(8,128)S(1)}, f32[96,1024]{1,0:T(8,128)S(1)}, u32[]{:S(2)}, u32[]{:S(2)}) collective-permute-start(f32[96,1024]{1,0:T(8,128)S(1)} %get-tuple-element.58), channel_id=1, source_target_pairs={{0,1},{1,0},{2,3},{3,2},{4,5},{5,4},{6,7},{7,6},{8,9},{9,8},{10,11... | collective-permute-start | bytes 1179656 | tf_op jit(solution)/shard_map/ppermute | solution.py:498
  54.7 0.7 collective-permute-start.12
  55.4 0.0 collective-permute-done.10.rest_2_
  55.4 5.0 %collective-permute-start.13 = (f32[48,896]{1,0:T(8,128)S(1)}, f32[48,896]{1,0:T(8,128)S(1)}, u32[]{:S(2)}, u32[]{:S(2)}) collective-permute-start(f32[48,896]{1,0:T(8,128)S(1)} %get-tuple-element.63), channel_id=1, source_target_pairs={{8,0},{16,8},{24,16},{0,24},{9,1},{17,9},{25,17},{1,25},{10,2},{18... | collective-permute-start | bytes 516104 | tf_op jit(solution)/shard_map/ppermute | solution.py:568
  60.4 0.0 collective-permute-done.11.rest_3_
  60.4 3.0 %edges.3 = (f32[128,1152]{1,0:T(8,128)S(1)}, f32[48,1152]{1,0:T(8,128)S(1)}, f32[48,1152]{1,0:T(8,128)S(1)}) custom-call(s32[4,4]{1,0:T(4,128)S(1)} %pad_add_fusion.scal, f32[4,4,256]{2,1,0:T(4,128)S(1)} %gather.15.taps, f32[4,96,1024]{2,1,0:T(8,128)S(1)} %get-tuple-element.46.rim, f32[96,1024]{1,0:T(8,128)S(1)} %get-tuple-element.55.rest_0_, ...), custom_call_target="tpu_custom_call" | custom-call | bytes 1024 | tf_op jit(solution)/shard_map/edges/pallas_call | solution.py:391
  63.4 0.1 collective-permute-start.17
  63.5 0.0 collective-permute-done.2.refs_0_
  63.5 3.8 %collective-permute-start.18 = (f32[48,1152]{1,0:T(8,128)S(1)}, f32[48,1152]{1,0:T(8,128)S(1)}, u32[]{:S(2)}, u32[]{:S(2)}) collective-permute-start(f32[48,1152]{1,0:T(8,128)S(1)} %get-tuple-element.70), channel_id=1, source_target_pairs={{8,0},{16,8},{24,16},{0,24},{9,1},{17,9},{25,17},{1,25},{10,2},{18... | collective-permute-start | bytes 663560 | tf_op jit(solution)/shard_map/ppermute | solution.py:568
  67.3 0.0 collective-permute-done.3.refs_1_
  67.3 0.0 collective-permute-done.12.refs_4_.rest_6_
  67.3 0.0 collective-permute-done.13.refs_5_.rest_7_
  67.4 1.7 %pair.5 = (f32[32,2048]{1,0:T(8,128)S(1)}, f32[32,2048]{1,0:T(8,128)S(1)}, f32[32,1408]{1,0:T(8,128)S(1)}, f32[32,1280]{1,0:T(8,128)S(1)}, f32[32,1408]{1,0:T(8,128)S(1)}) custom-call(s32[4]{0:T(128)S(1)} %pad_add_fusion.1.refs_0_.scal, f32[2,32,2048]{2,1,0:T(8,128)S(1)} %collective-permute-done.2.refs_0_, ...), custom_call_target="tpu_custom_call" | custom-call | bytes 1024 | tf_op jit(solution)/shard_map/pair/pallas_call | solution.py:323
  69.0 0.1 collective-permute-start.14
  69.1 0.5 collective-permute-start.16
  69.6 0.1 collective-permute-start.15
  69.7 0.6 fusion.1
  71.0 0.0 collective-permute-done.15.rest_3_
  71.0 0.0 collective-permute-done.14.rest_2_
  71.0 0.0 collective-permute-done.16.rest_4_
  71.0 3.0 %collective-permute-done.17.rest_9_ = f32[48,1152]{1,0:T(8,128)S(1)} collective-permute-done((f32[48,1152]{1,0:T(8,128)S(1)}, f32[48,1152]{1,0:T(8,128)S(1)}, u32[]{:S(2)}, u32[]{:S(2)}) %collective-permute-start.17) | collective-permute-done | bytes 221216 | tf_op jit(solution)/shard_map/ppermute | solution.py:567
  74.1 2.5 %collective-permute-done.18.rest_10_ = f32[48,1152]{1,0:T(8,128)S(1)} collective-permute-done((f32[48,1152]{1,0:T(8,128)S(1)}, f32[48,1152]{1,0:T(8,128)S(1)}, u32[]{:S(2)}, u32[]{:S(2)}) %collective-permute-start.18) | collective-permute-done | bytes 221216 | tf_op jit(solution)/shard_map/ppermute | solution.py:568
  76.6 0.7 copy-done.9
  77.3 4.6 %finish.1 = f32[128,2048]{1,0:T(8,128)} custom-call(s32[4,4]{1,0:T(4,128)S(1)} %pad_add_fusion.scal, f32[1]{0:T(128)} %bitcast.7.inv, f32[4,4,256]{2,1,0:T(4,128)S(1)} %gather.15.taps, f32[4,32,2048]{2,1,0:T(8,128)} %copy-done.1, f32[128,2048]{1,0:T(8,128)} %bitcast.20, f32[32,2048]{1,0:T(8,128)S(1)} %get-tuple-element.64.rest_0_, ...), custom_call_target="tpu_custom_call" | custom-call | bytes 1024 | tf_op jit(solution)/shard_map/finish/pallas_call | solution.py:418
  (28 shorter events, 0.1 us)
Async XLA Ops:
  3.2 32.8 %collective-permute-start.6 = (f32[2,96,1024]{2,1,0:T(8,128)}, f32[2,96,1024]{2,1,0:T(8,128)}, u32[]{:S(2)}, u32[]{:S(2)}) collective-permute-start(f32[2,96,1024]{2,1,0:T(8,128)} %get-tuple-element.38.refs_3_), channel_id=1, source_target_pairs={{0,2},{1,4},{2,0},{3,6},{4,1},{5,7},{6,3},{7,5},{8,10},{9,12},{10,... | collective-permute-start | bytes 2359304 | tf_op jit(solution)/shard_map/ppermute | solution.py:493
  7.9 13.9 %collective-permute-start = (f32[48,2048]{1,0:T(8,128)S(1)}, f32[48,2048]{1,0:T(8,128)S(1)}, u32[]{:S(2)}, u32[]{:S(2)}) collective-permute-start(f32[48,2048]{1,0:T(8,128)S(1)} %get-tuple-element.40.refs_2_), channel_id=1, source_target_pairs={{0,8},{8,16},{16,24},{24,0},{1,9},{9,17},{17,25},{25,1},{2,10},{10... | collective-permute-start | bytes 1179656 | tf_op jit(solution)/shard_map/ppermute | solution.py:516
  9.5 19.4 %collective-permute-start.1 = (f32[48,2048]{1,0:T(8,128)S(1)}, f32[48,2048]{1,0:T(8,128)}, u32[]{:S(2)}, u32[]{:S(2)}) collective-permute-start(f32[48,2048]{1,0:T(8,128)S(1)} %get-tuple-element.41), channel_id=1, source_target_pairs={{8,0},{16,8},{24,16},{0,24},{9,1},{17,9},{25,17},{1,25},{10,2},{18... | collective-permute-start | bytes 1179656 | tf_op jit(solution)/shard_map/ppermute | solution.py:517
  11.7 11.6 %copy-start.11 = (s32[4,2]{0,1:T(2,128)S(1)}, s32[4,2]{0,1:T(2,128)}, u32[]{:S(2)}) copy-start(s32[4,2]{0,1:T(2,128)} %param.9) | copy-start | bytes 100
  11.7 12.2 %copy-start.10 = (s32[4,2]{0,1:T(2,128)S(1)}, s32[4,2]{0,1:T(2,128)}, u32[]{:S(2)}) copy-start(s32[4,2]{0,1:T(2,128)} %param.8) | copy-start | bytes 100
  11.7 17.2 %copy-start = (f32[1,128,2048]{2,1,0:T(8,128)S(1)}, f32[1,128,2048]{2,1,0:T(8,128)}, u32[]{:S(2)}) copy-start(f32[1,128,2048]{2,1,0:T(8,128)} %param.5) | copy-start | bytes 3145732
  11.7 24.2 %collective-permute-start.7 = (f32[2,96,1024]{2,1,0:T(8,128)}, f32[2,96,1024]{2,1,0:T(8,128)}, u32[]{:S(2)}, u32[]{:S(2)}) collective-permute-start(f32[2,96,1024]{2,1,0:T(8,128)} %get-tuple-element.49.refs_2_), channel_id=1, source_target_pairs={{1,6},{3,4},{4,3},{6,1},{9,14},{11,12},{12,11},{14,9},{17,22},{19,... | collective-permute-start | bytes 2359304 | tf_op jit(solution)/shard_map/ppermute | solution.py:493
  16.3 28.2 %collective-permute-start.4 = (f32[2,96,1024]{2,1,0:T(8,128)S(1)}, f32[2,96,1024]{2,1,0:T(8,128)}, u32[]{:S(2)}, u32[]{:S(2)}) collective-permute-start(f32[2,96,1024]{2,1,0:T(8,128)S(1)} %get-tuple-element.43.refs_2_), channel_id=1, source_target_pairs={{0,2},{1,4},{2,0},{3,6},{4,1},{5,7},{6,3},{7,5},{8,10},{9,12},{10,... | collective-permute-start | bytes 2359304 | tf_op jit(solution)/shard_map/ppermute | solution.py:493
  21.7 7.2 %copy-start.7 = (f32[48,2048]{1,0:T(8,128)}, f32[48,2048]{1,0:T(8,128)S(1)}, u32[]{:S(2)}) copy-start(f32[48,2048]{1,0:T(8,128)S(1)} %collective-permute-done.above) | copy-start | bytes 1179652
  21.7 22.7 %collective-permute-start.5 = (f32[2,96,1024]{2,1,0:T(8,128)}, f32[2,96,1024]{2,1,0:T(8,128)}, u32[]{:S(2)}, u32[]{:S(2)}) collective-permute-start(f32[2,96,1024]{2,1,0:T(8,128)} %get-tuple-element.47.refs_2_), channel_id=1, source_target_pairs={{1,6},{3,4},{4,3},{6,1},{9,14},{11,12},{12,11},{14,9},{17,22},{19,... | collective-permute-start | bytes 2359304 | tf_op jit(solution)/shard_map/ppermute | solution.py:493
  36.0 3.2 %copy-start.1 = (f32[4,32,2048]{2,1,0:T(8,128)}, f32[4,32,2048]{2,1,0:T(8,128)S(1)}, u32[]{:S(2)}) copy-start(f32[4,32,2048]{2,1,0:T(8,128)S(1)} %get-tuple-element.42.refs_3_.rim) | copy-start | bytes 3145732
  39.2 1.8 %collective-permute-start.8 = (f32[96,1024]{1,0:T(8,128)S(1)}, f32[96,1024]{1,0:T(8,128)S(1)}, u32[]{:S(2)}, u32[]{:S(2)}) collective-permute-start(f32[96,1024]{1,0:T(8,128)S(1)} %get-tuple-element.52), channel_id=1, source_target_pairs={{0,1},{1,0},{2,3},{3,2},{4,5},{5,4},{6,7},{7,6},{8,9},{9,8},{10,11... | collective-permute-start | bytes 1179656 | tf_op jit(solution)/shard_map/ppermute | solution.py:498
  39.2 2.3 %collective-permute-start.9 = (f32[96,1024]{1,0:T(8,128)S(1)}, f32[96,1024]{1,0:T(8,128)S(1)}, u32[]{:S(2)}, u32[]{:S(2)}) collective-permute-start(f32[96,1024]{1,0:T(8,128)S(1)} %get-tuple-element.53), channel_id=1, source_target_pairs={{0,1},{1,0},{2,3},{3,2},{4,5},{5,4},{6,7},{7,6},{8,9},{9,8},{10,11... | collective-permute-start | bytes 1179656 | tf_op jit(solution)/shard_map/ppermute | solution.py:498
  44.4 5.0 %copy-start.3 = (f32[128,896]{1,0:T(8,128)}, f32[128,896]{1,0:T(8,128)S(1)}, u32[]{:S(2)}) copy-start(f32[128,896]{1,0:T(8,128)S(1)} %get-tuple-element.54.refs_3_.rest_5_) | copy-start | bytes 1376260
  47.6 7.8 %collective-permute-start.10 = (f32[96,1024]{1,0:T(8,128)S(1)}, f32[96,1024]{1,0:T(8,128)S(1)}, u32[]{:S(2)}, u32[]{:S(2)}) collective-permute-start(f32[96,1024]{1,0:T(8,128)S(1)} %get-tuple-element.57), channel_id=1, source_target_pairs={{0,1},{1,0},{2,3},{3,2},{4,5},{5,4},{6,7},{7,6},{8,9},{9,8},{10,11... | collective-permute-start | bytes 1179656 | tf_op jit(solution)/shard_map/ppermute | solution.py:498
  49.5 13.9 %copy-start.6 = (f32[2,32,2048]{2,1,0:T(8,128)}, f32[2,32,2048]{2,1,0:T(8,128)S(1)}, u32[]{:S(2)}) copy-start(f32[2,32,2048]{2,1,0:T(8,128)S(1)} %get-tuple-element.45.refs_2_) | copy-start | bytes 1572868
  49.5 14.0 %collective-permute-start.2 = (f32[2,32,2048]{2,1,0:T(8,128)S(1)}, f32[2,32,2048]{2,1,0:T(8,128)S(1)}, u32[]{:S(2)}, u32[]{:S(2)}) collective-permute-start(f32[2,32,2048]{2,1,0:T(8,128)S(1)} %get-tuple-element.44), channel_id=1, source_target_pairs={{0,2},{1,4},{2,0},{3,6},{4,1},{5,7},{6,3},{7,5},{8,10},{9,12},{10,... | collective-permute-start | bytes 1572872 | tf_op jit(solution)/shard_map/ppermute | solution.py:493
  51.0 16.3 %collective-permute-start.3 = (f32[2,32,2048]{2,1,0:T(8,128)S(1)}, f32[2,32,2048]{2,1,0:T(8,128)S(1)}, u32[]{:S(2)}, u32[]{:S(2)}) collective-permute-start(f32[2,32,2048]{2,1,0:T(8,128)S(1)} %get-tuple-element.45.refs_2_), channel_id=1, source_target_pairs={{1,6},{3,4},{4,3},{6,1},{9,14},{11,12},{12,11},{14,9},{17,22},{19,... | collective-permute-start | bytes 1572872 | tf_op jit(solution)/shard_map/ppermute | solution.py:493
  51.7 8.7 %collective-permute-start.11 = (f32[96,1024]{1,0:T(8,128)S(1)}, f32[96,1024]{1,0:T(8,128)S(1)}, u32[]{:S(2)}, u32[]{:S(2)}) collective-permute-start(f32[96,1024]{1,0:T(8,128)S(1)} %get-tuple-element.58), channel_id=1, source_target_pairs={{0,1},{1,0},{2,3},{3,2},{4,5},{5,4},{6,7},{7,6},{8,9},{9,8},{10,11... | collective-permute-start | bytes 1179656 | tf_op jit(solution)/shard_map/ppermute | solution.py:498
  54.7 12.7 %collective-permute-start.12 = (f32[48,896]{1,0:T(8,128)S(1)}, f32[48,896]{1,0:T(8,128)S(1)}, u32[]{:S(2)}, u32[]{:S(2)}) collective-permute-start(f32[48,896]{1,0:T(8,128)S(1)} %get-tuple-element.62), channel_id=1, source_target_pairs={{0,8},{8,16},{16,24},{24,0},{1,9},{9,17},{17,25},{25,1},{2,10},{10... | collective-permute-start | bytes 516104 | tf_op jit(solution)/shard_map/ppermute | solution.py:567
  55.4 11.9 %collective-permute-start.13 = (f32[48,896]{1,0:T(8,128)S(1)}, f32[48,896]{1,0:T(8,128)S(1)}, u32[]{:S(2)}, u32[]{:S(2)}) collective-permute-start(f32[48,896]{1,0:T(8,128)S(1)} %get-tuple-element.63), channel_id=1, source_target_pairs={{8,0},{16,8},{24,16},{0,24},{9,1},{17,9},{25,17},{1,25},{10,2},{18... | collective-permute-start | bytes 516104 | tf_op jit(solution)/shard_map/ppermute | solution.py:568
  63.4 13.2 %copy-start.2 = (f32[128,1152]{1,0:T(8,128)}, f32[128,1152]{1,0:T(8,128)S(1)}, u32[]{:S(2)}) copy-start(f32[128,1152]{1,0:T(8,128)S(1)} %get-tuple-element.61.refs_3_.rest_8_) | copy-start | bytes 1769476
  63.4 10.7 %collective-permute-start.17 = (f32[48,1152]{1,0:T(8,128)S(1)}, f32[48,1152]{1,0:T(8,128)S(1)}, u32[]{:S(2)}, u32[]{:S(2)}) collective-permute-start(f32[48,1152]{1,0:T(8,128)S(1)} %get-tuple-element.69), channel_id=1, source_target_pairs={{0,8},{8,16},{16,24},{24,0},{1,9},{9,17},{17,25},{25,1},{2,10},{10... | collective-permute-start | bytes 663560 | tf_op jit(solution)/shard_map/ppermute | solution.py:567
  63.5 13.1 %collective-permute-start.18 = (f32[48,1152]{1,0:T(8,128)S(1)}, f32[48,1152]{1,0:T(8,128)S(1)}, u32[]{:S(2)}, u32[]{:S(2)}) collective-permute-start(f32[48,1152]{1,0:T(8,128)S(1)} %get-tuple-element.70), channel_id=1, source_target_pairs={{8,0},{16,8},{24,16},{0,24},{9,1},{17,9},{25,17},{1,25},{10,2},{18... | collective-permute-start | bytes 663560 | tf_op jit(solution)/shard_map/ppermute | solution.py:568
  67.3 9.2 %copy-start.4 = (f32[48,896]{1,0:T(8,128)}, f32[48,896]{1,0:T(8,128)S(1)}, u32[]{:S(2)}) copy-start(f32[48,896]{1,0:T(8,128)S(1)} %collective-permute-done.12.refs_4_.rest_6_) | copy-start | bytes 516100
  67.4 9.2 %copy-start.5 = (f32[48,896]{1,0:T(8,128)}, f32[48,896]{1,0:T(8,128)S(1)}, u32[]{:S(2)}) copy-start(f32[48,896]{1,0:T(8,128)S(1)} %collective-permute-done.13.refs_5_.rest_7_) | copy-start | bytes 516100
  69.0 2.0 %collective-permute-start.14 = (f32[32,1408]{1,0:T(8,128)S(1)}, f32[32,1408]{1,0:T(8,128)S(1)}, u32[]{:S(2)}, u32[]{:S(2)}) collective-permute-start(f32[32,1408]{1,0:T(8,128)S(1)} %get-tuple-element.66), channel_id=1, source_target_pairs={{0,1},{1,0},{2,3},{3,2},{4,5},{5,4},{6,7},{7,6},{8,9},{9,8},{10,11... | collective-permute-start | bytes 540680 | tf_op jit(solution)/shard_map/ppermute | solution.py:498
  69.1 1.9 %collective-permute-start.16 = (f32[32,1408]{1,0:T(8,128)S(1)}, f32[32,1408]{1,0:T(8,128)S(1)}, u32[]{:S(2)}, u32[]{:S(2)}) collective-permute-start(f32[32,1408]{1,0:T(8,128)S(1)} %get-tuple-element.68), channel_id=1, source_target_pairs={{0,1},{1,0},{2,3},{3,2},{4,5},{5,4},{6,7},{7,6},{8,9},{9,8},{10,11... | collective-permute-start | bytes 540680 | tf_op jit(solution)/shard_map/ppermute | solution.py:498
  69.6 1.4 %collective-permute-start.15 = (f32[32,1280]{1,0:T(8,128)S(1)}, f32[32,1280]{1,0:T(8,128)S(1)}, u32[]{:S(2)}, u32[]{:S(2)}) collective-permute-start(f32[32,1280]{1,0:T(8,128)S(1)} %get-tuple-element.67), channel_id=1, source_target_pairs={{0,1},{1,0},{2,3},{3,2},{4,5},{5,4},{6,7},{7,6},{8,9},{9,8},{10,11... | collective-permute-start | bytes 491528 | tf_op jit(solution)/shard_map/ppermute | solution.py:498
  74.1 2.5 %copy-start.8 = (f32[48,1152]{1,0:T(8,128)}, f32[48,1152]{1,0:T(8,128)S(1)}, u32[]{:S(2)}) copy-start(f32[48,1152]{1,0:T(8,128)S(1)} %collective-permute-done.17.rest_9_) | copy-start | bytes 663556
  76.6 0.7 copy-start.9

commit v3 on v2

--- a/solution.py
+++ b/solution.py
@@ -44,7 +44,14 @@
     return copy
 
 
-def forward_kernel(radius, cut, scal, taps, est, above, below, *rest):
+def fetch_sides(odd, inside, across, target, first_sem, second_sem):
+    return [
+        fetch(inside, target.at[1 - odd], first_sem),
+        fetch(across, target.at[odd], second_sem),
+    ]
+
+
+def forward_kernel(radius, cut, scal, taps, est, inside, across, *rest):
     outs, (e_hi, e_lo, lhs, halo, sems) = rest[:-5], rest[-5:]
     slot = pl.program_id(0)
     margin = radius + MAXD
@@ -54,14 +61,11 @@
 
     @pl.when(slot == 0)
     def _():
-        copies = [fetch(x, halo.at[i], sems.at[i]) for i, x in enumerate((above, below))]
-        for piece, at, copy in (
-            (est, margin, None),
-            (halo.at[0], 0, copies[0]),
-            (halo.at[1], margin + tile, copies[1]),
-        ):
-            if copy is not None:
-                copy.wait()
+        copies = fetch_sides(scal[3, 2], inside, across, halo, sems.at[0], sems.at[1])
+        for piece, at in ((est, margin), (halo.at[0], 0), (halo.at[1], margin + tile)):
+            if at == 0:
+                for copy in copies:
+                    copy.wait()
             top, rest = split(pltpu.roll(piece[...], margin, 1))
             e_hi[at : at + piece.shape[0], :] = top
             e_lo[at : at + piece.shape[0], :] = rest
@@ -134,38 +138,51 @@
     return parts[0] if len(parts) == 1 else jnp.concatenate(parts, axis=1)
 
 
+def fetch_either(flag, source, other, target, sem):
+    @pl.when(flag != 0)
+    def _():
+        fetch(other, target, sem)
+
+    @pl.when(flag == 0)
+    def _():
+        fetch(source, target, sem)
+
+    return pltpu.make_async_copy(source, target, sem)
+
+
 def pair_kernel(half, runs, scal, *refs):
     kept, own, refs = refs[:half], refs[half], refs[half + 1 :]
-    (buffer, sem), refs = refs[-2:], refs[:-2]
-    outs = refs[-(half + len(runs)) :]
+    outs, sem = refs[-1 - len(runs) - half : -1], refs[-1]
     away, inner = scal[half], scal[half + 1]
-
-    @pl.when(inner != 0)
-    def _():
-        copy = fetch(own, buffer, sem.at[0])
-        copy.wait()
-
-    @pl.when(inner == 0)
-    def _():
-        buffer[...] = kept[half - 1][...]
-
-    sources = [*kept[: half - 1], buffer]
-    for s in range(half):
-        outs[s][...] = sources[s][1 - away]
-    for out, of_out in zip(outs[half:], runs):
+    copies = []
+    for out, of_out in zip(outs, runs):
         at = 0
         for view, c0, c1 in of_out:
-            width = (c1 - c0) * LANES
-            out[:, at : at + width] = sources[view][away, :, c0 * LANES : c1 * LANES]
-            at += width
+            cols = slice(c0 * LANES, c1 * LANES)
+            target = out.at[:, at : at + (c1 - c0) * LANES]
+            place = (kept[view].at[away, :, cols], target, sem.at[len(copies)])
+            if view < half - 1:
+                copies.append(fetch(*place))
+            else:
+                copies.append(fetch_either(inner, place[0], own.at[away, :, cols], *place[1:]))
+            at += (c1 - c0) * LANES
+    for s, out in enumerate(outs[len(runs) :]):
+        place = (kept[s].at[1 - away], out, sem.at[len(copies)])
+        if s < half - 1:
+            copies.append(fetch(*place))
+        else:
+            copies.append(fetch_either(inner, place[0], own.at[1 - away], *place[1:]))
+    for copy in copies:
+        copy.wait()
 
 
 def edge_kernel(radius, tile, is_first, is_last, half, runs, scal, taps, rim, *rest):
-    mine, sib, rest = rest[:half], rest[half : half + len(runs)], rest[half + len(runs) :]
+    mine, rest = rest[:half], rest[half:]
+    sib, rest = rest[: len(runs)], rest[len(runs) :]
     carries = []
     if not is_first:
         carries, rest = rest[: 1 + is_last], rest[1 + is_last :]
-    main, up, down = rest[:3]
+    main, inside, across = rest[:3]
     rest = rest[3:]
     if not is_last:
         (next_left, *rest) = rest
@@ -209,37 +226,33 @@
     b_hi, b_lo = split(jnp.concatenate(bands, axis=1))
     both = mm(jnp.concatenate([b_hi, b_lo], axis=0), s_hi[...])
     total = both[:extended] + both[extended:] + mm(b_hi, s_lo[...])
-    up[...] = total[:margin]
+    odd = scal[3, 2] != 0
     main[...] = total[margin : margin + tile]
-    down[...] = total[margin + tile :]
-
-
-def final_kernel(radius, tile, half, runs, nchunks, scal, inv, taps, rim, est, *rest):
-    mine, sib, rest = rest[:half], rest[half : half + len(runs)], rest[half + len(runs) :]
-    chunks, rest = rest[: 3 * nchunks], rest[3 * nchunks :]
-    out, lhs, s_hi, s_lo, total, rbuf, field, part, edge, sems = rest
-    first = fetch(rim, rbuf, sems.at[0])
-    late = [fetch(est, field, sems.at[1])]
-    at = 0
-    for c in range(nchunks):
-        main, above, below = chunks[3 * c : 3 * c + 3]
-        w = main.shape[1]
-        late.append(fetch(main, part.at[:, at : at + w], sems.at[2 + 3 * c]))
-        late.append(fetch(above, edge.at[0, :, at : at + w], sems.at[3 + 3 * c]))
-        late.append(fetch(below, edge.at[1, :, at : at + w], sems.at[4 + 3 * c]))
-        at += w
-    first.wait()
+    inside[...] = jnp.where(odd, total[:margin], total[margin + tile :])
+    across[...] = jnp.where(odd, total[margin + tile :], total[:margin])
+
+
+def middle_kernel(radius, tile, half, runs, scal, taps, rim, *rest):
+    mine, rest = rest[:half], rest[half:]
+    sib, rest = rest[: len(runs)], rest[len(runs) :]
+    first, second, inside, across, total, lhs, s_hi, s_lo, part, edge, sems = rest
+    width = first.shape[1]
+    late = [
+        fetch(first, part.at[:, :width], sems.at[0]),
+        fetch(second, part.at[:, width:], sems.at[1]),
+        *fetch_sides(scal[3, 2], inside, across, edge, sems.at[2], sems.at[3]),
+    ]
     slots = 2 * half
     margin = radius + MAXD
     mid = tile - 2 * margin
-    cols = est.shape[1]
+    cols = total.shape[1]
     blocks = cols // LANES
     wide = 2 * LANES * max(1, slots * mid // LANES)
     lane = lax.broadcasted_iota(jnp.int32, (tile, wide), 1)
     band = jnp.zeros((tile, wide), F32)
     for slot in range(slots):
         dx, dy = scal[0, slot], scal[1, slot]
-        value = slot_values(slot, half, runs, mine, sib) * rbuf[slot]
+        value = slot_values(slot, half, runs, mine, sib) * rim[slot]
         parts = ratio_blurred(slot, value, lhs, taps, dy, radius)
         base = slot * mid
         for j in range(1, blocks + 1):
@@ -257,10 +270,24 @@
     for copy in late:
         copy.wait()
     total[...] = both[:tile] + both[tile:] + mm(b_hi, s_lo[...]) + part[...]
-    total[:margin, :] += edge[0]
-    total[tile - margin :, :] += edge[1]
-    turned = pltpu.roll(total[...], LANES - margin, 1)
-    out[...] = field[...] * turned * inv[0]
+    total[:margin, :width] += edge[0]
+    total[tile - margin :, :width] += edge[1]
+
+
+def update_kernel(radius, tile, slots, scal, total, est, inside, across, out, edge, sems):
+    margin = radius + MAXD
+    copies = fetch_sides(scal[3, 2], inside, across, edge, sems.at[0], sems.at[1])
+    count = scal[2, 0]
+    for slot in range(1, slots):
+        count += scal[2, slot]
+    width, cols = inside.shape[1], est.shape[1]
+    weight = 1.0 / jnp.full((1, cols), count.astype(F32), F32)
+    for copy in copies:
+        copy.wait()
+    at = slice(cols - width, cols)
+    total[:margin, at] += edge[0]
+    total[tile - margin :, at] += edge[1]
+    out[...] = est[...] * weight * pltpu.roll(total[...], LANES - margin, 1)
 
 
 def light():
@@ -272,7 +299,11 @@
     ins, outs, sem = refs[:n_in], refs[n_in:-1], refs[-1]
     copies = []
     for i, (src, dst, start, src_at, dst_at) in enumerate(pieces):
-        ref = ins[src] if start is None else ins[src].at[pl.ds(scal[start], starts[start])]
+        ref = ins[src]
+        if start is not None and start < len(starts):
+            ref = ref.at[pl.ds(scal[start], starts[start])]
+        elif start is not None:
+            ref = ref.at[pl.ds(pl.multiple_of(scal[start], 8), outs[dst].shape[0])]
         copies.append(fetch(ref.at[src_at], outs[dst].at[dst_at], sem.at[i]))
     for copy in copies:
         copy.wait()
@@ -317,24 +348,24 @@
 
 def part_pair(scal, runs, kept, own, after):
     half = len(kept)
-    rows, cols = own.shape[1:]
-    shapes = [(rows, cols)] * half
-    shapes += [(rows, sum(c1 - c0 for _, c0, c1 in of) * LANES) for of in runs]
+    rows = own.shape[1]
+    shapes = [(rows, sum(c1 - c0 for _, c0, c1 in of) * LANES) for of in runs]
+    shapes += [(rows, own.shape[2])] * half
     out = pl.pallas_call(
         functools.partial(pair_kernel, half, runs),
         grid_spec=pltpu.PrefetchScalarGridSpec(
             num_scalar_prefetch=1,
             grid=(1,),
-            in_specs=[in_vmem()] * half + [in_hbm()] + [anywhere()] * len(after),
+            in_specs=[in_hbm()] * (half + 1) + [anywhere()] * len(after),
             out_specs=[in_vmem()] * len(shapes),
-            scratch_shapes=[pltpu.VMEM(own.shape, F32), pltpu.SemaphoreType.DMA((1,))],
+            scratch_shapes=[pltpu.SemaphoreType.DMA((half + sum(len(of) for of in runs),))],
         ),
         out_shape=[jax.ShapeDtypeStruct(s, F32) for s in shapes],
         compiler_params=params(),
         cost_estimate=light(),
         name="pair",
-    )(scal, *from_vmem(kept), *from_hbm([own]), *after)
-    return out[:half], out[half:]
+    )(scal, *from_hbm([*kept, own]), *after)
+    return out[: len(runs)], out[len(runs) :]
 
 
 def whole_spec(shape):
@@ -345,7 +376,7 @@
     return pltpu.CompilerParams(vmem_limit_bytes=VMEM_LIMIT, dimension_semantics=("arbitrary",))
 
 
-def forward(radius, cut, scal, taps, est, above, below):
+def forward(radius, cut, scal, taps, est, inside, across):
     slots = taps.shape[0]
     tile, cols = est.shape
     margin = radius + MAXD
@@ -372,7 +403,7 @@
         compiler_params=params(),
         cost_estimate=light(),
         name="forward",
-    )(scal, taps, *from_vmem([est]), *from_hbm([above, below]))
+    )(scal, taps, *from_vmem([est]), *from_hbm([inside, across]))
 
 
 def edges(radius, tile, is_first, is_last, runs, scal, taps, rim, mine, sib, carries):
@@ -387,13 +418,13 @@
         shapes.append(carried)
         if is_first:
             shapes.append(carried)
-    operands = [rim, *mine, *sib, *carries]
     return pl.pallas_call(
         functools.partial(edge_kernel, radius, tile, is_first, is_last, half, runs),
         grid_spec=pltpu.PrefetchScalarGridSpec(
             num_scalar_prefetch=1,
             grid=(1,),
-            in_specs=[whole_spec(taps.shape)] + [in_vmem()] * len(operands),
+            in_specs=[whole_spec(taps.shape)]
+            + [in_vmem()] * (1 + half + len(sib) + len(carries)),
             out_specs=[in_vmem()] * len(shapes),
             scratch_shapes=[
                 pltpu.VMEM((blocks * 2 * margin, 2 * LANES), BF16),
@@ -405,42 +436,57 @@
         compiler_params=params(),
         cost_estimate=light(),
         name="edges",
-    )(scal, taps, *from_vmem(operands))
-
-
-def finish(radius, runs, scal, inv, taps, rim, est, mine, sib, chunks):
+    )(scal, taps, *from_vmem([rim, *mine, *sib, *carries]))
+
+
+def middle(radius, tile, runs, scal, taps, rim, mine, sib, mains, inside, across):
     half = len(mine)
-    slots = 2 * half
-    margin = radius + MAXD
-    tile, cols = est.shape
-    mid = tile - 2 * margin
-    flat = [x for chunk in chunks for x in chunk]
+    slots, mid, cols = rim.shape
+    margin = radius + MAXD
     return pl.pallas_call(
-        functools.partial(final_kernel, radius, tile, half, runs, len(chunks)),
+        functools.partial(middle_kernel, radius, tile, half, runs),
         grid_spec=pltpu.PrefetchScalarGridSpec(
-            num_scalar_prefetch=2,
+            num_scalar_prefetch=1,
             grid=(1,),
-            in_specs=[whole_spec(taps.shape), in_hbm(), in_hbm()]
-            + [in_vmem()] * (half + len(runs))
-            + [in_hbm()] * len(flat),
-            out_specs=whole_spec(est.shape),
+            in_specs=[whole_spec(taps.shape)]
+            + [in_vmem()] * (1 + half + len(runs))
+            + [anywhere()] * 4,
+            out_specs=in_vmem(),
             scratch_shapes=[
                 pltpu.VMEM((cols // LANES * mid, 2 * LANES), BF16),
                 pltpu.VMEM((slots * mid, cols), BF16),
                 pltpu.VMEM((slots * mid, cols), BF16),
                 pltpu.VMEM((tile, cols), F32),
-                pltpu.VMEM(rim.shape, F32),
-                pltpu.VMEM((tile, cols), F32),
-                pltpu.VMEM((tile, cols), F32),
-                pltpu.VMEM((2, margin, cols), F32),
-                pltpu.SemaphoreType.DMA((2 + len(flat),)),
+                pltpu.VMEM((2,) + inside.shape, F32),
+                pltpu.SemaphoreType.DMA((4,)),
+            ],
+        ),
+        out_shape=jax.ShapeDtypeStruct((tile, cols), F32),
+        compiler_params=params(),
+        cost_estimate=light(),
+        name="middle",
+    )(scal, taps, *from_vmem([rim, *mine, *sib]), *mains, inside, across)
+
+
+def update(radius, slots, scal, total, est, inside, across):
+    tile = est.shape[0]
+    return pl.pallas_call(
+        functools.partial(update_kernel, radius, tile, slots),
+        grid_spec=pltpu.PrefetchScalarGridSpec(
+            num_scalar_prefetch=1,
+            grid=(1,),
+            in_specs=[in_vmem()] * 2 + [anywhere()] * 2,
+            out_specs=whole_spec(est.shape),
+            scratch_shapes=[
+                pltpu.VMEM((2,) + inside.shape, F32),
+                pltpu.SemaphoreType.DMA((2,)),
             ],
         ),
         out_shape=jax.ShapeDtypeStruct(est.shape, F32),
         compiler_params=params(),
         cost_estimate=light(),
-        name="finish",
-    )(scal, inv, taps, *from_hbm([rim, est]), *from_vmem([*mine, *sib]), *from_hbm(flat))
+        name="update",
+    )(scal, *from_vmem([total, est]), inside, across)
 
 
 def per_device(estimate, views, psf, offsets, lengths):
@@ -457,8 +503,9 @@
     est = estimate[0]
     total_blocks = cols // LANES
 
-    up = [(i, (i + 1) % joined) for i in range(joined)]
-    down = [(j, i) for i, j in up]
+    odd = lax.axis_index("joined") % 2
+    twin = [(i, i ^ 1) for i in range(joined)]
+    other = [(i, (i - 1 if i % 2 == 0 else i + 1) % joined) for i in range(joined)]
 
     def target(p, s):
         k, b = p // BLOCKS, p % BLOCKS
@@ -472,7 +519,9 @@
         for s in range(half)
     ]
     inner = (member // half == block).astype(jnp.int32)
-    away = jnp.stack(away + [1 - position % 2, inner]).astype(jnp.int32)
+    edge_at = (1 - odd) * (tile - margin)
+    away = away + [1 - position % 2, inner, edge_at, tile - margin - edge_at]
+    away = jnp.stack(away).astype(jnp.int32)
     starts = (2,) * half + (1,)
     top, bottom = slice(0, margin), slice(tile - margin, tile)
     low, high = slice(0, margin), slice(margin, 2 * margin)
@@ -494,7 +543,7 @@
         return sent
 
     def pair_send(runs, kept, own, after):
-        mine, others = part_pair(away, runs, kept, own, after)
+        others, mine = part_pair(away, runs, kept, own, after)
         return mine, [lax.ppermute(x, "view", [(p, p ^ 1) for p in range(size)]) for x in others]
 
     def edge_shape(c0, c1):
@@ -503,24 +552,30 @@
     packed_a = pack(
         away, starts, [stack], [], [edge_shape(*cut[0])] * half, edge_pieces(*cut[0]), "pack_first"
     )
-    kept_a = view_send(packed_a)
     slab = pack(
         away, starts, [est, psf], packed_a[:1], [(margin, cols)] * 2 + [psf.shape],
         [
-            (0, 0, None, (bottom,), (every,)),
-            (0, 1, None, (top,), (every,)),
+            (0, 0, half + 2, (every,), (every,)),
+            (0, 1, half + 3, (every,), (every,)),
             (1, 2, None, (every,), (every,)),
         ],
         "pack_slab",
     )
-    above = lax.ppermute(slab[0], "joined", up)
-    below = lax.ppermute(slab[1], "joined", down)
+    inside = lax.ppermute(slab[0], "joined", twin)
+    across = lax.ppermute(slab[1], "joined", other)
     psf = slab[2]
-    packed_b = pack(
-        away, starts, [stack], slab[:1], [edge_shape(*cut[1])] * half, edge_pieces(*cut[1]),
+    kept_a = view_send(packed_a)
+    center = slice(margin, tile - margin)
+    packed = pack(
+        away, starts, [stack], slab[:1],
+        [edge_shape(*cut[1])] * half + [(2, tile - 2 * margin, cols)] * half,
+        edge_pieces(*cut[1])
+        + [(0, half + s, s, (every, center), (every,)) for s in range(half)],
         "pack_second",
     )
+    packed_b, packed_c = packed[:half], packed[half:]
     kept_b = view_send(packed_b)
+    kept_c = view_send(packed_c)
 
     pair, core = position // 2, position % 2
     owned_block, place = pair // half, pair % half
@@ -540,36 +595,31 @@
     shifts = offsets[order]
     reach = lax.dynamic_index_in_dim(lengths, owned_block, 1, keepdims=False)
     live = (row < reach).astype(jnp.int32)
-    inv = (1.0 / jnp.sum(live).astype(F32)).reshape(1)
+    side = jnp.stack([core, (core == owned_block).astype(jnp.int32), odd])
+    side = jnp.pad(side, (0, members - 3))
     scal = jnp.stack(
-        [shifts[:, 0], shifts[:, 1], live[order], jnp.where(jnp.arange(members) == 0, core, (core == owned_block).astype(jnp.int32))]
+        [shifts[:, 0], shifts[:, 1], live[order], side]
     ).astype(jnp.int32)
 
-    rims = forward(radius, cut, scal, taps, est, above, below)
-    mid = slice(margin, tile - margin)
-    packed_c = pack(
-        away, starts, [stack], packed_b[:1], [(2, tile - 2 * margin, cols)] * half,
-        [(0, s, s, (every, slice(margin, tile - margin)), (every,)) for s in range(half)],
-        "pack_third",
-    )
-    kept_c = view_send(packed_c)
-
+    rims = forward(radius, cut, scal, taps, est, inside, across)
     chunks, carries, main = [], [], None
     for i, (kept, packed) in enumerate(((kept_a, packed_a), (kept_b, packed_b))):
-        runs = runs_of(half, half, cut[i][1] - cut[i][0])
+        runs = runs_of(half if i == 0 else 1, half, cut[i][1] - cut[i][0])
         mine, sib = pair_send(runs, kept, packed[-1], rims[-1:] if i == 0 else [main])
         is_first, is_last = i == 0, i == len(cut) - 1
         result = edges(
             radius, tile, is_first, is_last, runs, scal, taps, rims[i], mine, sib, carries
         )
-        main, upper, lower = result[:3]
+        main, inside, across = result[:3]
         carries = result[3:]
-        from_above = lax.ppermute(lower, "joined", up)
-        from_below = lax.ppermute(upper, "joined", down)
-        chunks.append((main, from_above, from_below))
+        inside = lax.ppermute(inside, "joined", twin)
+        across = lax.ppermute(across, "joined", other)
+        chunks.append((main, inside, across))
     runs = runs_of(3, half, total_blocks)
     mine, sib = pair_send(runs, kept_c, packed_c[-1], [main, *chunks[0][1:]])
-    out = finish(radius, runs, scal, inv, taps, rims[-1], est, mine, sib, chunks)
+    mains = [chunk[0] for chunk in chunks]
+    total = middle(radius, tile, runs, scal, taps, rims[-1], mine, sib, mains, *chunks[0][1:])
+    out = update(radius, members, scal, total, est, *chunks[1][1:])
     return out[None]
 
 

time: 82.3 us -> 76 us (0.923)
  waiting for transfers between devices: 15.3 us -> 9.75 us
  Pallas kernels: 34.9 us -> 31.7 us
  local copies, waits for them, and re-layouts: 2.96 us -> 4.75 us
  starting transfers between devices: 26.7 us -> 28 us
    ppermute x6, waiting for transfers between devices: 13.5 us -> 6.63 us  [the longest x1 6.62 us: per_device(): across = lax.ppermute(slab[1], 'joined', other)]
    ppermute x6, starting transfers between devices: 13.5 us -> 17.9 us  [the longest x2 11.9 us: per_device(): across = lax.ppermute(across, 'joined', other)]
    ppermute x7 -> x6, starting transfers between devices: 4.24 us -> 1.43 us  [pair_send(): lax.ppermute(x, 'view', [(p, p ^ 1) for p in range(size)])]
    pallas_call x3, Pallas kernels: 7.98 us -> 5.75 us  [part_pair(): pl.pallas_call(functools.partial(pair_kernel, half, runs), grid_spec=pltp...]
    unnamed x25 -> x23, local copies, waits for them, and re-layouts: 0.81 us -> 2.52 us
    pallas_call x4 -> x3, Pallas kernels: 9.36 us -> 7.69 us  [pack(): pl.pallas_call(functools.partial(pack_kernel, starts, pieces, len(ins) +...]
    ppermute x7 -> x6, waiting for transfers between devices: 1.79 us -> 3.1 us  [pair_send(): lax.ppermute(x, 'view', [(p, p ^ 1) for p in range(size)])]
    pallas_call x1 -> x2, Pallas kernels: 4.63 us -> 5.26 us  [the longest x1 2.74 us: middle(): pl.pallas_call(functools.partial(middle_kernel, radius, tile, half, runs)...]
  transfers between devices with their start and end apart: 19 -> 18, of which waited for: 6 -> 4; matrix products, arithmetic and copies ran while one was open for 4% -> 3% of each run, Pallas kernels for 29% -> 34%
where the time goes in v3:
time: 76 us; the launch traced here: 74.9 us
  Pallas kernels  31.7 us (42%)
  starting transfers between devices  28 us (37%)
  waiting for transfers between devices  9.75 us (13%)
  local copies, waits for them, and re-layouts  4.75 us (6%)
    ppermute x2, starting transfers between devices, per_device(): across = lax.ppermute(across, 'joined', other)  11.9 us
    ppermute x6, starting transfers between devices, view_send(): sent.append(lax.ppermute(x, 'view', [(p, q) for p, q in pairs if p != q]))  8.7 us
    pallas_call x3, Pallas kernels, pack(): pl.pallas_call(functools.partial(pack_kernel, starts, pieces, len(ins) +...  7.69 us
    pallas_call x1, Pallas kernels, forward(): pl.pallas_call(functools.partial(forward_kernel, radius, cut), grid_spec=...  7.09 us
    ppermute x1, waiting for transfers between devices, per_device(): across = lax.ppermute(slab[1], 'joined', other)  6.62 us
    pallas_call x2, Pallas kernels, edges(): pl.pallas_call(functools.partial(edge_kernel, radius, tile, is_first, is_...  5.9 us
    pallas_call x3, Pallas kernels, part_pair(): pl.pallas_call(functools.partial(pair_kernel, half, runs), grid_spec=pltp...  5.75 us
    ppermute x6, waiting for transfers between devices, pair_send(): lax.ppermute(x, 'view', [(p, p ^ 1) for p in range(size)])  3.1 us
  transfers between devices with their start and end apart: 18, of which 4 were waited for; matrix products, arithmetic and copies ran while one was open for 3% of the time, Pallas kernels for 34%

profile of v3, /device:TPU:0, one launch (start us, length us, event | category | flops | bytes accessed | tf_op | source)
XLA Modules:
  0.0 74.9 jit_solution(10040120470000870541)
XLA Ops:
  0.0 0.1 stack.78.refs_0_.scal
  0.1 1.9 %pack_first.1 = (f32[2,96,1024]{2,1,0:T(8,128)S(1)}, f32[2,96,1024]{2,1,0:T(8,128)S(1)}) custom-call(s32[6]{0:T(128)S(1)} %stack.78.refs_0_.scal, f32[4,128,2048]{2,1,0:T(8,128)} %bitcast.28), custom_call_target="tpu_custom_call" | custom-call | bytes 1024 | tf_op jit(solution)/shard_map/pack_first/pallas_call | solution.py:333
  2.0 3.0 %collective-permute-start.6 = (f32[2,96,1024]{2,1,0:T(8,128)S(1)}, f32[2,96,1024]{2,1,0:T(8,128)}, u32[]{:S(2)}, u32[]{:S(2)}) collective-permute-start(f32[2,96,1024]{2,1,0:T(8,128)S(1)} %get-tuple-element.37.refs_3_), channel_id=1, source_target_pairs={{0,2},{1,4},{2,0},{3,6},{4,1},{5,7},{6,3},{7,5},{8,10},{9,12},{10,... | collective-permute-start | bytes 2359304 | tf_op jit(solution)/shard_map/ppermute | solution.py:542
  5.0 2.6 %pack_slab.1 = (f32[48,2048]{1,0:T(8,128)}, f32[48,2048]{1,0:T(8,128)}, f32[4,2,65]{2,1,0:T(2,128)S(1)}) custom-call(s32[6]{0:T(128)S(1)} %stack.78.refs_0_.scal, f32[128,2048]{1,0:T(8,128)} %bitcast.25, f32[4,2,65]{2,1,0:T(2,128)} %refs_2_.1, f32[2,96,1024]{2,1,0:T(8,128)S(1)} %get-tuple-element.37.refs_3_), custom_call_target="tpu_custom_call" | custom-call | bytes 1024 | tf_op jit(solution)/shard_map/pack_slab/pallas_call | solution.py:333
  7.6 1.6 %collective-permute-start = (f32[48,2048]{1,0:T(8,128)}, f32[48,2048]{1,0:T(8,128)}, u32[]{:S(2)}, u32[]{:S(2)}) collective-permute-start(f32[48,2048]{1,0:T(8,128)} %get-tuple-element.39.refs_2_), channel_id=1, source_target_pairs={{0,8},{8,0},{16,24},{24,16},{1,9},{9,1},{17,25},{25,17},{2,10},{10... | collective-permute-start | bytes 1179656 | tf_op jit(solution)/shard_map/ppermute | solution.py:564
  9.3 2.5 %collective-permute-start.1 = (f32[48,2048]{1,0:T(8,128)}, f32[48,2048]{1,0:T(8,128)}, u32[]{:S(2)}, u32[]{:S(2)}) collective-permute-start(f32[48,2048]{1,0:T(8,128)} %get-tuple-element.40), channel_id=1, source_target_pairs={{0,24},{8,16},{16,8},{24,0},{1,25},{9,17},{17,9},{25,1},{2,26},{10... | collective-permute-start | bytes 1179656 | tf_op jit(solution)/shard_map/ppermute | solution.py:565
  11.8 1.7 %collective-permute-start.7 = (f32[2,96,1024]{2,1,0:T(8,128)S(1)}, f32[2,96,1024]{2,1,0:T(8,128)}, u32[]{:S(2)}, u32[]{:S(2)}) collective-permute-start(f32[2,96,1024]{2,1,0:T(8,128)S(1)} %get-tuple-element.48.refs_2_), channel_id=1, source_target_pairs={{1,6},{3,4},{4,3},{6,1},{9,14},{11,12},{12,11},{14,9},{17,22},{19,... | collective-permute-start | bytes 2359304 | tf_op jit(solution)/shard_map/ppermute | solution.py:542
  13.5 3.2 %pack_second.1 = (f32[2,96,1024]{2,1,0:T(8,128)}, f32[2,96,1024]{2,1,0:T(8,128)S(1)}, f32[2,32,2048]{2,1,0:T(8,128)S(1)}, f32[2,32,2048]{2,1,0:T(8,128)S(1)}) custom-call(s32[6]{0:T(128)S(1)} %stack.78.refs_0_.scal, f32[4,128,2048]{2,1,0:T(8,128)} %bitcast.29, f32[48,2048]{1,0:T(8,128)} %get-tuple-element.39.refs_2_), custom_call_target="tpu_custom_call" | custom-call | bytes 1024 | tf_op jit(solution)/shard_map/pack_second/pallas_call | solution.py:333
  16.6 0.0 copy-done.2
  16.6 0.0 copy-start.3
  16.7 0.8 %copy-done.3 = f32[2,32,2048]{2,1,0:T(8,128)} copy-done((f32[2,32,2048]{2,1,0:T(8,128)}, f32[2,32,2048]{2,1,0:T(8,128)S(1)}, u32[]{:S(2)}) %copy-start.3) | copy-done | bytes 524312
  17.5 0.8 %copy-done.5 = f32[2,32,2048]{2,1,0:T(8,128)} copy-done((f32[2,32,2048]{2,1,0:T(8,128)}, f32[2,32,2048]{2,1,0:T(8,128)S(1)}, u32[]{:S(2)}) %copy-start.5) | copy-done | bytes 524312
  18.3 0.5 collective-permute-start.4
  18.8 0.1 reduce_sum.9
  18.9 0.1 broadcast_divide_fusion
  19.1 0.1 rev.6
  19.2 0.1 rev.7
  19.3 0.1 fusion.1
  19.4 0.0 collective-permute-done.inside
  19.4 1.6 %collective-permute-start.5 = (f32[2,96,1024]{2,1,0:T(8,128)S(1)}, f32[2,96,1024]{2,1,0:T(8,128)}, u32[]{:S(2)}, u32[]{:S(2)}) collective-permute-start(f32[2,96,1024]{2,1,0:T(8,128)S(1)} %get-tuple-element.46.refs_2_), channel_id=1, source_target_pairs={{1,6},{3,4},{4,3},{6,1},{9,14},{11,12},{12,11},{14,9},{17,22},{19,... | collective-permute-start | bytes 2359304 | tf_op jit(solution)/shard_map/ppermute | solution.py:542
  21.0 0.1 pad_add_fusion.1
  21.0 0.6 gather_fusion.2
  21.6 0.1 copy.7
  21.7 0.6 gather_fusion
  22.3 0.6 gather_fusion.1
  22.9 0.2 slice_reduce_fusion.1
  23.1 6.6 %collective-permute-done.1.across = f32[48,2048]{1,0:T(8,128)} collective-permute-done((f32[48,2048]{1,0:T(8,128)}, f32[48,2048]{1,0:T(8,128)}, u32[]{:S(2)}, u32[]{:S(2)}) %collective-permute-start.1) | collective-permute-done | bytes 393248 | tf_op jit(solution)/shard_map/ppermute | solution.py:565
  29.8 7.1 %forward.1 = (f32[4,96,1024]{2,1,0:T(8,128)S(1)}, f32[4,96,1024]{2,1,0:T(8,128)S(1)}, f32[4,32,2048]{2,1,0:T(8,128)S(1)}) custom-call(s32[4,4]{1,0:T(4,128)S(1)} %pad_add_fusion.scal, f32[4,4,256]{2,1,0:T(4,128)S(1)} %gather.15.taps, f32[128,2048]{1,0:T(8,128)S(1)} %bitcast.26, f32[48,2048]{1,0:T(8,128)} %collective-permute-done.inside, ...), custom_call_target="tpu_custom_call" | custom-call | bytes 1024 | tf_op jit(solution)/shard_map/forward/pallas_call | solution.py:386
  36.8 0.0 collective-permute-done.6.refs_0_
  36.9 0.0 collective-permute-done.7.refs_1_
  36.9 1.9 %pair.3 = (f32[96,1024]{1,0:T(8,128)S(1)}, f32[96,1024]{1,0:T(8,128)S(1)}, f32[96,1024]{1,0:T(8,128)S(1)}, f32[96,1024]{1,0:T(8,128)S(1)}) custom-call(s32[6]{0:T(128)S(1)} %stack.78.refs_0_.scal, f32[2,96,1024]{2,1,0:T(8,128)} %collective-permute-done.6.refs_0_, f32[2,96,1024]{2,1,0:T(8,128)} %collective-permute-done.7.refs_1_, f32[2,96,1024]{2,1,0:T(8,128)} %copy-done.2, ...), custom_call_target="tpu_custom_call" | custom-call | bytes 1024 | tf_op jit(solution)/shard_map/pair/pallas_call | solution.py:354
  38.8 0.1 collective-permute-start.8
  38.9 0.5 collective-permute-start.9
  39.4 1.2 %collective-permute-done.8.rest_2_ = f32[96,1024]{1,0:T(8,128)S(1)} collective-permute-done((f32[96,1024]{1,0:T(8,128)S(1)}, f32[96,1024]{1,0:T(8,128)S(1)}, u32[]{:S(2)}, u32[]{:S(2)}) %collective-permute-start.8) | collective-permute-done | bytes 393248 | tf_op jit(solution)/shard_map/ppermute | solution.py:547
  40.6 0.6 collective-permute-done.9.rest_3_
  41.2 2.9 %edges.2 = (f32[128,896]{1,0:T(8,128)S(1)}, f32[48,896]{1,0:T(8,128)S(1)}, f32[48,896]{1,0:T(8,128)S(1)}, f32[4,96,128]{2,1,0:T(8,128)S(1)}, f32[4,96,128]{2,1,0:T(8,128)S(1)}) custom-call(s32[4,4]{1,0:T(4,128)S(1)} %pad_add_fusion.scal, f32[4,4,256]{2,1,0:T(4,128)S(1)} %gather.15.taps, f32[4,96,1024]{2,1,0:T(8,128)S(1)} %get-tuple-element.47.rim, ...), custom_call_target="tpu_custom_call" | custom-call | bytes 1024 | tf_op jit(solution)/shard_map/edges/pallas_call | solution.py:421
  44.1 0.0 collective-permute-done.4.refs_0_
  44.1 0.0 collective-permute-done.5.refs_1_
  44.1 1.9 %pair.4 = (f32[96,2048]{1,0:T(8,128)S(1)}, f32[96,1024]{1,0:T(8,128)S(1)}, f32[96,1024]{1,0:T(8,128)S(1)}) custom-call(s32[6]{0:T(128)S(1)} %stack.78.refs_0_.scal, f32[2,96,1024]{2,1,0:T(8,128)} %collective-permute-done.4.refs_0_, f32[2,96,1024]{2,1,0:T(8,128)} %collective-permute-done.5.refs_1_, f32[2,96,1024]{2,1,0:T(8,128)} %copy-done.1, ...), custom_call_target="tpu_custom_call" | custom-call | bytes 1024 | tf_op jit(solution)/shard_map/pair/pallas_call | solution.py:354
  46.1 0.2 collective-permute-start.10
  46.3 1.2 %collective-permute-start.2 = (f32[2,32,2048]{2,1,0:T(8,128)S(1)}, f32[2,32,2048]{2,1,0:T(8,128)S(1)}, u32[]{:S(2)}, u32[]{:S(2)}) collective-permute-start(f32[2,32,2048]{2,1,0:T(8,128)S(1)} %copy-done.6), channel_id=1, source_target_pairs={{0,2},{1,4},{2,0},{3,6},{4,1},{5,7},{6,3},{7,5},{8,10},{9,12},{10,... | collective-permute-start | bytes 1572872 | tf_op jit(solution)/shard_map/ppermute | solution.py:542
  47.5 0.7 collective-permute-start.3
  48.2 0.8 %collective-permute-start.11 = (f32[48,896]{1,0:T(8,128)S(1)}, f32[48,896]{1,0:T(8,128)S(1)}, u32[]{:S(2)}, u32[]{:S(2)}) collective-permute-start(f32[48,896]{1,0:T(8,128)S(1)} %get-tuple-element.60), channel_id=1, source_target_pairs={{0,8},{8,0},{16,24},{24,16},{1,9},{9,1},{17,25},{25,17},{2,10},{10... | collective-permute-start | bytes 516104 | tf_op jit(solution)/shard_map/ppermute | solution.py:615
  48.9 6.0 %collective-permute-start.12 = (f32[48,896]{1,0:T(8,128)S(1)}, f32[48,896]{1,0:T(8,128)S(1)}, u32[]{:S(2)}, u32[]{:S(2)}) collective-permute-start(f32[48,896]{1,0:T(8,128)S(1)} %get-tuple-element.61), channel_id=1, source_target_pairs={{0,24},{8,16},{16,8},{24,0},{1,25},{9,17},{17,9},{25,1},{2,26},{10... | collective-permute-start | bytes 516104 | tf_op jit(solution)/shard_map/ppermute | solution.py:616
  54.9 0.0 collective-permute-done.10.rest_2_
  54.9 3.0 %edges.3 = (f32[128,1152]{1,0:T(8,128)S(1)}, f32[48,1152]{1,0:T(8,128)S(1)}, f32[48,1152]{1,0:T(8,128)S(1)}) custom-call(s32[4,4]{1,0:T(4,128)S(1)} %pad_add_fusion.scal, f32[4,4,256]{2,1,0:T(4,128)S(1)} %gather.15.taps, f32[4,96,1024]{2,1,0:T(8,128)S(1)} %get-tuple-element.44.rim, f32[96,1024]{1,0:T(8,128)S(1)} %get-tuple-element.54.rest_0_, ...), custom_call_target="tpu_custom_call" | custom-call | bytes 1024 | tf_op jit(solution)/shard_map/edges/pallas_call | solution.py:421
  57.9 1.1 %collective-permute-start.16 = (f32[48,1152]{1,0:T(8,128)S(1)}, f32[48,1152]{1,0:T(8,128)S(1)}, u32[]{:S(2)}, u32[]{:S(2)}) collective-permute-start(f32[48,1152]{1,0:T(8,128)S(1)} %get-tuple-element.67), channel_id=1, source_target_pairs={{0,8},{8,0},{16,24},{24,16},{1,9},{9,1},{17,25},{25,17},{2,10},{10... | collective-permute-start | bytes 663560 | tf_op jit(solution)/shard_map/ppermute | solution.py:615
  59.0 0.0 collective-permute-done.2.refs_0_
  59.0 5.9 %collective-permute-start.17 = (f32[48,1152]{1,0:T(8,128)S(1)}, f32[48,1152]{1,0:T(8,128)S(1)}, u32[]{:S(2)}, u32[]{:S(2)}) collective-permute-start(f32[48,1152]{1,0:T(8,128)S(1)} %get-tuple-element.68), channel_id=1, source_target_pairs={{0,24},{8,16},{16,8},{24,0},{1,25},{9,17},{17,9},{25,1},{2,26},{10... | collective-permute-start | bytes 663560 | tf_op jit(solution)/shard_map/ppermute | solution.py:616
  64.9 0.0 collective-permute-done.3.refs_1_
  64.9 0.0 collective-permute-done.11.refs_4_.rest_7_
  65.0 0.0 collective-permute-done.12.refs_5_.rest_8_
  65.0 0.8 %copy-done.8 = f32[2,32,2048]{2,1,0:T(8,128)} copy-done((f32[2,32,2048]{2,1,0:T(8,128)}, f32[2,32,2048]{2,1,0:T(8,128)S(1)}, u32[]{:S(2)}) %copy-start.8) | copy-done | bytes 524312
  65.8 1.9 %pair.5 = (f32[32,1408]{1,0:T(8,128)S(1)}, f32[32,1280]{1,0:T(8,128)S(1)}, f32[32,1408]{1,0:T(8,128)S(1)}, f32[32,2048]{1,0:T(8,128)S(1)}, f32[32,2048]{1,0:T(8,128)S(1)}) custom-call(s32[6]{0:T(128)S(1)} %stack.78.refs_0_.scal, f32[2,32,2048]{2,1,0:T(8,128)} %copy-done.7, f32[2,32,2048]{2,1,0:T(8,128)} %copy-done.8, f32[2,32,2048]{2,1,0:T(8,128)} %copy-done.3, ...), custom_call_target="tpu_custom_call" | custom-call | bytes 1024 | tf_op jit(solution)/shard_map/pair/pallas_call | solution.py:354
  67.6 0.1 collective-permute-start.13
  67.7 0.5 collective-permute-start.15
  68.2 0.1 collective-permute-start.14
  68.3 1.3 %collective-permute-done.14.rest_3_ = f32[32,1280]{1,0:T(8,128)S(1)} collective-permute-done((f32[32,1280]{1,0:T(8,128)S(1)}, f32[32,1280]{1,0:T(8,128)S(1)}, u32[]{:S(2)}, u32[]{:S(2)}) %collective-permute-start.14) | collective-permute-done | bytes 163872 | tf_op jit(solution)/shard_map/ppermute | solution.py:547
  69.6 0.0 collective-permute-done.13.rest_2_
  69.6 0.0 collective-permute-done.15.rest_4_
  69.6 2.7 %middle.1.total = f32[128,2048]{1,0:T(8,128)S(1)} custom-call(s32[4,4]{1,0:T(4,128)S(1)} %pad_add_fusion.scal, f32[4,4,256]{2,1,0:T(4,128)S(1)} %gather.15.taps, f32[4,32,2048]{2,1,0:T(8,128)S(1)} %get-tuple-element.41.refs_3_.rim, f32[32,2048]{1,0:T(8,128)S(1)} %get-tuple-element.62.rest_0_, f32[32,2048]{1,0:T(8,128)S(1)} %get-tuple-element.63.rest_1_, ...), custom_call_target="tpu_custom_call" | custom-call | bytes 1024 | tf_op jit(solution)/shard_map/middle/pallas_call | solution.py:446
  72.4 0.0 collective-permute-done.16.inside
  72.4 0.0 collective-permute-done.17.across
  72.4 2.5 %update.1 = f32[128,2048]{1,0:T(8,128)} custom-call(s32[4,4]{1,0:T(4,128)S(1)} %pad_add_fusion.scal, f32[128,2048]{1,0:T(8,128)S(1)} %middle.1.total, f32[128,2048]{1,0:T(8,128)S(1)} %bitcast.27, f32[48,1152]{1,0:T(8,128)S(1)} %collective-permute-done.16.inside, f32[48,1152]{1,0:T(8,128)S(1)} %collective-permute-done.17.across), custom_call_target="tpu_custom_call" | custom-call | bytes 1024 | tf_op jit(solution)/shard_map/update/pallas_call | solution.py:473
  (24 shorter events, 0.1 us)
Async XLA Ops:
  2.0 14.6 %copy-start.2 = (f32[2,96,1024]{2,1,0:T(8,128)}, f32[2,96,1024]{2,1,0:T(8,128)S(1)}, u32[]{:S(2)}) copy-start(f32[2,96,1024]{2,1,0:T(8,128)S(1)} %get-tuple-element.48.refs_2_) | copy-start | bytes 2359300
  2.0 34.8 %collective-permute-start.6 = (f32[2,96,1024]{2,1,0:T(8,128)S(1)}, f32[2,96,1024]{2,1,0:T(8,128)}, u32[]{:S(2)}, u32[]{:S(2)}) collective-permute-start(f32[2,96,1024]{2,1,0:T(8,128)S(1)} %get-tuple-element.37.refs_3_), channel_id=1, source_target_pairs={{0,2},{1,4},{2,0},{3,6},{4,1},{5,7},{6,3},{7,5},{8,10},{9,12},{10,... | collective-permute-start | bytes 2359304 | tf_op jit(solution)/shard_map/ppermute | solution.py:542
  7.6 11.8 %collective-permute-start = (f32[48,2048]{1,0:T(8,128)}, f32[48,2048]{1,0:T(8,128)}, u32[]{:S(2)}, u32[]{:S(2)}) collective-permute-start(f32[48,2048]{1,0:T(8,128)} %get-tuple-element.39.refs_2_), channel_id=1, source_target_pairs={{0,8},{8,0},{16,24},{24,16},{1,9},{9,1},{17,25},{25,17},{2,10},{10... | collective-permute-start | bytes 1179656 | tf_op jit(solution)/shard_map/ppermute | solution.py:564
  9.3 20.5 %collective-permute-start.1 = (f32[48,2048]{1,0:T(8,128)}, f32[48,2048]{1,0:T(8,128)}, u32[]{:S(2)}, u32[]{:S(2)}) collective-permute-start(f32[48,2048]{1,0:T(8,128)} %get-tuple-element.40), channel_id=1, source_target_pairs={{0,24},{8,16},{16,8},{24,0},{1,25},{9,17},{17,9},{25,1},{2,26},{10... | collective-permute-start | bytes 1179656 | tf_op jit(solution)/shard_map/ppermute | solution.py:565
  11.8 7.2 %copy-start.10 = (s32[4,2]{0,1:T(2,128)S(1)}, s32[4,2]{0,1:T(2,128)}, u32[]{:S(2)}) copy-start(s32[4,2]{0,1:T(2,128)} %param.9) | copy-start | bytes 100
  11.8 9.9 %copy-start.9 = (s32[4,2]{0,1:T(2,128)S(1)}, s32[4,2]{0,1:T(2,128)}, u32[]{:S(2)}) copy-start(s32[4,2]{0,1:T(2,128)} %param.8) | copy-start | bytes 100
  11.8 18.0 %copy-start = (f32[1,128,2048]{2,1,0:T(8,128)S(1)}, f32[1,128,2048]{2,1,0:T(8,128)}, u32[]{:S(2)}) copy-start(f32[1,128,2048]{2,1,0:T(8,128)} %param.5) | copy-start | bytes 3145732
  11.8 25.1 %collective-permute-start.7 = (f32[2,96,1024]{2,1,0:T(8,128)S(1)}, f32[2,96,1024]{2,1,0:T(8,128)}, u32[]{:S(2)}, u32[]{:S(2)}) collective-permute-start(f32[2,96,1024]{2,1,0:T(8,128)S(1)} %get-tuple-element.48.refs_2_), channel_id=1, source_target_pairs={{1,6},{3,4},{4,3},{6,1},{9,14},{11,12},{12,11},{14,9},{17,22},{19,... | collective-permute-start | bytes 2359304 | tf_op jit(solution)/shard_map/ppermute | solution.py:542
  16.6 0.8 %copy-start.3 = (f32[2,32,2048]{2,1,0:T(8,128)}, f32[2,32,2048]{2,1,0:T(8,128)S(1)}, u32[]{:S(2)}) copy-start(f32[2,32,2048]{2,1,0:T(8,128)S(1)} %get-tuple-element.43.refs_2_) | copy-start | bytes 1572868
  17.5 0.8 %copy-start.5 = (f32[2,32,2048]{2,1,0:T(8,128)}, f32[2,32,2048]{2,1,0:T(8,128)S(1)}, u32[]{:S(2)}) copy-start(f32[2,32,2048]{2,1,0:T(8,128)S(1)} %get-tuple-element.42) | copy-start | bytes 1572868
  18.3 20.5 %copy-start.1 = (f32[2,96,1024]{2,1,0:T(8,128)}, f32[2,96,1024]{2,1,0:T(8,128)S(1)}, u32[]{:S(2)}) copy-start(f32[2,96,1024]{2,1,0:T(8,128)S(1)} %get-tuple-element.46.refs_2_) | copy-start | bytes 2359300
  18.3 25.8 %collective-permute-start.4 = (f32[2,96,1024]{2,1,0:T(8,128)}, f32[2,96,1024]{2,1,0:T(8,128)}, u32[]{:S(2)}, u32[]{:S(2)}) collective-permute-start(f32[2,96,1024]{2,1,0:T(8,128)} %get-tuple-element.45), channel_id=1, source_target_pairs={{0,2},{1,4},{2,0},{3,6},{4,1},{5,7},{6,3},{7,5},{8,10},{9,12},{10,... | collective-permute-start | bytes 2359304 | tf_op jit(solution)/shard_map/ppermute | solution.py:542
  19.4 24.7 %collective-permute-start.5 = (f32[2,96,1024]{2,1,0:T(8,128)S(1)}, f32[2,96,1024]{2,1,0:T(8,128)}, u32[]{:S(2)}, u32[]{:S(2)}) collective-permute-start(f32[2,96,1024]{2,1,0:T(8,128)S(1)} %get-tuple-element.46.refs_2_), channel_id=1, source_target_pairs={{1,6},{3,4},{4,3},{6,1},{9,14},{11,12},{12,11},{14,9},{17,22},{19,... | collective-permute-start | bytes 2359304 | tf_op jit(solution)/shard_map/ppermute | solution.py:542
  38.8 1.8 %collective-permute-start.8 = (f32[96,1024]{1,0:T(8,128)S(1)}, f32[96,1024]{1,0:T(8,128)S(1)}, u32[]{:S(2)}, u32[]{:S(2)}) collective-permute-start(f32[96,1024]{1,0:T(8,128)S(1)} %get-tuple-element.51), channel_id=1, source_target_pairs={{0,1},{1,0},{2,3},{3,2},{4,5},{5,4},{6,7},{7,6},{8,9},{9,8},{10,11... | collective-permute-start | bytes 1179656 | tf_op jit(solution)/shard_map/ppermute | solution.py:547
  38.9 2.3 %collective-permute-start.9 = (f32[96,1024]{1,0:T(8,128)S(1)}, f32[96,1024]{1,0:T(8,128)S(1)}, u32[]{:S(2)}, u32[]{:S(2)}) collective-permute-start(f32[96,1024]{1,0:T(8,128)S(1)} %get-tuple-element.52), channel_id=1, source_target_pairs={{0,1},{1,0},{2,3},{3,2},{4,5},{5,4},{6,7},{7,6},{8,9},{9,8},{10,11... | collective-permute-start | bytes 1179656 | tf_op jit(solution)/shard_map/ppermute | solution.py:547
  44.1 2.2 %copy-start.6 = (f32[2,32,2048]{2,1,0:T(8,128)S(1)}, f32[2,32,2048]{2,1,0:T(8,128)}, u32[]{:S(2)}) copy-start(f32[2,32,2048]{2,1,0:T(8,128)} %copy-done.5) | copy-start | bytes 1572868
  44.1 3.4 %copy-start.4 = (f32[2,32,2048]{2,1,0:T(8,128)S(1)}, f32[2,32,2048]{2,1,0:T(8,128)}, u32[]{:S(2)}) copy-start(f32[2,32,2048]{2,1,0:T(8,128)} %copy-done.3) | copy-start | bytes 1572868
  46.1 8.9 %collective-permute-start.10 = (f32[96,2048]{1,0:T(8,128)S(1)}, f32[96,2048]{1,0:T(8,128)S(1)}, u32[]{:S(2)}, u32[]{:S(2)}) collective-permute-start(f32[96,2048]{1,0:T(8,128)S(1)} %get-tuple-element.56), channel_id=1, source_target_pairs={{0,1},{1,0},{2,3},{3,2},{4,5},{5,4},{6,7},{7,6},{8,9},{9,8},{10,11... | collective-permute-start | bytes 2359304 | tf_op jit(solution)/shard_map/ppermute | solution.py:547
  46.3 12.8 %collective-permute-start.2 = (f32[2,32,2048]{2,1,0:T(8,128)S(1)}, f32[2,32,2048]{2,1,0:T(8,128)S(1)}, u32[]{:S(2)}, u32[]{:S(2)}) collective-permute-start(f32[2,32,2048]{2,1,0:T(8,128)S(1)} %copy-done.6), channel_id=1, source_target_pairs={{0,2},{1,4},{2,0},{3,6},{4,1},{5,7},{6,3},{7,5},{8,10},{9,12},{10,... | collective-permute-start | bytes 1572872 | tf_op jit(solution)/shard_map/ppermute | solution.py:542
  47.5 17.5 %collective-permute-start.3 = (f32[2,32,2048]{2,1,0:T(8,128)S(1)}, f32[2,32,2048]{2,1,0:T(8,128)S(1)}, u32[]{:S(2)}, u32[]{:S(2)}) collective-permute-start(f32[2,32,2048]{2,1,0:T(8,128)S(1)} %copy-done.4), channel_id=1, source_target_pairs={{1,6},{3,4},{4,3},{6,1},{9,14},{11,12},{12,11},{14,9},{17,22},{19,... | collective-permute-start | bytes 1572872 | tf_op jit(solution)/shard_map/ppermute | solution.py:542
  48.2 16.8 %collective-permute-start.11 = (f32[48,896]{1,0:T(8,128)S(1)}, f32[48,896]{1,0:T(8,128)S(1)}, u32[]{:S(2)}, u32[]{:S(2)}) collective-permute-start(f32[48,896]{1,0:T(8,128)S(1)} %get-tuple-element.60), channel_id=1, source_target_pairs={{0,8},{8,0},{16,24},{24,16},{1,9},{9,1},{17,25},{25,17},{2,10},{10... | collective-permute-start | bytes 516104 | tf_op jit(solution)/shard_map/ppermute | solution.py:615
  48.9 16.0 %collective-permute-start.12 = (f32[48,896]{1,0:T(8,128)S(1)}, f32[48,896]{1,0:T(8,128)S(1)}, u32[]{:S(2)}, u32[]{:S(2)}) collective-permute-start(f32[48,896]{1,0:T(8,128)S(1)} %get-tuple-element.61), channel_id=1, source_target_pairs={{0,24},{8,16},{16,8},{24,0},{1,25},{9,17},{17,9},{25,1},{2,26},{10... | collective-permute-start | bytes 516104 | tf_op jit(solution)/shard_map/ppermute | solution.py:616
  57.9 14.5 %collective-permute-start.16 = (f32[48,1152]{1,0:T(8,128)S(1)}, f32[48,1152]{1,0:T(8,128)S(1)}, u32[]{:S(2)}, u32[]{:S(2)}) collective-permute-start(f32[48,1152]{1,0:T(8,128)S(1)} %get-tuple-element.67), channel_id=1, source_target_pairs={{0,8},{8,0},{16,24},{24,16},{1,9},{9,1},{17,25},{25,17},{2,10},{10... | collective-permute-start | bytes 663560 | tf_op jit(solution)/shard_map/ppermute | solution.py:615
  59.0 5.9 %copy-start.7 = (f32[2,32,2048]{2,1,0:T(8,128)}, f32[2,32,2048]{2,1,0:T(8,128)S(1)}, u32[]{:S(2)}) copy-start(f32[2,32,2048]{2,1,0:T(8,128)S(1)} %collective-permute-done.2.refs_0_) | copy-start | bytes 1572868
  59.0 13.3 %collective-permute-start.17 = (f32[48,1152]{1,0:T(8,128)S(1)}, f32[48,1152]{1,0:T(8,128)S(1)}, u32[]{:S(2)}, u32[]{:S(2)}) collective-permute-start(f32[48,1152]{1,0:T(8,128)S(1)} %get-tuple-element.68), channel_id=1, source_target_pairs={{0,24},{8,16},{16,8},{24,0},{1,25},{9,17},{17,9},{25,1},{2,26},{10... | collective-permute-start | bytes 663560 | tf_op jit(solution)/shard_map/ppermute | solution.py:616
  64.9 0.8 %copy-start.8 = (f32[2,32,2048]{2,1,0:T(8,128)}, f32[2,32,2048]{2,1,0:T(8,128)S(1)}, u32[]{:S(2)}) copy-start(f32[2,32,2048]{2,1,0:T(8,128)S(1)} %collective-permute-done.3.refs_1_) | copy-start | bytes 1572868
  67.6 2.0 %collective-permute-start.13 = (f32[32,1408]{1,0:T(8,128)S(1)}, f32[32,1408]{1,0:T(8,128)S(1)}, u32[]{:S(2)}, u32[]{:S(2)}) collective-permute-start(f32[32,1408]{1,0:T(8,128)S(1)} %get-tuple-element.64), channel_id=1, source_target_pairs={{0,1},{1,0},{2,3},{3,2},{4,5},{5,4},{6,7},{7,6},{8,9},{9,8},{10,11... | collective-permute-start | bytes 540680 | tf_op jit(solution)/shard_map/ppermute | solution.py:547
  67.7 1.9 %collective-permute-start.15 = (f32[32,1408]{1,0:T(8,128)S(1)}, f32[32,1408]{1,0:T(8,128)S(1)}, u32[]{:S(2)}, u32[]{:S(2)}) collective-permute-start(f32[32,1408]{1,0:T(8,128)S(1)} %get-tuple-element.66), channel_id=1, source_target_pairs={{0,1},{1,0},{2,3},{3,2},{4,5},{5,4},{6,7},{7,6},{8,9},{9,8},{10,11... | collective-permute-start | bytes 540680 | tf_op jit(solution)/shard_map/ppermute | solution.py:547
  68.2 1.4 %collective-permute-start.14 = (f32[32,1280]{1,0:T(8,128)S(1)}, f32[32,1280]{1,0:T(8,128)S(1)}, u32[]{:S(2)}, u32[]{:S(2)}) collective-permute-start(f32[32,1280]{1,0:T(8,128)S(1)} %get-tuple-element.65), channel_id=1, source_target_pairs={{0,1},{1,0},{2,3},{3,2},{4,5},{5,4},{6,7},{7,6},{8,9},{9,8},{10,11... | collective-permute-start | bytes 491528 | tf_op jit(solution)/shard_map/ppermute | solution.py:547

commit v4 on v3

--- a/solution.py
+++ b/solution.py
@@ -24,16 +24,31 @@
     return jnp.dot(a, b, preferred_element_type=F32)
 
 
+def slot_view(info, names, slot, half):
+    core, block = info[names["core"]], info[names["block"]]
+    other = slot >= half
+    if isinstance(slot, int):
+        side = 1 - core if other else core
+        turn = slot % half
+    else:
+        side = jnp.where(other, 1 - core, core)
+        turn = lax.rem(slot, half)
+    step = jnp.where(side == block, 1, 0)
+    return side * half + lax.rem(info[names["place"]] - turn - step + 2 * half, half)
+
+
+def alive(info, names, lengths, slot, half):
+    view = slot_view(info, names, slot, half)
+    return jnp.where(info[names["row"]] < lengths[view, info[names["block"]]], 1.0, 0.0)
+
+
 def toeplitz(row, rows, shift, width):
     turned = pltpu.roll(jnp.broadcast_to(row, (8, width)), lax.rem(shift + 4 * width, width), 1)
     wide = jnp.broadcast_to(turned[0:1], (rows, width))
     return pltpu.roll(wide, 0, 1, stride=1, stride_axis=0)
 
 
-def lateral_factors(row, shift):
-    width = row.shape[1]
-    left = toeplitz(row, LANES, shift, width)[:, :LANES]
-    right = toeplitz(row, LANES, shift + LANES, width)[:, :LANES]
+def side_by_side(left, right):
     hi, lo = split(jnp.concatenate([left, right], axis=1))
     return jnp.concatenate([hi, hi], axis=0), lo
 
@@ -51,17 +66,84 @@
     ]
 
 
-def forward_kernel(radius, cut, scal, taps, est, inside, across, *rest):
+def images(lhs, first, second, rows, blocks):
+    part = mm(lhs[...], first) + mm(lhs[:, :LANES], second)
+    result = []
+    for j in range(blocks):
+        n = (j + 1) % blocks
+        here = part[j * rows : (j + 1) * rows, :LANES]
+        result.append(here + part[n * rows : (n + 1) * rows, LANES:])
+    return result
+
+
+def spread(value, lhs):
+    rows, cols = value.shape
+    hi, lo = split(value)
+    for j in range(cols // LANES):
+        at = slice(j * LANES, (j + 1) * LANES)
+        lhs[j * rows : (j + 1) * rows, :LANES] = hi[:, at]
+        lhs[j * rows : (j + 1) * rows, LANES:] = lo[:, at]
+
+
+def prepare_kernel(radius, names, info, offsets, lengths, psf, est, *refs):
+    rim, fx, fy, fy_low, by, by_low, bx, bm, hi, lo, lhs, taps = refs
+    slot = pl.program_id(0)
+    half = rim.shape[0] // 2
+    margin = radius + MAXD
+    tile, cols = est.shape
+    extended = tile + 2 * margin
+    mid = tile - 2 * margin
+    width = taps.shape[1]
+
+    @pl.when(slot == 0)
+    def _():
+        hi[...], lo[...] = split(pltpu.roll(est[...], margin, 1))
+        taps[...] = jnp.zeros(taps.shape, F32)
+
+    view = slot_view(info, names, slot, half)
+    dx, dy = offsets[view, 0], offsets[view, 1]
+    weights = psf[view]
+    taps[0:2, : 2 * radius + 1] = weights / jnp.sum(weights, axis=1, keepdims=True)
+    gx, gy = taps[0:1, :], taps[1:2, :]
+    band = toeplitz(gx, tile, dx + MAXD, width)
+    back = jnp.transpose(band)[:extended, :]
+    band = band[:, :extended]
+    edge = jnp.concatenate([band[:margin], band[tile - margin :]], axis=0)
+    fx[0] = jnp.concatenate(split(edge), axis=0)
+    ahead = jnp.transpose(toeplitz(gy, LANES, dy + MAXD, width))
+    fy[0], fy_low[0] = side_by_side(ahead[:LANES], ahead[LANES:])
+    by[0], by_low[0] = side_by_side(
+        toeplitz(gy, LANES, dy + MAXD - LANES, width)[:, :LANES],
+        toeplitz(gy, LANES, dy + MAXD, width)[:, :LANES],
+    )
+    bx[...] = jnp.concatenate(split(back), axis=0)
+    line = back[margin : margin + tile]
+    wide = bm.shape[2]
+    if wide > tile:
+        line = jnp.concatenate([line, jnp.zeros((tile, wide - tile), F32)], axis=1)
+    line = pltpu.roll(line, lax.rem(mid * slot - margin + wide, wide), 1)
+    lane = lax.broadcasted_iota(jnp.int32, line.shape, 1)
+    line = jnp.where((lane >= mid * slot) & (lane < mid * (slot + 1)), line, 0.0)
+    bm[0] = jnp.concatenate(split(line), axis=0)
+
+    b_hi, b_lo = split(band[margin : tile - margin, margin : margin + tile])
+    both = mm(jnp.concatenate([b_hi, b_lo], axis=0), hi[...])
+    spread(both[:mid] + both[mid:] + mm(b_hi, lo[...]), lhs)
+    live = alive(info, names, lengths, slot, half)
+    for j, image in enumerate(images(lhs, fy[0], fy_low[0], mid, cols // LANES)):
+        rim[slot, :, j * LANES : (j + 1) * LANES] = live / image
+
+
+def forward_kernel(radius, cut, names, info, lengths, est, across, inside, fx, fy, fy_low, *rest):
     outs, (e_hi, e_lo, lhs, halo, sems) = rest[:-5], rest[-5:]
     slot = pl.program_id(0)
     margin = radius + MAXD
     tile, cols = est.shape
-    extended = tile + 2 * margin
-    blocks = cols // LANES
+    edge = 2 * margin
 
     @pl.when(slot == 0)
     def _():
-        copies = fetch_sides(scal[3, 2], inside, across, halo, sems.at[0], sems.at[1])
+        copies = fetch_sides(info[names["odd"]], inside, across, halo, sems.at[0], sems.at[1])
         for piece, at in ((est, margin), (halo.at[0], 0), (halo.at[1], margin + tile)):
             if at == 0:
                 for copy in copies:
@@ -70,44 +152,20 @@
             e_hi[at : at + piece.shape[0], :] = top
             e_lo[at : at + piece.shape[0], :] = rest
 
-    dx, dy = scal[0, slot], scal[1, slot]
-    live = scal[2, slot].astype(F32)
-    width = taps.shape[2]
-    gx, gyr = taps[0, 0:1, :], taps[0, 3:4, :]
-    band = toeplitz(gx, tile, dx + MAXD, width)[:, :extended]
-    b_hi, b_lo = split(band)
-    both = mm(jnp.concatenate([b_hi, b_lo], axis=0), e_hi[...])
-    blurred = both[:tile] + both[tile:] + mm(b_hi, e_lo[...])
-    hi, lo = split(blurred)
-    for j in range(blocks):
-        at = slice(j * LANES, (j + 1) * LANES)
-        lhs[j * tile : (j + 1) * tile, :LANES] = hi[:, at]
-        lhs[j * tile : (j + 1) * tile, LANES:] = lo[:, at]
-    first, second = lateral_factors(gyr, -dy - MAXD - 2 * radius)
+    live = alive(info, names, lengths, slot, outs[0].shape[0] // 2)
+    both = mm(fx[0], e_hi[...])
+    spread(both[:edge] + both[edge:] + mm(fx[0, :edge], e_lo[...]), lhs)
+    for j, image in enumerate(images(lhs, fy[0], fy_low[0], edge, cols // LANES)):
+        for out, (c0, c1) in zip(outs, cut):
+            if c0 <= j < c1:
+                out[slot, :, (j - c0) * LANES : (j - c0 + 1) * LANES] = live / image
+
+
+def ratio_blurred(value, lhs, first, second):
+    rows, cols = value.shape
+    spread(value, lhs)
     part = mm(lhs[...], first) + mm(lhs[:, :LANES], second)
-    for j in range(blocks):
-        n = (j + 1) % blocks
-        image = part[j * tile : (j + 1) * tile, :LANES] + part[n * tile : (n + 1) * tile, LANES:]
-        value = live / image
-        for out, (c0, c1) in zip(outs[:-1], cut):
-            if c0 <= j < c1:
-                at = slice((j - c0) * LANES, (j - c0 + 1) * LANES)
-                out[slot, :margin, at] = value[:margin]
-                out[slot, margin:, at] = value[tile - margin :]
-        outs[-1][slot, :, j * LANES : (j + 1) * LANES] = value[margin : tile - margin]
-
-
-def ratio_blurred(slot, value, lhs, taps, dy, radius):
-    rows, cols = value.shape
-    hi, lo = split(value)
-    blocks = cols // LANES
-    for j in range(blocks):
-        at = slice(j * LANES, (j + 1) * LANES)
-        lhs[j * rows : (j + 1) * rows, :LANES] = hi[:, at]
-        lhs[j * rows : (j + 1) * rows, LANES:] = lo[:, at]
-    first, second = lateral_factors(taps[slot, 2:3, :], dy + MAXD - LANES)
-    part = mm(lhs[...], first) + mm(lhs[:, :LANES], second)
-    return [part[j * rows : (j + 1) * rows] for j in range(blocks)]
+    return [part[j * rows : (j + 1) * rows] for j in range(cols // LANES)]
 
 
 def runs_of(arrays, half, blocks):
@@ -176,13 +234,13 @@
         copy.wait()
 
 
-def edge_kernel(radius, tile, is_first, is_last, half, runs, scal, taps, rim, *rest):
+def edge_kernel(radius, tile, is_first, is_last, half, runs, names, scal, by, by_low, bx, rim, *rest):
     mine, rest = rest[:half], rest[half:]
     sib, rest = rest[: len(runs)], rest[len(runs) :]
     carries = []
     if not is_first:
         carries, rest = rest[: 1 + is_last], rest[1 + is_last :]
-    main, inside, across = rest[:3]
+    main, across, inside = rest[:3]
     rest = rest[3:]
     if not is_last:
         (next_left, *rest) = rest
@@ -192,12 +250,9 @@
     slots = 2 * half
     margin = radius + MAXD
     extended = tile + 2 * margin
-    width = taps.shape[2]
-    bands = []
     for slot in range(slots):
-        dx, dy = scal[0, slot], scal[1, slot]
         value = slot_values(slot, half, runs, mine, sib) * rim[slot]
-        parts = ratio_blurred(slot, value, lhs, taps, dy, radius)
+        parts = ratio_blurred(value, lhs, by[slot], by_low[slot])
         lefts = [x[:, :LANES] for x in parts]
         rights = [x[:, LANES:] for x in parts]
         if not is_first:
@@ -221,67 +276,57 @@
                 ref[base : base + margin, at] = piece[:margin]
                 ref[base + margin : base + tile - margin, at] = jnp.zeros((tile - 2 * margin, LANES), BF16)
                 ref[base + tile - margin : base + tile, at] = piece[margin:]
-        gxr = taps[slot, 1:2, :]
-        bands.append(toeplitz(gxr, extended, -dx - MAXD - 2 * radius, width)[:, :tile])
-    b_hi, b_lo = split(jnp.concatenate(bands, axis=1))
-    both = mm(jnp.concatenate([b_hi, b_lo], axis=0), s_hi[...])
-    total = both[:extended] + both[extended:] + mm(b_hi, s_lo[...])
-    odd = scal[3, 2] != 0
+    both = mm(bx[...], s_hi[...])
+    total = both[:extended] + both[extended:] + mm(bx[:extended], s_lo[...])
+    odd = scal[names["odd"]] != 0
     main[...] = total[margin : margin + tile]
     inside[...] = jnp.where(odd, total[:margin], total[margin + tile :])
     across[...] = jnp.where(odd, total[margin + tile :], total[:margin])
 
 
-def middle_kernel(radius, tile, half, runs, scal, taps, rim, *rest):
+def middle_kernel(radius, tile, half, runs, names, scal, by, by_low, bm, rim, *rest):
     mine, rest = rest[:half], rest[half:]
     sib, rest = rest[: len(runs)], rest[len(runs) :]
-    first, second, inside, across, total, lhs, s_hi, s_lo, part, edge, sems = rest
+    first, second, across, inside, total, lhs, s_hi, s_lo, part, edge, sems = rest
     width = first.shape[1]
     late = [
         fetch(first, part.at[:, :width], sems.at[0]),
         fetch(second, part.at[:, width:], sems.at[1]),
-        *fetch_sides(scal[3, 2], inside, across, edge, sems.at[2], sems.at[3]),
+        *fetch_sides(scal[names["odd"]], inside, across, edge, sems.at[2], sems.at[3]),
     ]
     slots = 2 * half
     margin = radius + MAXD
     mid = tile - 2 * margin
     cols = total.shape[1]
     blocks = cols // LANES
-    wide = 2 * LANES * max(1, slots * mid // LANES)
-    lane = lax.broadcasted_iota(jnp.int32, (tile, wide), 1)
-    band = jnp.zeros((tile, wide), F32)
+    band = bm[0]
+    for slot in range(1, slots):
+        band = band + bm[slot]
     for slot in range(slots):
-        dx, dy = scal[0, slot], scal[1, slot]
         value = slot_values(slot, half, runs, mine, sib) * rim[slot]
-        parts = ratio_blurred(slot, value, lhs, taps, dy, radius)
+        parts = ratio_blurred(value, lhs, by[slot], by_low[slot])
         base = slot * mid
         for j in range(1, blocks + 1):
             at = slice((j - 1) * LANES, j * LANES)
             hi, lo = split(parts[j - 1][:, :LANES] + parts[j % blocks][:, LANES:])
             s_hi[base : base + mid, at] = hi
             s_lo[base : base + mid, at] = lo
-        gxr = taps[slot, 1:2, :]
-        if wide > gxr.shape[1]:
-            gxr = jnp.concatenate([gxr, jnp.zeros((1, wide - gxr.shape[1]), F32)], axis=1)
-        line = toeplitz(gxr, tile, base - dx - MAXD - 2 * radius, wide)
-        band = jnp.where((lane >= base) & (lane < base + mid), line, band)
-    b_hi, b_lo = split(band[:, : slots * mid])
-    both = mm(jnp.concatenate([b_hi, b_lo], axis=0), s_hi[...])
+    both = mm(band, s_hi[...])
     for copy in late:
         copy.wait()
-    total[...] = both[:tile] + both[tile:] + mm(b_hi, s_lo[...]) + part[...]
+    total[...] = both[:tile] + both[tile:] + mm(band[:tile], s_lo[...]) + part[...]
     total[:margin, :width] += edge[0]
     total[tile - margin :, :width] += edge[1]
 
 
-def update_kernel(radius, tile, slots, scal, total, est, inside, across, out, edge, sems):
-    margin = radius + MAXD
-    copies = fetch_sides(scal[3, 2], inside, across, edge, sems.at[0], sems.at[1])
-    count = scal[2, 0]
+def update_kernel(radius, tile, slots, names, scal, lengths, total, est, across, inside, out, edge, sems):
+    margin = radius + MAXD
+    copies = fetch_sides(scal[names["odd"]], inside, across, edge, sems.at[0], sems.at[1])
+    count = alive(scal, names, lengths, 0, slots // 2)
     for slot in range(1, slots):
-        count += scal[2, slot]
+        count += alive(scal, names, lengths, slot, slots // 2)
     width, cols = inside.shape[1], est.shape[1]
-    weight = 1.0 / jnp.full((1, cols), count.astype(F32), F32)
+    weight = 1.0 / jnp.full((1, cols), count, F32)
     for copy in copies:
         copy.wait()
     at = slice(cols - width, cols)
@@ -376,25 +421,62 @@
     return pltpu.CompilerParams(vmem_limit_bytes=VMEM_LIMIT, dimension_semantics=("arbitrary",))
 
 
-def forward(radius, cut, scal, taps, est, inside, across):
-    slots = taps.shape[0]
+def prepare(radius, names, info, offsets, lengths, psf, est):
+    slots = psf.shape[0]
     tile, cols = est.shape
     margin = radius + MAXD
-    widths = [(c1 - c0) * LANES for c0, c1 in cut]
-    shapes = [(slots, 2 * margin, w) for w in widths] + [(slots, tile - 2 * margin, cols)]
+    mid, extended = tile - 2 * margin, tile + 2 * margin
+    bands = [
+        (slots, 4 * margin, extended),
+        (slots, 2 * LANES, 2 * LANES),
+        (slots, LANES, 2 * LANES),
+        (slots, 2 * LANES, 2 * LANES),
+        (slots, LANES, 2 * LANES),
+        (2 * extended, slots * tile),
+        (slots, 2 * tile, slots * mid),
+    ]
+    specs = [pl.BlockSpec((1,) + s[1:], lambda i, *_: (i, 0, 0)) for s in bands]
+    specs[5] = pl.BlockSpec((2 * extended, tile), lambda i, *_: (0, i))
+    return pl.pallas_call(
+        functools.partial(prepare_kernel, radius, names),
+        grid_spec=pltpu.PrefetchScalarGridSpec(
+            num_scalar_prefetch=3,
+            grid=(slots,),
+            in_specs=[whole_spec(psf.shape), in_vmem()],
+            out_specs=[in_vmem()] + specs,
+            scratch_shapes=[
+                pltpu.VMEM((tile, cols), BF16),
+                pltpu.VMEM((tile, cols), BF16),
+                pltpu.VMEM((mid * cols // LANES, 2 * LANES), BF16),
+                pltpu.VMEM((8, 2 * LANES), F32),
+            ],
+        ),
+        out_shape=[jax.ShapeDtypeStruct((slots, mid, cols), F32)]
+        + [jax.ShapeDtypeStruct(s, BF16) for s in bands],
+        compiler_params=params(),
+        cost_estimate=light(),
+        name="prepare",
+    )(info, offsets, lengths, psf, *from_vmem([est]))
+
+
+def forward(radius, cut, names, info, lengths, est, across, inside, fx, fy, fy_low):
+    slots = fx.shape[0]
+    tile, cols = est.shape
+    margin = radius + MAXD
+    shapes = [(slots, 2 * margin, (c1 - c0) * LANES) for c0, c1 in cut]
     extended = tile + 2 * margin
     return pl.pallas_call(
-        functools.partial(forward_kernel, radius, cut),
+        functools.partial(forward_kernel, radius, cut, names),
         grid_spec=pltpu.PrefetchScalarGridSpec(
-            num_scalar_prefetch=1,
+            num_scalar_prefetch=2,
             grid=(slots,),
-            in_specs=[pl.BlockSpec((1,) + taps.shape[1:], lambda i, *_: (i, 0, 0))]
-            + [in_vmem(), in_hbm(), in_hbm()],
+            in_specs=[in_vmem(), in_hbm(), in_hbm()]
+            + [pl.BlockSpec((1,) + x.shape[1:], lambda i, *_: (i, 0, 0)) for x in (fx, fy, fy_low)],
             out_specs=[in_vmem()] * len(shapes),
             scratch_shapes=[
                 pltpu.VMEM((extended, cols), BF16),
                 pltpu.VMEM((extended, cols), BF16),
-                pltpu.VMEM((tile * cols // LANES, 2 * LANES), BF16),
+                pltpu.VMEM((2 * margin * cols // LANES, 2 * LANES), BF16),
                 pltpu.VMEM((2, margin, cols), F32),
                 pltpu.SemaphoreType.DMA((2,)),
             ],
@@ -403,10 +485,10 @@
         compiler_params=params(),
         cost_estimate=light(),
         name="forward",
-    )(scal, taps, *from_vmem([est]), *from_hbm([inside, across]))
-
-
-def edges(radius, tile, is_first, is_last, runs, scal, taps, rim, mine, sib, carries):
+    )(info, lengths, *from_vmem([est]), *from_hbm([across, inside]), fx, fy, fy_low)
+
+
+def edges(radius, tile, is_first, is_last, runs, names, scal, bands, rim, mine, sib, carries):
     half = len(mine)
     slots = 2 * half
     margin = radius + MAXD
@@ -419,12 +501,11 @@
         if is_first:
             shapes.append(carried)
     return pl.pallas_call(
-        functools.partial(edge_kernel, radius, tile, is_first, is_last, half, runs),
+        functools.partial(edge_kernel, radius, tile, is_first, is_last, half, runs, names),
         grid_spec=pltpu.PrefetchScalarGridSpec(
             num_scalar_prefetch=1,
             grid=(1,),
-            in_specs=[whole_spec(taps.shape)]
-            + [in_vmem()] * (1 + half + len(sib) + len(carries)),
+            in_specs=[in_vmem()] * (4 + half + len(sib) + len(carries)),
             out_specs=[in_vmem()] * len(shapes),
             scratch_shapes=[
                 pltpu.VMEM((blocks * 2 * margin, 2 * LANES), BF16),
@@ -436,20 +517,19 @@
         compiler_params=params(),
         cost_estimate=light(),
         name="edges",
-    )(scal, taps, *from_vmem([rim, *mine, *sib, *carries]))
-
-
-def middle(radius, tile, runs, scal, taps, rim, mine, sib, mains, inside, across):
+    )(scal, *from_vmem([*bands, rim, *mine, *sib, *carries]))
+
+
+def middle(radius, tile, runs, names, scal, bands, rim, mine, sib, mains, inside, across):
     half = len(mine)
     slots, mid, cols = rim.shape
     margin = radius + MAXD
     return pl.pallas_call(
-        functools.partial(middle_kernel, radius, tile, half, runs),
+        functools.partial(middle_kernel, radius, tile, half, runs, names),
         grid_spec=pltpu.PrefetchScalarGridSpec(
             num_scalar_prefetch=1,
             grid=(1,),
-            in_specs=[whole_spec(taps.shape)]
-            + [in_vmem()] * (1 + half + len(runs))
+            in_specs=[in_vmem()] * (4 + half + len(runs))
             + [anywhere()] * 4,
             out_specs=in_vmem(),
             scratch_shapes=[
@@ -465,15 +545,15 @@
         compiler_params=params(),
         cost_estimate=light(),
         name="middle",
-    )(scal, taps, *from_vmem([rim, *mine, *sib]), *mains, inside, across)
-
-
-def update(radius, slots, scal, total, est, inside, across):
+    )(scal, *from_vmem([*bands, rim, *mine, *sib]), *mains, across, inside)
+
+
+def update(radius, slots, names, info, lengths, total, est, inside, across):
     tile = est.shape[0]
     return pl.pallas_call(
-        functools.partial(update_kernel, radius, tile, slots),
+        functools.partial(update_kernel, radius, tile, slots, names),
         grid_spec=pltpu.PrefetchScalarGridSpec(
-            num_scalar_prefetch=1,
+            num_scalar_prefetch=2,
             grid=(1,),
             in_specs=[in_vmem()] * 2 + [anywhere()] * 2,
             out_specs=whole_spec(est.shape),
@@ -486,7 +566,7 @@
         compiler_params=params(),
         cost_estimate=light(),
         name="update",
-    )(scal, *from_vmem([total, est]), inside, across)
+    )(info, lengths, *from_vmem([total, est]), across, inside)
 
 
 def per_device(estimate, views, psf, offsets, lengths):
@@ -512,7 +592,7 @@
         t = (k % half + s + (1 if k // half == b else 0)) % half
         return 2 * (b * half + t) + k // half
 
-    first = total_blocks // 2
+    first = total_blocks * 8 // 16
     cut = ((0, first), (first, total_blocks))
     away = [
         2 * ((member % half + s + (member // half == block).astype(jnp.int32)) % half)
@@ -521,7 +601,13 @@
     inner = (member // half == block).astype(jnp.int32)
     edge_at = (1 - odd) * (tile - margin)
     away = away + [1 - position % 2, inner, edge_at, tile - margin - edge_at]
-    away = jnp.stack(away).astype(jnp.int32)
+    pair, core = position // 2, position % 2
+    extra = {
+        "odd": odd, "core": core, "block": pair // half, "place": pair % half,
+        "row": position % planes,
+    }
+    names = {name: len(away) + i for i, name in enumerate(extra)}
+    away = jnp.stack(away + list(extra.values())).astype(jnp.int32)
     starts = (2,) * half + (1,)
     top, bottom = slice(0, margin), slice(tile - margin, tile)
     low, high = slice(0, margin), slice(margin, 2 * margin)
@@ -553,17 +639,15 @@
         away, starts, [stack], [], [edge_shape(*cut[0])] * half, edge_pieces(*cut[0]), "pack_first"
     )
     slab = pack(
-        away, starts, [est, psf], packed_a[:1], [(margin, cols)] * 2 + [psf.shape],
+        away, starts, [est], packed_a[:1], [(margin, cols)] * 2,
         [
             (0, 0, half + 2, (every,), (every,)),
             (0, 1, half + 3, (every,), (every,)),
-            (1, 2, None, (every,), (every,)),
         ],
         "pack_slab",
     )
+    across = lax.ppermute(slab[1], "joined", other)
     inside = lax.ppermute(slab[0], "joined", twin)
-    across = lax.ppermute(slab[1], "joined", other)
-    psf = slab[2]
     kept_a = view_send(packed_a)
     center = slice(margin, tile - margin)
     packed = pack(
@@ -573,53 +657,42 @@
         + [(0, half + s, s, (every, center), (every,)) for s in range(half)],
         "pack_second",
     )
-    packed_b, packed_c = packed[:half], packed[half:]
+    rim_middle, fx, fy, fy_low, by, by_low, bx, bm = prepare(
+        radius, names, away, offsets, lengths, psf, est
+    )
+    packed_b, packed_c = list(packed[:half]), packed[half:]
+    fellow = [(p, p ^ 1) for p in range(size)]
+    runs_a, runs_b = [
+        runs_of(arrays, half, c1 - c0) for arrays, (c0, c1) in zip((2, 1), cut)
+    ]
+    others, mine_a = part_pair(away, runs_a, kept_a, packed_a[-1], [rim_middle])
+    others = list(others)
+    packed_b[0], across, inside, others[0] = lax.optimization_barrier(
+        (packed_b[0], across, inside, others[0])
+    )
+    sib_a = [lax.ppermute(x, "view", fellow) for x in others]
     kept_b = view_send(packed_b)
     kept_c = view_send(packed_c)
-
-    pair, core = position // 2, position % 2
-    owned_block, place = pair // half, pair % half
-    row = position % planes
-
-    def slot_view(c, s):
-        return c * half + (place - s - (c == owned_block).astype(jnp.int32)) % half
-
-    order = [slot_view(core, s) for s in range(half)] + [slot_view(1 - core, s) for s in range(half)]
-    order = jnp.stack(order).astype(jnp.int32)
-    weights = psf / jnp.sum(psf, axis=2, keepdims=True)
-    taps = jnp.stack(
-        [weights[:, 0], weights[:, 0, ::-1], weights[:, 1], weights[:, 1, ::-1]], axis=1
-    )
-    taps = jnp.pad(taps, ((0, 0), (0, 0), (0, 2 * LANES - taps.shape[2])))
-    taps = taps[order]
-    shifts = offsets[order]
-    reach = lax.dynamic_index_in_dim(lengths, owned_block, 1, keepdims=False)
-    live = (row < reach).astype(jnp.int32)
-    side = jnp.stack([core, (core == owned_block).astype(jnp.int32), odd])
-    side = jnp.pad(side, (0, members - 3))
-    scal = jnp.stack(
-        [shifts[:, 0], shifts[:, 1], live[order], side]
-    ).astype(jnp.int32)
-
-    rims = forward(radius, cut, scal, taps, est, inside, across)
-    chunks, carries, main = [], [], None
-    for i, (kept, packed) in enumerate(((kept_a, packed_a), (kept_b, packed_b))):
-        runs = runs_of(half if i == 0 else 1, half, cut[i][1] - cut[i][0])
-        mine, sib = pair_send(runs, kept, packed[-1], rims[-1:] if i == 0 else [main])
-        is_first, is_last = i == 0, i == len(cut) - 1
-        result = edges(
-            radius, tile, is_first, is_last, runs, scal, taps, rims[i], mine, sib, carries
-        )
-        main, inside, across = result[:3]
-        carries = result[3:]
-        inside = lax.ppermute(inside, "joined", twin)
-        across = lax.ppermute(across, "joined", other)
-        chunks.append((main, inside, across))
+    rims = forward(radius, cut, names, away, lengths, est, across, inside, fx, fy, fy_low)
+    main, across, inside, *carries = edges(
+        radius, tile, True, False, runs_a, names, away, (by, by_low, bx), rims[0], mine_a, sib_a, []
+    )
+    across = lax.ppermute(across, "joined", other)
+    inside = lax.ppermute(inside, "joined", twin)
+    chunks = [(main, inside, across)]
+    mine, sib = pair_send(runs_b, kept_b, packed_b[-1], [main])
+    main, across, inside = edges(
+        radius, tile, False, True, runs_b, names, away, (by, by_low, bx), rims[1], mine, sib, carries
+    )
+    across = lax.ppermute(across, "joined", other)
+    inside = lax.ppermute(inside, "joined", twin)
+    chunks.append((main, inside, across))
     runs = runs_of(3, half, total_blocks)
-    mine, sib = pair_send(runs, kept_c, packed_c[-1], [main, *chunks[0][1:]])
+    mine, sib = pair_send(runs, kept_c, packed_c[-1], [main, chunks[0][2], chunks[0][1]])
     mains = [chunk[0] for chunk in chunks]
-    total = middle(radius, tile, runs, scal, taps, rims[-1], mine, sib, mains, *chunks[0][1:])
-    out = update(radius, members, scal, total, est, *chunks[1][1:])
+    bands = (by, by_low, bm)
+    total = middle(radius, tile, runs, names, away, bands, rim_middle, mine, sib, mains, *chunks[0][1:])
+    out = update(radius, members, names, away, lengths, total, est, *chunks[1][1:])
     return out[None]
 
 

time: 76 us -> 72.9 us (0.959)
  starting transfers between devices: 28 us -> 19.9 us
  waiting for transfers between devices: 9.75 us -> 15.8 us
  Pallas kernels: 31.7 us -> 33 us
  local copies, waits for them, and re-layouts: 4.75 us -> 3.67 us
    ppermute x2, starting transfers between devices: 11.9 us -> 4.64 us  [per_device(): across = lax.ppermute(across, 'joined', other)]
    ppermute x1, waiting for transfers between devices: 6.62 us -> 0.01 us  [per_device(): across = lax.ppermute(slab[1], 'joined', other)]
    ppermute x6, waiting for transfers between devices: 0.02 us -> 6.33 us  [view_send(): sent.append(lax.ppermute(x, 'view', [(p, q) for p, q in pairs if p != q]))]
    ppermute x1, waiting for transfers between devices: 0.01 us -> 5.99 us  [per_device(): inside = lax.ppermute(slab[0], 'joined', twin)]
    pallas_call x3 -> x4, Pallas kernels: 12.3 us -> 15.1 us  [the longest x1 5.76 us: forward(): pl.pallas_call(functools.partial(forward_kernel, radius, cut, names), gri...]
    ppermute x2, waiting for transfers between devices: 0.01 us -> 2.34 us  [per_device(): inside = lax.ppermute(inside, 'joined', twin)]
    ppermute x6 -> x4, waiting for transfers between devices: 3.1 us -> 1.15 us  [pair_send(): lax.ppermute(x, 'view', [(p, p ^ 1) for p in range(size)])]
    gather x4 -> x0, local copies, waits for them, and re-layouts: 1.77 us -> none  [the longest x1 0.64 us: per_device(): live[order]]
  transfers between devices with their start and end apart: 18 -> 18, of which waited for: 4 -> 5; matrix products, arithmetic and copies ran while one was open for 3% -> 0% of each run, Pallas kernels for 34% -> 37%
where the time goes in v4:
time: 72.9 us; the launch traced here: 72.6 us
  Pallas kernels  33 us (45%)
  starting transfers between devices  19.9 us (27%)
  waiting for transfers between devices  15.8 us (22%)
  local copies, waits for them, and re-layouts  3.67 us (5%)
    ppermute x6, starting transfers between devices, view_send(): sent.append(lax.ppermute(x, 'view', [(p, q) for p, q in pairs if p != q]))  7.47 us
    pallas_call x3, Pallas kernels, pack(): pl.pallas_call(functools.partial(pack_kernel, starts, pieces, len(ins) +...  6.78 us
    ppermute x6, waiting for transfers between devices, view_send(): sent.append(lax.ppermute(x, 'view', [(p, q) for p, q in pairs if p != q]))  6.33 us
    ppermute x1, waiting for transfers between devices, per_device(): inside = lax.ppermute(slab[0], 'joined', twin)  5.99 us
    pallas_call x1, Pallas kernels, forward(): pl.pallas_call(functools.partial(forward_kernel, radius, cut, names), gri...  5.76 us
    pallas_call x3, Pallas kernels, part_pair(): pl.pallas_call(functools.partial(pair_kernel, half, runs), grid_spec=pltp...  5.74 us
    pallas_call x2, Pallas kernels, edges(): pl.pallas_call(functools.partial(edge_kernel, radius, tile, is_first, is_...  5.29 us
    ppermute x2, starting transfers between devices, per_device(): across = lax.ppermute(across, 'joined', other)  4.64 us
  transfers between devices with their start and end apart: 18, of which 5 were waited for; matrix products, arithmetic and copies ran while one was open for 0% of the time, Pallas kernels for 37%

profile of v4, /device:TPU:0, one launch (start us, length us, event | category | flops | bytes accessed | tf_op | source)
XLA Modules:
  0.0 72.6 jit_solution(9999490299023101360)
XLA Ops:
  0.0 0.1 stack.47.info.refs_0_.scal
  0.1 1.9 %pack_first.1 = (f32[2,96,1024]{2,1,0:T(8,128)S(1)}, f32[2,96,1024]{2,1,0:T(8,128)S(1)}) custom-call(s32[11]{0:T(128)S(1)} %stack.47.info.refs_0_.scal, f32[4,128,2048]{2,1,0:T(8,128)} %bitcast.18), custom_call_target="tpu_custom_call" | custom-call | bytes 1024 | tf_op jit(solution)/shard_map/pack_first/pallas_call | solution.py:378
  2.0 0.0 copy-start.2
  2.0 3.0 %collective-permute-start.4 = (f32[2,96,1024]{2,1,0:T(8,128)S(1)}, f32[2,96,1024]{2,1,0:T(8,128)}, u32[]{:S(2)}, u32[]{:S(2)}) collective-permute-start(f32[2,96,1024]{2,1,0:T(8,128)S(1)} %get-tuple-element.51.refs_2_), channel_id=1, source_target_pairs={{0,2},{1,4},{2,0},{3,6},{4,1},{5,7},{6,3},{7,5},{8,10},{9,12},{10,... | collective-permute-start | bytes 2359304 | tf_op jit(solution)/shard_map/ppermute | solution.py:628
  5.0 1.6 %collective-permute-start.5 = (f32[2,96,1024]{2,1,0:T(8,128)S(1)}, f32[2,96,1024]{2,1,0:T(8,128)}, u32[]{:S(2)}, u32[]{:S(2)}) collective-permute-start(f32[2,96,1024]{2,1,0:T(8,128)S(1)} %get-tuple-element.58.refs_2_), channel_id=1, source_target_pairs={{1,6},{3,4},{4,3},{6,1},{9,14},{11,12},{12,11},{14,9},{17,22},{19,... | collective-permute-start | bytes 2359304 | tf_op jit(solution)/shard_map/ppermute | solution.py:628
  6.6 2.6 %pack_slab.1 = (f32[48,2048]{1,0:T(8,128)}, f32[48,2048]{1,0:T(8,128)}) custom-call(s32[11]{0:T(128)S(1)} %stack.47.info.refs_0_.scal, f32[128,2048]{1,0:T(8,128)} %bitcast.14, f32[2,96,1024]{2,1,0:T(8,128)S(1)} %get-tuple-element.51.refs_2_), custom_call_target="tpu_custom_call" | custom-call | bytes 1024 | tf_op jit(solution)/shard_map/pack_slab/pallas_call | solution.py:378
  9.2 3.7 %collective-permute-start.2 = (f32[48,2048]{1,0:T(8,128)}, f32[48,2048]{1,0:T(8,128)}, u32[]{:S(2)}, u32[]{:S(2)}) collective-permute-start(f32[48,2048]{1,0:T(8,128)} %get-tuple-element.57), channel_id=1, source_target_pairs={{0,24},{8,16},{16,8},{24,0},{1,25},{9,17},{17,9},{25,1},{2,26},{10... | collective-permute-start | bytes 1179656 | tf_op jit(solution)/shard_map/ppermute | solution.py:649
  12.8 0.1 collective-permute-start.3
  12.9 2.3 %pack_second.1 = (f32[2,96,1024]{2,1,0:T(8,128)S(1)}, f32[2,96,1024]{2,1,0:T(8,128)S(1)}, f32[2,32,2048]{2,1,0:T(8,128)S(1)}, f32[2,32,2048]{2,1,0:T(8,128)S(1)}) custom-call(s32[11]{0:T(128)S(1)} %stack.47.info.refs_0_.scal, f32[4,128,2048]{2,1,0:T(8,128)} %bitcast.19, f32[48,2048]{1,0:T(8,128)} %get-tuple-element.52.refs_2_), custom_call_target="tpu_custom_call" | custom-call | bytes 1024 | tf_op jit(solution)/shard_map/pack_second/pallas_call | solution.py:378
  15.2 0.0 copy-done.2
  15.2 0.0 copy-start.3
  15.2 0.8 %copy-done.3 = f32[2,32,2048]{2,1,0:T(8,128)} copy-done((f32[2,32,2048]{2,1,0:T(8,128)}, f32[2,32,2048]{2,1,0:T(8,128)S(1)}, u32[]{:S(2)}) %copy-start.3) | copy-done | bytes 524312
  16.0 0.9 %copy-done.6 = f32[2,96,1024]{2,1,0:T(8,128)} copy-done((f32[2,96,1024]{2,1,0:T(8,128)}, f32[2,96,1024]{2,1,0:T(8,128)S(1)}, u32[]{:S(2)}) %copy-start.6) | copy-done | bytes 786456
  16.9 0.8 %copy-done.8 = f32[2,32,2048]{2,1,0:T(8,128)} copy-done((f32[2,32,2048]{2,1,0:T(8,128)}, f32[2,32,2048]{2,1,0:T(8,128)S(1)}, u32[]{:S(2)}) %copy-start.8) | copy-done | bytes 524312
  17.7 1.5 %collective-permute-start.7 = (f32[2,96,1024]{2,1,0:T(8,128)S(1)}, f32[2,96,1024]{2,1,0:T(8,128)}, u32[]{:S(2)}, u32[]{:S(2)}) collective-permute-start(f32[2,96,1024]{2,1,0:T(8,128)S(1)} %get-tuple-element.67.refs_2_), channel_id=1, source_target_pairs={{1,6},{3,4},{4,3},{6,1},{9,14},{11,12},{12,11},{14,9},{17,22},{19,... | collective-permute-start | bytes 2359304 | tf_op jit(solution)/shard_map/ppermute | solution.py:628
  19.3 0.0 copy-done.13
  19.3 0.1 copy.9.lengths
  19.4 0.0 copy-done.14
  19.4 0.1 copy.6.offsets
  19.5 0.0 copy-done
  19.5 4.4 %prepare.1 = (f32[4,32,2048]{2,1,0:T(8,128)S(1)}, bf16[4,192,224]{2,1,0:T(8,128)(2,1)S(1)}, bf16[4,256,256]{2,1,0:T(8,128)(2,1)S(1)}, bf16[4,128,256]{2,1,0:T(8,...) custom-call(s32[11]{0:T(128)S(1)} %stack.47.info.refs_0_.scal, ...), custom_call_target="tpu_custom_call" | custom-call | bytes 1024 | tf_op jit(solution)/shard_map/prepare/pallas_call | solution.py:440
  23.9 0.0 collective-permute-done.4.refs_0_
  23.9 0.0 collective-permute-done.5.refs_1_
  23.9 0.0 copy-start.7
  23.9 1.9 %pair.3 = (f32[96,1024]{1,0:T(8,128)S(1)}, f32[96,1024]{1,0:T(8,128)S(1)}, f32[96,1024]{1,0:T(8,128)S(1)}, f32[96,1024]{1,0:T(8,128)S(1)}) custom-call(s32[11]{0:T(128)S(1)} %stack.47.info.refs_0_.scal, f32[2,96,1024]{2,1,0:T(8,128)} %collective-permute-done.4.refs_0_, f32[2,96,1024]{2,1,0:T(8,128)} %collective-permute-done.5.refs_1_, ...), custom_call_target="tpu_custom_call" | custom-call | bytes 1024 | tf_op jit(solution)/shard_map/pair/pallas_call | solution.py:399
  25.9 0.0 collective-permute-done.2.across
  25.9 6.0 %collective-permute-done.3.inside = f32[48,2048]{1,0:T(8,128)} collective-permute-done((f32[48,2048]{1,0:T(8,128)}, f32[48,2048]{1,0:T(8,128)}, u32[]{:S(2)}, u32[]{:S(2)}) %collective-permute-start.3) | collective-permute-done | bytes 393248 | tf_op jit(solution)/shard_map/ppermute | solution.py:650
  31.9 0.0 copy-done.7
  31.9 0.3 collective-permute-start.6
  32.2 0.0 collective-permute-start.8
  32.2 0.5 collective-permute-start.9
  32.7 5.8 %forward.1 = (f32[4,96,1024]{2,1,0:T(8,128)S(1)}, f32[4,96,1024]{2,1,0:T(8,128)S(1)}) custom-call(s32[11]{0:T(128)S(1)} %stack.47.info.refs_0_.scal, s32[4,2]{1,0:T(4,128)S(1)} %copy.9.lengths, f32[128,2048]{1,0:T(8,128)S(1)} %bitcast.16, f32[48,2048]{1,0:T(8,128)} %collective-permute-done.2.across, f32[48,2048]{1,0:T(8,128)} %collective-permute-done.3.inside, ...), custom_call_target="tpu_custom_call" | custom-call | bytes 1024 | tf_op jit(solution)/shard_map/forward/pallas_call | solution.py:468
  38.4 0.0 collective-permute-done.8.rest_2_
  38.5 0.0 collective-permute-done.9.rest_3_
  38.5 2.5 %edges.2 = (f32[128,896]{1,0:T(8,128)S(1)}, f32[48,896]{1,0:T(8,128)S(1)}, f32[48,896]{1,0:T(8,128)S(1)}, f32[4,96,128]{2,1,0:T(8,128)S(1)}, f32[4,96,128]{2,1,0:T(8,128)S(1)}) custom-call(s32[11]{0:T(128)S(1)} %stack.47.info.refs_0_.scal, bf16[4,256,256]{2,1,0:T(8,128)(2,1)S(1)} %get-tuple-element.47.by, bf16[4,128,256]{2,1,0:T(8,128)(2,1)S(1)} %get-tuple-element.48.by_low, ...), custom_call_target="tpu_custom_call" | custom-call | bytes 1024 | tf_op jit(solution)/shard_map/edges/pallas_call | solution.py:503
  41.0 0.0 collective-permute-done.7.refs_1_
  41.0 2.8 %collective-permute-done.6.refs_0_ = f32[2,96,1024]{2,1,0:T(8,128)S(1)} collective-permute-done((f32[2,96,1024]{2,1,0:T(8,128)S(1)}, f32[2,96,1024]{2,1,0:T(8,128)S(1)}, u32[]{:S(2)}, u32[]{:S(2)}) %collective-permute-start.6) | collective-permute-done | bytes 786464 | tf_op jit(solution)/shard_map/ppermute | solution.py:628
  43.8 0.9 %copy-done.10 = f32[2,96,1024]{2,1,0:T(8,128)} copy-done((f32[2,96,1024]{2,1,0:T(8,128)}, f32[2,96,1024]{2,1,0:T(8,128)S(1)}, u32[]{:S(2)}) %copy-start.10) | copy-done | bytes 786456
  44.7 1.9 %pair.4 = (f32[96,2048]{1,0:T(8,128)S(1)}, f32[96,1024]{1,0:T(8,128)S(1)}, f32[96,1024]{1,0:T(8,128)S(1)}) custom-call(s32[11]{0:T(128)S(1)} %stack.47.info.refs_0_.scal, f32[2,96,1024]{2,1,0:T(8,128)} %copy-done.10, f32[2,96,1024]{2,1,0:T(8,128)} %collective-permute-done.7.refs_1_, f32[2,96,1024]{2,1,0:T(8,128)} %copy-done.1, ...), custom_call_target="tpu_custom_call" | custom-call | bytes 1024 | tf_op jit(solution)/shard_map/pair/pallas_call | solution.py:399
  46.7 0.1 collective-permute-start.10
  46.7 0.4 collective-permute-start
  47.1 0.7 collective-permute-start.1
  47.8 2.7 %collective-permute-start.11 = (f32[48,896]{1,0:T(8,128)S(1)}, f32[48,896]{1,0:T(8,128)S(1)}, u32[]{:S(2)}, u32[]{:S(2)}) collective-permute-start(f32[48,896]{1,0:T(8,128)S(1)} %get-tuple-element.80), channel_id=1, source_target_pairs={{0,24},{8,16},{16,8},{24,0},{1,25},{9,17},{17,9},{25,1},{2,26},{10... | collective-permute-start | bytes 516104 | tf_op jit(solution)/shard_map/ppermute | solution.py:680
  50.5 0.0 collective-permute-start.12
  50.5 0.0 collective-permute-done.10.rest_2_
  50.5 2.7 %edges.3 = (f32[128,1152]{1,0:T(8,128)S(1)}, f32[48,1152]{1,0:T(8,128)S(1)}, f32[48,1152]{1,0:T(8,128)S(1)}) custom-call(s32[11]{0:T(128)S(1)} %stack.47.info.refs_0_.scal, bf16[4,256,256]{2,1,0:T(8,128)(2,1)S(1)} %get-tuple-element.47.by, bf16[4,128,256]{2,1,0:T(8,128)(2,1)S(1)} %get-tuple-element.48.by_low, bf16[448,512]{1,0:T(8,128)(2,1)S(1)} %get-tuple-element.55.bx, ...), custom_call_target="tpu_custom_call" | custom-call | bytes 1024 | tf_op jit(solution)/shard_map/edges/pallas_call | solution.py:503
  53.2 2.0 %collective-permute-start.16 = (f32[48,1152]{1,0:T(8,128)S(1)}, f32[48,1152]{1,0:T(8,128)S(1)}, u32[]{:S(2)}, u32[]{:S(2)}) collective-permute-start(f32[48,1152]{1,0:T(8,128)S(1)} %get-tuple-element.87), channel_id=1, source_target_pairs={{0,24},{8,16},{16,8},{24,0},{1,25},{9,17},{17,9},{25,1},{2,26},{10... | collective-permute-start | bytes 663560 | tf_op jit(solution)/shard_map/ppermute | solution.py:687
  55.2 3.5 %collective-permute-done.refs_0_ = f32[2,32,2048]{2,1,0:T(8,128)S(1)} collective-permute-done((f32[2,32,2048]{2,1,0:T(8,128)S(1)}, f32[2,32,2048]{2,1,0:T(8,128)S(1)}, u32[]{:S(2)}, u32[]{:S(2)}) %collective-permute-start) | collective-permute-done | bytes 524320 | tf_op jit(solution)/shard_map/ppermute | solution.py:628
  58.7 1.4 %collective-permute-start.17 = (f32[48,1152]{1,0:T(8,128)S(1)}, f32[48,1152]{1,0:T(8,128)S(1)}, u32[]{:S(2)}, u32[]{:S(2)}) collective-permute-start(f32[48,1152]{1,0:T(8,128)S(1)} %get-tuple-element.88), channel_id=1, source_target_pairs={{0,8},{8,0},{16,24},{24,16},{1,9},{9,1},{17,25},{25,17},{2,10},{10... | collective-permute-start | bytes 663560 | tf_op jit(solution)/shard_map/ppermute | solution.py:688
  60.1 0.0 collective-permute-done.1.refs_1_
  60.1 0.0 collective-permute-done.11.refs_4_.rest_7_
  60.1 2.3 %collective-permute-done.12.refs_5_.rest_8_ = f32[48,896]{1,0:T(8,128)S(1)} collective-permute-done((f32[48,896]{1,0:T(8,128)S(1)}, f32[48,896]{1,0:T(8,128)S(1)}, u32[]{:S(2)}, u32[]{:S(2)}) %collective-permute-start.12) | collective-permute-done | bytes 172064 | tf_op jit(solution)/shard_map/ppermute | solution.py:681
  62.4 0.0 copy-done.12
  62.4 1.9 %pair.5 = (f32[32,1408]{1,0:T(8,128)S(1)}, f32[32,1280]{1,0:T(8,128)S(1)}, f32[32,1408]{1,0:T(8,128)S(1)}, f32[32,2048]{1,0:T(8,128)S(1)}, f32[32,2048]{1,0:T(8,128)S(1)}) custom-call(s32[11]{0:T(128)S(1)} %stack.47.info.refs_0_.scal, f32[2,32,2048]{2,1,0:T(8,128)} %copy-done.11, f32[2,32,2048]{2,1,0:T(8,128)} %copy-done.12, f32[2,32,2048]{2,1,0:T(8,128)} %copy-done.3, ...), custom_call_target="tpu_custom_call" | custom-call | bytes 1024 | tf_op jit(solution)/shard_map/pair/pallas_call | solution.py:399
  64.3 1.6 %collective-permute-start.13 = (f32[32,1408]{1,0:T(8,128)S(1)}, f32[32,1408]{1,0:T(8,128)S(1)}, u32[]{:S(2)}, u32[]{:S(2)}) collective-permute-start(f32[32,1408]{1,0:T(8,128)S(1)} %get-tuple-element.84), channel_id=1, source_target_pairs={{0,1},{1,0},{2,3},{3,2},{4,5},{5,4},{6,7},{7,6},{8,9},{9,8},{10,11... | collective-permute-start | bytes 540680 | tf_op jit(solution)/shard_map/ppermute | solution.py:633
  65.9 0.1 collective-permute-start.15
  66.0 0.4 collective-permute-start.14
  66.4 1.1 %collective-permute-done.14.rest_3_ = f32[32,1280]{1,0:T(8,128)S(1)} collective-permute-done((f32[32,1280]{1,0:T(8,128)S(1)}, f32[32,1280]{1,0:T(8,128)S(1)}, u32[]{:S(2)}, u32[]{:S(2)}) %collective-permute-start.14) | collective-permute-done | bytes 163872 | tf_op jit(solution)/shard_map/ppermute | solution.py:633
  67.6 0.0 collective-permute-done.13.rest_2_
  67.6 0.0 collective-permute-done.15.rest_4_
  67.6 2.4 %middle.1.total = f32[128,2048]{1,0:T(8,128)S(1)} custom-call(s32[11]{0:T(128)S(1)} %stack.47.info.refs_0_.scal, bf16[4,256,256]{2,1,0:T(8,128)(2,1)S(1)} %get-tuple-element.47.by, bf16[4,128,256]{2,1,0:T(8,128)(2,1)S(1)} %get-tuple-element.48.by_low, bf16[4,256,128]{2,1,0:T(8,128)(2,1)S(1)} %get-tuple-element.49.bm, ...), custom_call_target="tpu_custom_call" | custom-call | bytes 1024 | tf_op jit(solution)/shard_map/middle/pallas_call | solution.py:527
  70.0 0.0 collective-permute-done.16.across
  70.0 0.0 collective-permute-done.17.inside
  70.0 2.5 %update.1 = f32[128,2048]{1,0:T(8,128)} custom-call(s32[11]{0:T(128)S(1)} %stack.47.info.refs_0_.scal, s32[4,2]{1,0:T(4,128)S(1)} %copy.9.lengths, f32[128,2048]{1,0:T(8,128)S(1)} %middle.1.total, f32[128,2048]{1,0:T(8,128)S(1)} %bitcast.17, f32[48,1152]{1,0:T(8,128)S(1)} %collective-permute-done.16.across, f32[48,1152]{1,0:T(8,128)S(1)} %collective-permute-done.17.inside), custom_call_target="tpu_custom_call" | custom-call | bytes 1024 | tf_op jit(solution)/shard_map/update/pallas_call | solution.py:553
  (17 shorter events, 0.0 us)
Async XLA Ops:
  2.0 13.2 %copy-start.2 = (f32[2,96,1024]{2,1,0:T(8,128)}, f32[2,96,1024]{2,1,0:T(8,128)S(1)}, u32[]{:S(2)}) copy-start(f32[2,96,1024]{2,1,0:T(8,128)S(1)} %get-tuple-element.58.refs_2_) | copy-start | bytes 2359300
  2.0 21.8 %collective-permute-start.4 = (f32[2,96,1024]{2,1,0:T(8,128)S(1)}, f32[2,96,1024]{2,1,0:T(8,128)}, u32[]{:S(2)}, u32[]{:S(2)}) collective-permute-start(f32[2,96,1024]{2,1,0:T(8,128)S(1)} %get-tuple-element.51.refs_2_), channel_id=1, source_target_pairs={{0,2},{1,4},{2,0},{3,6},{4,1},{5,7},{6,3},{7,5},{8,10},{9,12},{10,... | collective-permute-start | bytes 2359304 | tf_op jit(solution)/shard_map/ppermute | solution.py:628
  5.0 18.8 %collective-permute-start.5 = (f32[2,96,1024]{2,1,0:T(8,128)S(1)}, f32[2,96,1024]{2,1,0:T(8,128)}, u32[]{:S(2)}, u32[]{:S(2)}) collective-permute-start(f32[2,96,1024]{2,1,0:T(8,128)S(1)} %get-tuple-element.58.refs_2_), channel_id=1, source_target_pairs={{1,6},{3,4},{4,3},{6,1},{9,14},{11,12},{12,11},{14,9},{17,22},{19,... | collective-permute-start | bytes 2359304 | tf_op jit(solution)/shard_map/ppermute | solution.py:628
  9.2 16.7 %collective-permute-start.2 = (f32[48,2048]{1,0:T(8,128)}, f32[48,2048]{1,0:T(8,128)}, u32[]{:S(2)}, u32[]{:S(2)}) collective-permute-start(f32[48,2048]{1,0:T(8,128)} %get-tuple-element.57), channel_id=1, source_target_pairs={{0,24},{8,16},{16,8},{24,0},{1,25},{9,17},{17,9},{25,1},{2,26},{10... | collective-permute-start | bytes 1179656 | tf_op jit(solution)/shard_map/ppermute | solution.py:649
  12.8 6.4 %copy-start.13 = (s32[4,2]{0,1:T(2,128)S(1)}, s32[4,2]{0,1:T(2,128)}, u32[]{:S(2)}) copy-start(s32[4,2]{0,1:T(2,128)} %param.9) | copy-start | bytes 100
  12.8 6.5 %copy-start.14 = (s32[4,2]{0,1:T(2,128)S(1)}, s32[4,2]{0,1:T(2,128)}, u32[]{:S(2)}) copy-start(s32[4,2]{0,1:T(2,128)} %param.8) | copy-start | bytes 100
  12.8 6.6 %copy-start = (f32[1,128,2048]{2,1,0:T(8,128)S(1)}, f32[1,128,2048]{2,1,0:T(8,128)}, u32[]{:S(2)}) copy-start(f32[1,128,2048]{2,1,0:T(8,128)} %param.5) | copy-start | bytes 3145732
  12.8 6.6 %copy-start.5 = (f32[4,2,65]{2,1,0:T(2,128)S(1)}, f32[4,2,65]{2,1,0:T(2,128)}, u32[]{:S(2)}) copy-start(f32[4,2,65]{2,1,0:T(2,128)} %psf.1) | copy-start | bytes 6244
  12.8 19.0 %collective-permute-start.3 = (f32[48,2048]{1,0:T(8,128)}, f32[48,2048]{1,0:T(8,128)}, u32[]{:S(2)}, u32[]{:S(2)}) collective-permute-start(f32[48,2048]{1,0:T(8,128)} %get-tuple-element.52.refs_2_), channel_id=1, source_target_pairs={{0,8},{8,0},{16,24},{24,16},{1,9},{9,1},{17,25},{25,17},{2,10},{10... | collective-permute-start | bytes 1179656 | tf_op jit(solution)/shard_map/ppermute | solution.py:650
  15.2 0.8 %copy-start.3 = (f32[2,32,2048]{2,1,0:T(8,128)}, f32[2,32,2048]{2,1,0:T(8,128)S(1)}, u32[]{:S(2)}) copy-start(f32[2,32,2048]{2,1,0:T(8,128)S(1)} %get-tuple-element.54.refs_2_) | copy-start | bytes 1572868
  16.0 0.9 %copy-start.6 = (f32[2,96,1024]{2,1,0:T(8,128)}, f32[2,96,1024]{2,1,0:T(8,128)S(1)}, u32[]{:S(2)}) copy-start(f32[2,96,1024]{2,1,0:T(8,128)S(1)} %get-tuple-element.66) | copy-start | bytes 2359300
  16.9 0.8 %copy-start.8 = (f32[2,32,2048]{2,1,0:T(8,128)}, f32[2,32,2048]{2,1,0:T(8,128)S(1)}, u32[]{:S(2)}) copy-start(f32[2,32,2048]{2,1,0:T(8,128)S(1)} %get-tuple-element.53) | copy-start | bytes 1572868
  17.7 8.1 %copy-start.1 = (f32[2,96,1024]{2,1,0:T(8,128)}, f32[2,96,1024]{2,1,0:T(8,128)S(1)}, u32[]{:S(2)}) copy-start(f32[2,96,1024]{2,1,0:T(8,128)S(1)} %get-tuple-element.67.refs_2_) | copy-start | bytes 2359300
  17.7 23.3 %collective-permute-start.7 = (f32[2,96,1024]{2,1,0:T(8,128)S(1)}, f32[2,96,1024]{2,1,0:T(8,128)}, u32[]{:S(2)}, u32[]{:S(2)}) collective-permute-start(f32[2,96,1024]{2,1,0:T(8,128)S(1)} %get-tuple-element.67.refs_2_), channel_id=1, source_target_pairs={{1,6},{3,4},{4,3},{6,1},{9,14},{11,12},{12,11},{14,9},{17,22},{19,... | collective-permute-start | bytes 2359304 | tf_op jit(solution)/shard_map/ppermute | solution.py:628
  23.9 8.0 %copy-start.7 = (f32[2,96,1024]{2,1,0:T(8,128)S(1)}, f32[2,96,1024]{2,1,0:T(8,128)}, u32[]{:S(2)}) copy-start(f32[2,96,1024]{2,1,0:T(8,128)} %copy-done.6) | copy-start | bytes 2359300
  31.9 12.0 %collective-permute-start.6 = (f32[2,96,1024]{2,1,0:T(8,128)S(1)}, f32[2,96,1024]{2,1,0:T(8,128)S(1)}, u32[]{:S(2)}, u32[]{:S(2)}) collective-permute-start(f32[2,96,1024]{2,1,0:T(8,128)S(1)} %copy-done.7), channel_id=1, source_target_pairs={{0,2},{1,4},{2,0},{3,6},{4,1},{5,7},{6,3},{7,5},{8,10},{9,12},{10,... | collective-permute-start | bytes 2359304 | tf_op jit(solution)/shard_map/ppermute | solution.py:628
  32.2 6.3 %collective-permute-start.8 = (f32[96,1024]{1,0:T(8,128)S(1)}, f32[96,1024]{1,0:T(8,128)S(1)}, u32[]{:S(2)}, u32[]{:S(2)}) collective-permute-start(f32[96,1024]{1,0:T(8,128)S(1)} %get-tuple-element.71), channel_id=1, source_target_pairs={{0,1},{1,0},{2,3},{3,2},{4,5},{5,4},{6,7},{7,6},{8,9},{9,8},{10,11... | collective-permute-start | bytes 1179656 | tf_op jit(solution)/shard_map/ppermute | solution.py:673
  32.2 6.3 %collective-permute-start.9 = (f32[96,1024]{1,0:T(8,128)S(1)}, f32[96,1024]{1,0:T(8,128)S(1)}, u32[]{:S(2)}, u32[]{:S(2)}) collective-permute-start(f32[96,1024]{1,0:T(8,128)S(1)} %get-tuple-element.72), channel_id=1, source_target_pairs={{0,1},{1,0},{2,3},{3,2},{4,5},{5,4},{6,7},{7,6},{8,9},{9,8},{10,11... | collective-permute-start | bytes 1179656 | tf_op jit(solution)/shard_map/ppermute | solution.py:673
  41.0 5.7 %copy-start.9 = (f32[2,32,2048]{2,1,0:T(8,128)S(1)}, f32[2,32,2048]{2,1,0:T(8,128)}, u32[]{:S(2)}) copy-start(f32[2,32,2048]{2,1,0:T(8,128)} %copy-done.8) | copy-start | bytes 1572868
  41.0 6.1 %copy-start.4 = (f32[2,32,2048]{2,1,0:T(8,128)S(1)}, f32[2,32,2048]{2,1,0:T(8,128)}, u32[]{:S(2)}) copy-start(f32[2,32,2048]{2,1,0:T(8,128)} %copy-done.3) | copy-start | bytes 1572868
  43.8 0.9 %copy-start.10 = (f32[2,96,1024]{2,1,0:T(8,128)}, f32[2,96,1024]{2,1,0:T(8,128)S(1)}, u32[]{:S(2)}) copy-start(f32[2,96,1024]{2,1,0:T(8,128)S(1)} %collective-permute-done.6.refs_0_) | copy-start | bytes 2359300
  46.7 3.8 %collective-permute-start.10 = (f32[96,2048]{1,0:T(8,128)S(1)}, f32[96,2048]{1,0:T(8,128)S(1)}, u32[]{:S(2)}, u32[]{:S(2)}) collective-permute-start(f32[96,2048]{1,0:T(8,128)S(1)} %get-tuple-element.76), channel_id=1, source_target_pairs={{0,1},{1,0},{2,3},{3,2},{4,5},{5,4},{6,7},{7,6},{8,9},{9,8},{10,11... | collective-permute-start | bytes 2359304 | tf_op jit(solution)/shard_map/ppermute | solution.py:633
  46.7 12.0 %collective-permute-start = (f32[2,32,2048]{2,1,0:T(8,128)S(1)}, f32[2,32,2048]{2,1,0:T(8,128)S(1)}, u32[]{:S(2)}, u32[]{:S(2)}) collective-permute-start(f32[2,32,2048]{2,1,0:T(8,128)S(1)} %copy-done.9), channel_id=1, source_target_pairs={{0,2},{1,4},{2,0},{3,6},{4,1},{5,7},{6,3},{7,5},{8,10},{9,12},{10,... | collective-permute-start | bytes 1572872 | tf_op jit(solution)/shard_map/ppermute | solution.py:628
  47.1 13.0 %collective-permute-start.1 = (f32[2,32,2048]{2,1,0:T(8,128)S(1)}, f32[2,32,2048]{2,1,0:T(8,128)S(1)}, u32[]{:S(2)}, u32[]{:S(2)}) collective-permute-start(f32[2,32,2048]{2,1,0:T(8,128)S(1)} %copy-done.4), channel_id=1, source_target_pairs={{1,6},{3,4},{4,3},{6,1},{9,14},{11,12},{12,11},{14,9},{17,22},{19,... | collective-permute-start | bytes 1572872 | tf_op jit(solution)/shard_map/ppermute | solution.py:628
  47.8 12.3 %collective-permute-start.11 = (f32[48,896]{1,0:T(8,128)S(1)}, f32[48,896]{1,0:T(8,128)S(1)}, u32[]{:S(2)}, u32[]{:S(2)}) collective-permute-start(f32[48,896]{1,0:T(8,128)S(1)} %get-tuple-element.80), channel_id=1, source_target_pairs={{0,24},{8,16},{16,8},{24,0},{1,25},{9,17},{17,9},{25,1},{2,26},{10... | collective-permute-start | bytes 516104 | tf_op jit(solution)/shard_map/ppermute | solution.py:680
  50.5 12.0 %collective-permute-start.12 = (f32[48,896]{1,0:T(8,128)S(1)}, f32[48,896]{1,0:T(8,128)S(1)}, u32[]{:S(2)}, u32[]{:S(2)}) collective-permute-start(f32[48,896]{1,0:T(8,128)S(1)} %get-tuple-element.81), channel_id=1, source_target_pairs={{0,8},{8,0},{16,24},{24,16},{1,9},{9,1},{17,25},{25,17},{2,10},{10... | collective-permute-start | bytes 516104 | tf_op jit(solution)/shard_map/ppermute | solution.py:681
  53.2 16.8 %collective-permute-start.16 = (f32[48,1152]{1,0:T(8,128)S(1)}, f32[48,1152]{1,0:T(8,128)S(1)}, u32[]{:S(2)}, u32[]{:S(2)}) collective-permute-start(f32[48,1152]{1,0:T(8,128)S(1)} %get-tuple-element.87), channel_id=1, source_target_pairs={{0,24},{8,16},{16,8},{24,0},{1,25},{9,17},{17,9},{25,1},{2,26},{10... | collective-permute-start | bytes 663560 | tf_op jit(solution)/shard_map/ppermute | solution.py:687
  58.7 3.7 %copy-start.11 = (f32[2,32,2048]{2,1,0:T(8,128)}, f32[2,32,2048]{2,1,0:T(8,128)S(1)}, u32[]{:S(2)}) copy-start(f32[2,32,2048]{2,1,0:T(8,128)S(1)} %collective-permute-done.refs_0_) | copy-start | bytes 1572868
  58.7 11.3 %collective-permute-start.17 = (f32[48,1152]{1,0:T(8,128)S(1)}, f32[48,1152]{1,0:T(8,128)S(1)}, u32[]{:S(2)}, u32[]{:S(2)}) collective-permute-start(f32[48,1152]{1,0:T(8,128)S(1)} %get-tuple-element.88), channel_id=1, source_target_pairs={{0,8},{8,0},{16,24},{24,16},{1,9},{9,1},{17,25},{25,17},{2,10},{10... | collective-permute-start | bytes 663560 | tf_op jit(solution)/shard_map/ppermute | solution.py:688
  60.1 2.3 %copy-start.12 = (f32[2,32,2048]{2,1,0:T(8,128)}, f32[2,32,2048]{2,1,0:T(8,128)S(1)}, u32[]{:S(2)}) copy-start(f32[2,32,2048]{2,1,0:T(8,128)S(1)} %collective-permute-done.1.refs_1_) | copy-start | bytes 1572868
  64.3 3.2 %collective-permute-start.13 = (f32[32,1408]{1,0:T(8,128)S(1)}, f32[32,1408]{1,0:T(8,128)S(1)}, u32[]{:S(2)}, u32[]{:S(2)}) collective-permute-start(f32[32,1408]{1,0:T(8,128)S(1)} %get-tuple-element.84), channel_id=1, source_target_pairs={{0,1},{1,0},{2,3},{3,2},{4,5},{5,4},{6,7},{7,6},{8,9},{9,8},{10,11... | collective-permute-start | bytes 540680 | tf_op jit(solution)/shard_map/ppermute | solution.py:633
  65.9 1.7 %collective-permute-start.15 = (f32[32,1408]{1,0:T(8,128)S(1)}, f32[32,1408]{1,0:T(8,128)S(1)}, u32[]{:S(2)}, u32[]{:S(2)}) collective-permute-start(f32[32,1408]{1,0:T(8,128)S(1)} %get-tuple-element.86), channel_id=1, source_target_pairs={{0,1},{1,0},{2,3},{3,2},{4,5},{5,4},{6,7},{7,6},{8,9},{9,8},{10,11... | collective-permute-start | bytes 540680 | tf_op jit(solution)/shard_map/ppermute | solution.py:633
  66.0 1.6 %collective-permute-start.14 = (f32[32,1280]{1,0:T(8,128)S(1)}, f32[32,1280]{1,0:T(8,128)S(1)}, u32[]{:S(2)}, u32[]{:S(2)}) collective-permute-start(f32[32,1280]{1,0:T(8,128)S(1)} %get-tuple-element.85), channel_id=1, source_target_pairs={{0,1},{1,0},{2,3},{3,2},{4,5},{5,4},{6,7},{7,6},{8,9},{9,8},{10,11... | collective-permute-start | bytes 491528 | tf_op jit(solution)/shard_map/ppermute | solution.py:633

commit v5 on v4

--- a/solution.py
+++ b/solution.py
@@ -319,19 +319,29 @@
     total[tile - margin :, :width] += edge[1]
 
 
-def update_kernel(radius, tile, slots, names, scal, lengths, total, est, across, inside, out, edge, sems):
-    margin = radius + MAXD
-    copies = fetch_sides(scal[names["odd"]], inside, across, edge, sems.at[0], sems.at[1])
+def add_rows(total, first, rows, margin, start):
+    tile = total.shape[0]
+    at = slice(start, start + rows.shape[1])
+
+    @pl.when(first)
+    def _():
+        total[:margin, at] += rows[...]
+
+    @pl.when(jnp.logical_not(first))
+    def _():
+        total[tile - margin :, at] += rows[...]
+
+
+def update_kernel(radius, tile, slots, names, scal, lengths, total, est, across, inside, out):
+    margin = radius + MAXD
     count = alive(scal, names, lengths, 0, slots // 2)
     for slot in range(1, slots):
         count += alive(scal, names, lengths, slot, slots // 2)
     width, cols = inside.shape[1], est.shape[1]
     weight = 1.0 / jnp.full((1, cols), count, F32)
-    for copy in copies:
-        copy.wait()
-    at = slice(cols - width, cols)
-    total[:margin, at] += edge[0]
-    total[tile - margin :, at] += edge[1]
+    even = scal[names["odd"]] == 0
+    add_rows(total, even, across, margin, cols - width)
+    add_rows(total, jnp.logical_not(even), inside, margin, cols - width)
     out[...] = est[...] * weight * pltpu.roll(total[...], LANES - margin, 1)
 
 
@@ -555,18 +565,14 @@
         grid_spec=pltpu.PrefetchScalarGridSpec(
             num_scalar_prefetch=2,
             grid=(1,),
-            in_specs=[in_vmem()] * 2 + [anywhere()] * 2,
+            in_specs=[in_vmem()] * 4,
             out_specs=whole_spec(est.shape),
-            scratch_shapes=[
-                pltpu.VMEM((2,) + inside.shape, F32),
-                pltpu.SemaphoreType.DMA((2,)),
-            ],
         ),
         out_shape=jax.ShapeDtypeStruct(est.shape, F32),
         compiler_params=params(),
         cost_estimate=light(),
         name="update",
-    )(info, lengths, *from_vmem([total, est]), across, inside)
+    )(info, lengths, *from_vmem([total, est, across, inside]))
 
 
 def per_device(estimate, views, psf, offsets, lengths):
@@ -667,9 +673,7 @@
     ]
     others, mine_a = part_pair(away, runs_a, kept_a, packed_a[-1], [rim_middle])
     others = list(others)
-    packed_b[0], across, inside, others[0] = lax.optimization_barrier(
-        (packed_b[0], across, inside, others[0])
-    )
+    others[0], others[1], across, inside = lax.optimization_barrier((others[0], others[1], across, inside))
     sib_a = [lax.ppermute(x, "view", fellow) for x in others]
     kept_b = view_send(packed_b)
     kept_c = view_send(packed_c)

time: 72.9 us -> 70 us (0.960)
  waiting for transfers between devices: 15.8 us -> 11 us
  starting transfers between devices: 19.9 us -> 22.7 us
  local copies, waits for them, and re-layouts: 3.67 us -> 2.73 us
    ppermute x1, waiting for transfers between devices: 5.99 us -> 1.43 us  [per_device(): inside = lax.ppermute(slab[0], 'joined', twin)]
    ppermute x2, starting transfers between devices: 0.51 us -> 1.55 us  [per_device(): sib_a = [lax.ppermute(x, 'view', fellow) for x in others]]
    ppermute x4, starting transfers between devices: 2.15 us -> 3.13 us  [pair_send(): lax.ppermute(x, 'view', [(p, p ^ 1) for p in range(size)])]
    unnamed x32 -> x24, local copies, waits for them, and re-layouts: 3.59 us -> 2.64 us
    ppermute x2, waiting for transfers between devices: 2.34 us -> 1.6 us  [per_device(): inside = lax.ppermute(inside, 'joined', twin)]
    pallas_call x3, Pallas kernels: 6.78 us -> 7.52 us  [pack(): pl.pallas_call(functools.partial(pack_kernel, starts, pieces, len(ins) +...]
  transfers between devices with their start and end apart: 18 -> 18, of which waited for: 5 -> 6; matrix products, arithmetic and copies ran while one was open for 0% -> 1% of each run, Pallas kernels for 37% -> 39%
where the time goes in v5:
time: 70 us; the launch traced here: 69.6 us
  Pallas kernels  33 us (47%)
  starting transfers between devices  22.7 us (32%)
  waiting for transfers between devices  11 us (16%)
  local copies, waits for them, and re-layouts  2.73 us (4%)
    ppermute x6, starting transfers between devices, view_send(): sent.append(lax.ppermute(x, 'view', [(p, q) for p, q in pairs if p != q]))  7.91 us
    pallas_call x3, Pallas kernels, pack(): pl.pallas_call(functools.partial(pack_kernel, starts, pieces, len(ins) +...  7.52 us
    ppermute x6, waiting for transfers between devices, view_send(): sent.append(lax.ppermute(x, 'view', [(p, q) for p, q in pairs if p != q]))  6.82 us
    pallas_call x3, Pallas kernels, part_pair(): pl.pallas_call(functools.partial(pair_kernel, half, runs), grid_spec=pltp...  5.75 us
    pallas_call x1, Pallas kernels, forward(): pl.pallas_call(functools.partial(forward_kernel, radius, cut, names), gri...  5.74 us
    pallas_call x2, Pallas kernels, edges(): pl.pallas_call(functools.partial(edge_kernel, radius, tile, is_first, is_...  5.2 us
    ppermute x2, starting transfers between devices, per_device(): across = lax.ppermute(across, 'joined', other)  4.85 us
    pallas_call x1, Pallas kernels, prepare(): pl.pallas_call(functools.partial(prepare_kernel, radius, names), grid_spe...  4.4 us
  transfers between devices with their start and end apart: 18, of which 6 were waited for; matrix products, arithmetic and copies ran while one was open for 1% of the time, Pallas kernels for 39%

profile of v5, /device:TPU:0, one launch (start us, length us, event | category | flops | bytes accessed | tf_op | source)
XLA Modules:
  0.0 69.6 jit_solution(10632045547102277095)
XLA Ops:
  0.0 0.1 stack.47.info.refs_0_.scal
  0.1 1.9 %pack_first.1 = (f32[2,96,1024]{2,1,0:T(8,128)S(1)}, f32[2,96,1024]{2,1,0:T(8,128)S(1)}) custom-call(s32[11]{0:T(128)S(1)} %stack.47.info.refs_0_.scal, f32[4,128,2048]{2,1,0:T(8,128)} %bitcast.18), custom_call_target="tpu_custom_call" | custom-call | bytes 1024 | tf_op jit(solution)/shard_map/pack_first/pallas_call | solution.py:388
  2.0 0.0 copy-start.2
  2.0 3.0 %collective-permute-start.2 = (f32[2,96,1024]{2,1,0:T(8,128)S(1)}, f32[2,96,1024]{2,1,0:T(8,128)S(1)}, u32[]{:S(2)}, u32[]{:S(2)}) collective-permute-start(f32[2,96,1024]{2,1,0:T(8,128)S(1)} %get-tuple-element.51.refs_2_), channel_id=1, source_target_pairs={{0,2},{1,4},{2,0},{3,6},{4,1},{5,7},{6,3},{7,5},{8,10},{9,12},{10,... | collective-permute-start | bytes 2359304 | tf_op jit(solution)/shard_map/ppermute | solution.py:634
  5.0 1.6 %collective-permute-start.3 = (f32[2,96,1024]{2,1,0:T(8,128)S(1)}, f32[2,96,1024]{2,1,0:T(8,128)}, u32[]{:S(2)}, u32[]{:S(2)}) collective-permute-start(f32[2,96,1024]{2,1,0:T(8,128)S(1)} %get-tuple-element.56.refs_2_), channel_id=1, source_target_pairs={{1,6},{3,4},{4,3},{6,1},{9,14},{11,12},{12,11},{14,9},{17,22},{19,... | collective-permute-start | bytes 2359304 | tf_op jit(solution)/shard_map/ppermute | solution.py:634
  6.6 2.4 %pack_slab.1 = (f32[48,2048]{1,0:T(8,128)S(1)}, f32[48,2048]{1,0:T(8,128)}) custom-call(s32[11]{0:T(128)S(1)} %stack.47.info.refs_0_.scal, f32[128,2048]{1,0:T(8,128)} %bitcast.14, f32[2,96,1024]{2,1,0:T(8,128)S(1)} %get-tuple-element.51.refs_2_), custom_call_target="tpu_custom_call" | custom-call | bytes 1024 | tf_op jit(solution)/shard_map/pack_slab/pallas_call | solution.py:388
  9.0 3.7 %collective-permute-start.4 = (f32[48,2048]{1,0:T(8,128)}, f32[48,2048]{1,0:T(8,128)}, u32[]{:S(2)}, u32[]{:S(2)}) collective-permute-start(f32[48,2048]{1,0:T(8,128)} %get-tuple-element.59), channel_id=1, source_target_pairs={{0,24},{8,16},{16,8},{24,0},{1,25},{9,17},{17,9},{25,1},{2,26},{10... | collective-permute-start | bytes 1179656 | tf_op jit(solution)/shard_map/ppermute | solution.py:655
  12.7 0.0 collective-permute-start.5
  12.7 3.2 %pack_second.1 = (f32[2,96,1024]{2,1,0:T(8,128)}, f32[2,96,1024]{2,1,0:T(8,128)S(1)}, f32[2,32,2048]{2,1,0:T(8,128)S(1)}, f32[2,32,2048]{2,1,0:T(8,128)S(1)}) custom-call(s32[11]{0:T(128)S(1)} %stack.47.info.refs_0_.scal, f32[4,128,2048]{2,1,0:T(8,128)} %bitcast.19, f32[48,2048]{1,0:T(8,128)S(1)} %get-tuple-element.52.refs_2_), custom_call_target="tpu_custom_call" | custom-call | bytes 1024 | tf_op jit(solution)/shard_map/pack_second/pallas_call | solution.py:388
  15.9 0.0 copy-done.2
  15.9 0.0 copy-start.5
  15.9 0.8 %copy-done.5 = f32[2,32,2048]{2,1,0:T(8,128)} copy-done((f32[2,32,2048]{2,1,0:T(8,128)}, f32[2,32,2048]{2,1,0:T(8,128)S(1)}, u32[]{:S(2)}) %copy-start.5) | copy-done | bytes 524312
  16.7 0.5 collective-permute-start.6
  17.3 3.4 %collective-permute-done.2.refs_0_ = f32[2,96,1024]{2,1,0:T(8,128)S(1)} collective-permute-done((f32[2,96,1024]{2,1,0:T(8,128)S(1)}, f32[2,96,1024]{2,1,0:T(8,128)S(1)}, u32[]{:S(2)}, u32[]{:S(2)}) %collective-permute-start.2) | collective-permute-done | bytes 786464 | tf_op jit(solution)/shard_map/ppermute | solution.py:634
  20.6 0.9 %copy-done.7 = f32[2,96,1024]{2,1,0:T(8,128)} copy-done((f32[2,96,1024]{2,1,0:T(8,128)}, f32[2,96,1024]{2,1,0:T(8,128)S(1)}, u32[]{:S(2)}) %copy-start.7) | copy-done | bytes 786456
  21.5 1.5 %collective-permute-start.7 = (f32[2,96,1024]{2,1,0:T(8,128)S(1)}, f32[2,96,1024]{2,1,0:T(8,128)}, u32[]{:S(2)}, u32[]{:S(2)}) collective-permute-start(f32[2,96,1024]{2,1,0:T(8,128)S(1)} %get-tuple-element.67.refs_2_), channel_id=1, source_target_pairs={{1,6},{3,4},{4,3},{6,1},{9,14},{11,12},{12,11},{14,9},{17,22},{19,... | collective-permute-start | bytes 2359304 | tf_op jit(solution)/shard_map/ppermute | solution.py:634
  23.1 0.0 copy-done.10
  23.1 0.1 copy.9.lengths
  23.2 0.8 %copy.6.offsets = s32[4,2]{1,0:T(4,128)S(1)} copy(s32[4,2]{0,1:T(2,128)} %param.8) | data formatting | bytes 64 | tf_op args[3]
  23.9 0.0 copy-done
  23.9 0.0 copy-done.4
  23.9 4.4 %prepare.1 = (f32[4,32,2048]{2,1,0:T(8,128)S(1)}, bf16[4,192,224]{2,1,0:T(8,128)(2,1)S(1)}, bf16[4,256,256]{2,1,0:T(8,128)(2,1)S(1)}, bf16[4,128,256]{2,1,0:T(8,...) custom-call(s32[11]{0:T(128)S(1)} %stack.47.info.refs_0_.scal, ...), custom_call_target="tpu_custom_call" | custom-call | bytes 1024 | tf_op jit(solution)/shard_map/prepare/pallas_call | solution.py:450
  28.3 0.0 collective-permute-done.3.refs_1_
  28.3 1.9 %pair.3 = (f32[96,1024]{1,0:T(8,128)S(1)}, f32[96,1024]{1,0:T(8,128)S(1)}, f32[96,1024]{1,0:T(8,128)S(1)}, f32[96,1024]{1,0:T(8,128)S(1)}) custom-call(s32[11]{0:T(128)S(1)} %stack.47.info.refs_0_.scal, f32[2,96,1024]{2,1,0:T(8,128)} %copy-done.7, f32[2,96,1024]{2,1,0:T(8,128)} %collective-permute-done.3.refs_1_, f32[2,96,1024]{2,1,0:T(8,128)} %copy-done.2, ...), custom_call_target="tpu_custom_call" | custom-call | bytes 1024 | tf_op jit(solution)/shard_map/pair/pallas_call | solution.py:409
  30.3 0.0 copy-done.1
  30.3 0.0 collective-permute-done.4.across
  30.3 1.4 %collective-permute-done.5.inside = f32[48,2048]{1,0:T(8,128)} collective-permute-done((f32[48,2048]{1,0:T(8,128)S(1)}, f32[48,2048]{1,0:T(8,128)}, u32[]{:S(2)}, u32[]{:S(2)}) %collective-permute-start.5) | collective-permute-done | bytes 393248 | tf_op jit(solution)/shard_map/ppermute | solution.py:656
  31.7 1.5 %collective-permute-start.8 = (f32[96,1024]{1,0:T(8,128)S(1)}, f32[96,1024]{1,0:T(8,128)S(1)}, u32[]{:S(2)}, u32[]{:S(2)}) collective-permute-start(f32[96,1024]{1,0:T(8,128)S(1)} %get-tuple-element.71), channel_id=1, source_target_pairs={{0,1},{1,0},{2,3},{3,2},{4,5},{5,4},{6,7},{7,6},{8,9},{9,8},{10,11... | collective-permute-start | bytes 1179656 | tf_op jit(solution)/shard_map/ppermute | solution.py:677
  33.2 0.1 collective-permute-start.9
  33.3 5.7 %forward.1 = (f32[4,96,1024]{2,1,0:T(8,128)S(1)}, f32[4,96,1024]{2,1,0:T(8,128)S(1)}) custom-call(s32[11]{0:T(128)S(1)} %stack.47.info.refs_0_.scal, s32[4,2]{1,0:T(4,128)S(1)} %copy.9.lengths, f32[128,2048]{1,0:T(8,128)S(1)} %bitcast.16, f32[48,2048]{1,0:T(8,128)} %collective-permute-done.4.across, f32[48,2048]{1,0:T(8,128)} %collective-permute-done.5.inside, ...), custom_call_target="tpu_custom_call" | custom-call | bytes 1024 | tf_op jit(solution)/shard_map/forward/pallas_call | solution.py:478
  39.0 0.0 collective-permute-done.8.rest_2_
  39.0 0.0 collective-permute-done.9.rest_3_
  39.0 2.5 %edges.2 = (f32[128,896]{1,0:T(8,128)S(1)}, f32[48,896]{1,0:T(8,128)S(1)}, f32[48,896]{1,0:T(8,128)S(1)}, f32[4,96,128]{2,1,0:T(8,128)S(1)}, f32[4,96,128]{2,1,0:T(8,128)S(1)}) custom-call(s32[11]{0:T(128)S(1)} %stack.47.info.refs_0_.scal, bf16[4,256,256]{2,1,0:T(8,128)(2,1)S(1)} %get-tuple-element.47.by, bf16[4,128,256]{2,1,0:T(8,128)(2,1)S(1)} %get-tuple-element.48.by_low, ...), custom_call_target="tpu_custom_call" | custom-call | bytes 1024 | tf_op jit(solution)/shard_map/edges/pallas_call | solution.py:513
  41.5 0.0 copy-start.6
  41.5 0.0 collective-permute-done.6.refs_0_
  41.6 0.0 collective-permute-done.7.refs_1_
  41.6 1.9 %pair.4 = (f32[96,2048]{1,0:T(8,128)S(1)}, f32[96,1024]{1,0:T(8,128)S(1)}, f32[96,1024]{1,0:T(8,128)S(1)}) custom-call(s32[11]{0:T(128)S(1)} %stack.47.info.refs_0_.scal, f32[2,96,1024]{2,1,0:T(8,128)} %collective-permute-done.6.refs_0_, f32[2,96,1024]{2,1,0:T(8,128)} %collective-permute-done.7.refs_1_, f32[2,96,1024]{2,1,0:T(8,128)} %copy-done.1, ...), custom_call_target="tpu_custom_call" | custom-call | bytes 1024 | tf_op jit(solution)/shard_map/pair/pallas_call | solution.py:409
  43.5 0.5 collective-permute-start.10
  44.0 0.0 copy-done.6
  44.0 0.6 collective-permute-start
  44.6 0.0 copy-done.3
  44.6 0.7 collective-permute-start.1
  45.3 3.6 %collective-permute-start.11 = (f32[48,896]{1,0:T(8,128)S(1)}, f32[48,896]{1,0:T(8,128)S(1)}, u32[]{:S(2)}, u32[]{:S(2)}) collective-permute-start(f32[48,896]{1,0:T(8,128)S(1)} %get-tuple-element.80), channel_id=1, source_target_pairs={{0,24},{8,16},{16,8},{24,0},{1,25},{9,17},{17,9},{25,1},{2,26},{10... | collective-permute-start | bytes 516104 | tf_op jit(solution)/shard_map/ppermute | solution.py:684
  48.9 0.0 collective-permute-start.12
  48.9 0.0 collective-permute-done.10.rest_2_
  48.9 2.7 %edges.3 = (f32[128,1152]{1,0:T(8,128)S(1)}, f32[48,1152]{1,0:T(8,128)S(1)}, f32[48,1152]{1,0:T(8,128)S(1)}) custom-call(s32[11]{0:T(128)S(1)} %stack.47.info.refs_0_.scal, bf16[4,256,256]{2,1,0:T(8,128)(2,1)S(1)} %get-tuple-element.47.by, bf16[4,128,256]{2,1,0:T(8,128)(2,1)S(1)} %get-tuple-element.48.by_low, bf16[448,512]{1,0:T(8,128)(2,1)S(1)} %get-tuple-element.55.bx, ...), custom_call_target="tpu_custom_call" | custom-call | bytes 1024 | tf_op jit(solution)/shard_map/edges/pallas_call | solution.py:513
  51.6 1.2 %collective-permute-start.16 = (f32[48,1152]{1,0:T(8,128)S(1)}, f32[48,1152]{1,0:T(8,128)S(1)}, u32[]{:S(2)}, u32[]{:S(2)}) collective-permute-start(f32[48,1152]{1,0:T(8,128)S(1)} %get-tuple-element.87), channel_id=1, source_target_pairs={{0,24},{8,16},{16,8},{24,0},{1,25},{9,17},{17,9},{25,1},{2,26},{10... | collective-permute-start | bytes 663560 | tf_op jit(solution)/shard_map/ppermute | solution.py:691
  52.8 3.4 %collective-permute-done.refs_0_ = f32[2,32,2048]{2,1,0:T(8,128)S(1)} collective-permute-done((f32[2,32,2048]{2,1,0:T(8,128)S(1)}, f32[2,32,2048]{2,1,0:T(8,128)S(1)}, u32[]{:S(2)}, u32[]{:S(2)}) %collective-permute-start) | collective-permute-done | bytes 524320 | tf_op jit(solution)/shard_map/ppermute | solution.py:634
  56.3 1.6 %collective-permute-start.17 = (f32[48,1152]{1,0:T(8,128)S(1)}, f32[48,1152]{1,0:T(8,128)S(1)}, u32[]{:S(2)}, u32[]{:S(2)}) collective-permute-start(f32[48,1152]{1,0:T(8,128)S(1)} %get-tuple-element.88), channel_id=1, source_target_pairs={{0,8},{8,0},{16,24},{24,16},{1,9},{9,1},{17,25},{25,17},{2,10},{10... | collective-permute-start | bytes 663560 | tf_op jit(solution)/shard_map/ppermute | solution.py:692
  57.9 0.0 collective-permute-done.1.refs_1_
  57.9 0.0 collective-permute-done.11.refs_4_.rest_7_
  57.9 0.7 %collective-permute-done.12.refs_5_.rest_8_ = f32[48,896]{1,0:T(8,128)S(1)} collective-permute-done((f32[48,896]{1,0:T(8,128)S(1)}, f32[48,896]{1,0:T(8,128)S(1)}, u32[]{:S(2)}, u32[]{:S(2)}) %collective-permute-start.12) | collective-permute-done | bytes 172064 | tf_op jit(solution)/shard_map/ppermute | solution.py:685
  58.6 0.1 copy-done.9
  58.7 1.9 %pair.5 = (f32[32,1408]{1,0:T(8,128)S(1)}, f32[32,1280]{1,0:T(8,128)S(1)}, f32[32,1408]{1,0:T(8,128)S(1)}, f32[32,2048]{1,0:T(8,128)S(1)}, f32[32,2048]{1,0:T(8,128)S(1)}) custom-call(s32[11]{0:T(128)S(1)} %stack.47.info.refs_0_.scal, f32[2,32,2048]{2,1,0:T(8,128)} %copy-done.8, f32[2,32,2048]{2,1,0:T(8,128)} %copy-done.9, f32[2,32,2048]{2,1,0:T(8,128)} %copy-done.3, ...), custom_call_target="tpu_custom_call" | custom-call | bytes 1024 | tf_op jit(solution)/shard_map/pair/pallas_call | solution.py:409
  60.5 2.1 %collective-permute-start.13 = (f32[32,1408]{1,0:T(8,128)S(1)}, f32[32,1408]{1,0:T(8,128)S(1)}, u32[]{:S(2)}, u32[]{:S(2)}) collective-permute-start(f32[32,1408]{1,0:T(8,128)S(1)} %get-tuple-element.84), channel_id=1, source_target_pairs={{0,1},{1,0},{2,3},{3,2},{4,5},{5,4},{6,7},{7,6},{8,9},{9,8},{10,11... | collective-permute-start | bytes 540680 | tf_op jit(solution)/shard_map/ppermute | solution.py:639
  62.7 0.1 collective-permute-start.15
  62.7 0.4 collective-permute-start.14
  63.2 1.1 %collective-permute-done.14.rest_3_ = f32[32,1280]{1,0:T(8,128)S(1)} collective-permute-done((f32[32,1280]{1,0:T(8,128)S(1)}, f32[32,1280]{1,0:T(8,128)S(1)}, u32[]{:S(2)}, u32[]{:S(2)}) %collective-permute-start.14) | collective-permute-done | bytes 163872 | tf_op jit(solution)/shard_map/ppermute | solution.py:639
  64.3 0.0 collective-permute-done.13.rest_2_
  64.3 0.0 collective-permute-done.15.rest_4_
  64.3 2.4 %middle.1.total = f32[128,2048]{1,0:T(8,128)S(1)} custom-call(s32[11]{0:T(128)S(1)} %stack.47.info.refs_0_.scal, bf16[4,256,256]{2,1,0:T(8,128)(2,1)S(1)} %get-tuple-element.47.by, bf16[4,128,256]{2,1,0:T(8,128)(2,1)S(1)} %get-tuple-element.48.by_low, bf16[4,256,128]{2,1,0:T(8,128)(2,1)S(1)} %get-tuple-element.49.bm, ...), custom_call_target="tpu_custom_call" | custom-call | bytes 1024 | tf_op jit(solution)/shard_map/middle/pallas_call | solution.py:537
  66.8 0.0 collective-permute-done.16.across
  66.8 0.9 %collective-permute-done.17.inside = f32[48,1152]{1,0:T(8,128)S(1)} collective-permute-done((f32[48,1152]{1,0:T(8,128)S(1)}, f32[48,1152]{1,0:T(8,128)S(1)}, u32[]{:S(2)}, u32[]{:S(2)}) %collective-permute-start.17) | collective-permute-done | bytes 221216 | tf_op jit(solution)/shard_map/ppermute | solution.py:692
  67.7 2.0 %update.1 = f32[128,2048]{1,0:T(8,128)} custom-call(s32[11]{0:T(128)S(1)} %stack.47.info.refs_0_.scal, s32[4,2]{1,0:T(4,128)S(1)} %copy.9.lengths, f32[128,2048]{1,0:T(8,128)S(1)} %middle.1.total, f32[128,2048]{1,0:T(8,128)S(1)} %bitcast.17, f32[48,1152]{1,0:T(8,128)S(1)} %collective-permute-done.16.across, f32[48,1152]{1,0:T(8,128)S(1)} %collective-permute-done.17.inside), custom_call_target="tpu_custom_call" | custom-call | bytes 1024 | tf_op jit(solution)/shard_map/update/pallas_call | solution.py:563
  (9 shorter events, 0.0 us)
Async XLA Ops:
  2.0 13.9 %copy-start.2 = (f32[2,96,1024]{2,1,0:T(8,128)}, f32[2,96,1024]{2,1,0:T(8,128)S(1)}, u32[]{:S(2)}) copy-start(f32[2,96,1024]{2,1,0:T(8,128)S(1)} %get-tuple-element.56.refs_2_) | copy-start | bytes 2359300
  2.0 18.6 %collective-permute-start.2 = (f32[2,96,1024]{2,1,0:T(8,128)S(1)}, f32[2,96,1024]{2,1,0:T(8,128)S(1)}, u32[]{:S(2)}, u32[]{:S(2)}) collective-permute-start(f32[2,96,1024]{2,1,0:T(8,128)S(1)} %get-tuple-element.51.refs_2_), channel_id=1, source_target_pairs={{0,2},{1,4},{2,0},{3,6},{4,1},{5,7},{6,3},{7,5},{8,10},{9,12},{10,... | collective-permute-start | bytes 2359304 | tf_op jit(solution)/shard_map/ppermute | solution.py:634
  5.0 23.3 %collective-permute-start.3 = (f32[2,96,1024]{2,1,0:T(8,128)S(1)}, f32[2,96,1024]{2,1,0:T(8,128)}, u32[]{:S(2)}, u32[]{:S(2)}) collective-permute-start(f32[2,96,1024]{2,1,0:T(8,128)S(1)} %get-tuple-element.56.refs_2_), channel_id=1, source_target_pairs={{1,6},{3,4},{4,3},{6,1},{9,14},{11,12},{12,11},{14,9},{17,22},{19,... | collective-permute-start | bytes 2359304 | tf_op jit(solution)/shard_map/ppermute | solution.py:634
  9.0 21.2 %collective-permute-start.4 = (f32[48,2048]{1,0:T(8,128)}, f32[48,2048]{1,0:T(8,128)}, u32[]{:S(2)}, u32[]{:S(2)}) collective-permute-start(f32[48,2048]{1,0:T(8,128)} %get-tuple-element.59), channel_id=1, source_target_pairs={{0,24},{8,16},{16,8},{24,0},{1,25},{9,17},{17,9},{25,1},{2,26},{10... | collective-permute-start | bytes 1179656 | tf_op jit(solution)/shard_map/ppermute | solution.py:655
  12.7 10.3 %copy-start.10 = (s32[4,2]{0,1:T(2,128)S(1)}, s32[4,2]{0,1:T(2,128)}, u32[]{:S(2)}) copy-start(s32[4,2]{0,1:T(2,128)} %param.9) | copy-start | bytes 100
  12.7 11.2 %copy-start = (f32[1,128,2048]{2,1,0:T(8,128)S(1)}, f32[1,128,2048]{2,1,0:T(8,128)}, u32[]{:S(2)}) copy-start(f32[1,128,2048]{2,1,0:T(8,128)} %param.5) | copy-start | bytes 3145732
  12.7 11.2 %copy-start.4 = (f32[4,2,65]{2,1,0:T(2,128)S(1)}, f32[4,2,65]{2,1,0:T(2,128)}, u32[]{:S(2)}) copy-start(f32[4,2,65]{2,1,0:T(2,128)} %psf.1) | copy-start | bytes 6244
  12.7 19.0 %collective-permute-start.5 = (f32[48,2048]{1,0:T(8,128)S(1)}, f32[48,2048]{1,0:T(8,128)}, u32[]{:S(2)}, u32[]{:S(2)}) collective-permute-start(f32[48,2048]{1,0:T(8,128)S(1)} %get-tuple-element.52.refs_2_), channel_id=1, source_target_pairs={{0,8},{8,0},{16,24},{24,16},{1,9},{9,1},{17,25},{25,17},{2,10},{10... | collective-permute-start | bytes 1179656 | tf_op jit(solution)/shard_map/ppermute | solution.py:656
  15.9 0.8 %copy-start.5 = (f32[2,32,2048]{2,1,0:T(8,128)}, f32[2,32,2048]{2,1,0:T(8,128)S(1)}, u32[]{:S(2)}) copy-start(f32[2,32,2048]{2,1,0:T(8,128)S(1)} %get-tuple-element.53) | copy-start | bytes 1572868
  16.7 13.6 %copy-start.1 = (f32[2,96,1024]{2,1,0:T(8,128)}, f32[2,96,1024]{2,1,0:T(8,128)S(1)}, u32[]{:S(2)}) copy-start(f32[2,96,1024]{2,1,0:T(8,128)S(1)} %get-tuple-element.67.refs_2_) | copy-start | bytes 2359300
  16.7 27.9 %copy-start.3 = (f32[2,32,2048]{2,1,0:T(8,128)}, f32[2,32,2048]{2,1,0:T(8,128)S(1)}, u32[]{:S(2)}) copy-start(f32[2,32,2048]{2,1,0:T(8,128)S(1)} %get-tuple-element.54.refs_2_) | copy-start | bytes 1572868
  16.7 24.8 %collective-permute-start.6 = (f32[2,96,1024]{2,1,0:T(8,128)}, f32[2,96,1024]{2,1,0:T(8,128)}, u32[]{:S(2)}, u32[]{:S(2)}) collective-permute-start(f32[2,96,1024]{2,1,0:T(8,128)} %get-tuple-element.66), channel_id=1, source_target_pairs={{0,2},{1,4},{2,0},{3,6},{4,1},{5,7},{6,3},{7,5},{8,10},{9,12},{10,... | collective-permute-start | bytes 2359304 | tf_op jit(solution)/shard_map/ppermute | solution.py:634
  20.6 0.9 %copy-start.7 = (f32[2,96,1024]{2,1,0:T(8,128)}, f32[2,96,1024]{2,1,0:T(8,128)S(1)}, u32[]{:S(2)}) copy-start(f32[2,96,1024]{2,1,0:T(8,128)S(1)} %collective-permute-done.2.refs_0_) | copy-start | bytes 2359300
  21.5 20.1 %collective-permute-start.7 = (f32[2,96,1024]{2,1,0:T(8,128)S(1)}, f32[2,96,1024]{2,1,0:T(8,128)}, u32[]{:S(2)}, u32[]{:S(2)}) collective-permute-start(f32[2,96,1024]{2,1,0:T(8,128)S(1)} %get-tuple-element.67.refs_2_), channel_id=1, source_target_pairs={{1,6},{3,4},{4,3},{6,1},{9,14},{11,12},{12,11},{14,9},{17,22},{19,... | collective-permute-start | bytes 2359304 | tf_op jit(solution)/shard_map/ppermute | solution.py:634
  31.7 7.3 %collective-permute-start.8 = (f32[96,1024]{1,0:T(8,128)S(1)}, f32[96,1024]{1,0:T(8,128)S(1)}, u32[]{:S(2)}, u32[]{:S(2)}) collective-permute-start(f32[96,1024]{1,0:T(8,128)S(1)} %get-tuple-element.71), channel_id=1, source_target_pairs={{0,1},{1,0},{2,3},{3,2},{4,5},{5,4},{6,7},{7,6},{8,9},{9,8},{10,11... | collective-permute-start | bytes 1179656 | tf_op jit(solution)/shard_map/ppermute | solution.py:677
  33.2 5.8 %collective-permute-start.9 = (f32[96,1024]{1,0:T(8,128)S(1)}, f32[96,1024]{1,0:T(8,128)S(1)}, u32[]{:S(2)}, u32[]{:S(2)}) collective-permute-start(f32[96,1024]{1,0:T(8,128)S(1)} %get-tuple-element.72), channel_id=1, source_target_pairs={{0,1},{1,0},{2,3},{3,2},{4,5},{5,4},{6,7},{7,6},{8,9},{9,8},{10,11... | collective-permute-start | bytes 1179656 | tf_op jit(solution)/shard_map/ppermute | solution.py:677
  41.5 2.5 %copy-start.6 = (f32[2,32,2048]{2,1,0:T(8,128)S(1)}, f32[2,32,2048]{2,1,0:T(8,128)}, u32[]{:S(2)}) copy-start(f32[2,32,2048]{2,1,0:T(8,128)} %copy-done.5) | copy-start | bytes 1572868
  43.5 5.4 %collective-permute-start.10 = (f32[96,2048]{1,0:T(8,128)S(1)}, f32[96,2048]{1,0:T(8,128)S(1)}, u32[]{:S(2)}, u32[]{:S(2)}) collective-permute-start(f32[96,2048]{1,0:T(8,128)S(1)} %get-tuple-element.76), channel_id=1, source_target_pairs={{0,1},{1,0},{2,3},{3,2},{4,5},{5,4},{6,7},{7,6},{8,9},{9,8},{10,11... | collective-permute-start | bytes 2359304 | tf_op jit(solution)/shard_map/ppermute | solution.py:639
  44.0 12.3 %collective-permute-start = (f32[2,32,2048]{2,1,0:T(8,128)S(1)}, f32[2,32,2048]{2,1,0:T(8,128)S(1)}, u32[]{:S(2)}, u32[]{:S(2)}) collective-permute-start(f32[2,32,2048]{2,1,0:T(8,128)S(1)} %copy-done.6), channel_id=1, source_target_pairs={{0,2},{1,4},{2,0},{3,6},{4,1},{5,7},{6,3},{7,5},{8,10},{9,12},{10,... | collective-permute-start | bytes 1572872 | tf_op jit(solution)/shard_map/ppermute | solution.py:634
  44.6 13.3 %collective-permute-start.1 = (f32[2,32,2048]{2,1,0:T(8,128)S(1)}, f32[2,32,2048]{2,1,0:T(8,128)S(1)}, u32[]{:S(2)}, u32[]{:S(2)}) collective-permute-start(f32[2,32,2048]{2,1,0:T(8,128)S(1)} %get-tuple-element.54.refs_2_), channel_id=1, source_target_pairs={{1,6},{3,4},{4,3},{6,1},{9,14},{11,12},{12,11},{14,9},{17,22},{19,... | collective-permute-start | bytes 1572872 | tf_op jit(solution)/shard_map/ppermute | solution.py:634
  45.3 12.6 %collective-permute-start.11 = (f32[48,896]{1,0:T(8,128)S(1)}, f32[48,896]{1,0:T(8,128)S(1)}, u32[]{:S(2)}, u32[]{:S(2)}) collective-permute-start(f32[48,896]{1,0:T(8,128)S(1)} %get-tuple-element.80), channel_id=1, source_target_pairs={{0,24},{8,16},{16,8},{24,0},{1,25},{9,17},{17,9},{25,1},{2,26},{10... | collective-permute-start | bytes 516104 | tf_op jit(solution)/shard_map/ppermute | solution.py:684
  48.9 9.7 %collective-permute-start.12 = (f32[48,896]{1,0:T(8,128)S(1)}, f32[48,896]{1,0:T(8,128)S(1)}, u32[]{:S(2)}, u32[]{:S(2)}) collective-permute-start(f32[48,896]{1,0:T(8,128)S(1)} %get-tuple-element.81), channel_id=1, source_target_pairs={{0,8},{8,0},{16,24},{24,16},{1,9},{9,1},{17,25},{25,17},{2,10},{10... | collective-permute-start | bytes 516104 | tf_op jit(solution)/shard_map/ppermute | solution.py:685
  51.6 15.1 %collective-permute-start.16 = (f32[48,1152]{1,0:T(8,128)S(1)}, f32[48,1152]{1,0:T(8,128)S(1)}, u32[]{:S(2)}, u32[]{:S(2)}) collective-permute-start(f32[48,1152]{1,0:T(8,128)S(1)} %get-tuple-element.87), channel_id=1, source_target_pairs={{0,24},{8,16},{16,8},{24,0},{1,25},{9,17},{17,9},{25,1},{2,26},{10... | collective-permute-start | bytes 663560 | tf_op jit(solution)/shard_map/ppermute | solution.py:691
  56.3 2.3 %copy-start.8 = (f32[2,32,2048]{2,1,0:T(8,128)}, f32[2,32,2048]{2,1,0:T(8,128)S(1)}, u32[]{:S(2)}) copy-start(f32[2,32,2048]{2,1,0:T(8,128)S(1)} %collective-permute-done.refs_0_) | copy-start | bytes 1572868
  56.3 11.4 %collective-permute-start.17 = (f32[48,1152]{1,0:T(8,128)S(1)}, f32[48,1152]{1,0:T(8,128)S(1)}, u32[]{:S(2)}, u32[]{:S(2)}) collective-permute-start(f32[48,1152]{1,0:T(8,128)S(1)} %get-tuple-element.88), channel_id=1, source_target_pairs={{0,8},{8,0},{16,24},{24,16},{1,9},{9,1},{17,25},{25,17},{2,10},{10... | collective-permute-start | bytes 663560 | tf_op jit(solution)/shard_map/ppermute | solution.py:692
  57.9 0.8 %copy-start.9 = (f32[2,32,2048]{2,1,0:T(8,128)}, f32[2,32,2048]{2,1,0:T(8,128)S(1)}, u32[]{:S(2)}) copy-start(f32[2,32,2048]{2,1,0:T(8,128)S(1)} %collective-permute-done.1.refs_1_) | copy-start | bytes 1572868
  60.5 3.8 %collective-permute-start.13 = (f32[32,1408]{1,0:T(8,128)S(1)}, f32[32,1408]{1,0:T(8,128)S(1)}, u32[]{:S(2)}, u32[]{:S(2)}) collective-permute-start(f32[32,1408]{1,0:T(8,128)S(1)} %get-tuple-element.84), channel_id=1, source_target_pairs={{0,1},{1,0},{2,3},{3,2},{4,5},{5,4},{6,7},{7,6},{8,9},{9,8},{10,11... | collective-permute-start | bytes 540680 | tf_op jit(solution)/shard_map/ppermute | solution.py:639
  62.7 1.7 %collective-permute-start.15 = (f32[32,1408]{1,0:T(8,128)S(1)}, f32[32,1408]{1,0:T(8,128)S(1)}, u32[]{:S(2)}, u32[]{:S(2)}) collective-permute-start(f32[32,1408]{1,0:T(8,128)S(1)} %get-tuple-element.86), channel_id=1, source_target_pairs={{0,1},{1,0},{2,3},{3,2},{4,5},{5,4},{6,7},{7,6},{8,9},{9,8},{10,11... | collective-permute-start | bytes 540680 | tf_op jit(solution)/shard_map/ppermute | solution.py:639
  62.7 1.6 %collective-permute-start.14 = (f32[32,1280]{1,0:T(8,128)S(1)}, f32[32,1280]{1,0:T(8,128)S(1)}, u32[]{:S(2)}, u32[]{:S(2)}) collective-permute-start(f32[32,1280]{1,0:T(8,128)S(1)} %get-tuple-element.85), channel_id=1, source_target_pairs={{0,1},{1,0},{2,3},{3,2},{4,5},{5,4},{6,7},{7,6},{8,9},{9,8},{10,11... | collective-permute-start | bytes 491528 | tf_op jit(solution)/shard_map/ppermute | solution.py:639

commit v6 on v5

--- a/solution.py
+++ b/solution.py
@@ -39,7 +39,7 @@
 
 def alive(info, names, lengths, slot, half):
     view = slot_view(info, names, slot, half)
-    return jnp.where(info[names["row"]] < lengths[view, info[names["block"]]], 1.0, 0.0)
+    return jnp.where(info[names["row"]] < lengths[info[names["block"]], view], 1.0, 0.0)
 
 
 def toeplitz(row, rows, shift, width):
@@ -101,7 +101,7 @@
         taps[...] = jnp.zeros(taps.shape, F32)
 
     view = slot_view(info, names, slot, half)
-    dx, dy = offsets[view, 0], offsets[view, 1]
+    dx, dy = offsets[0, view], offsets[1, view]
     weights = psf[view]
     taps[0:2, : 2 * radius + 1] = weights / jnp.sum(weights, axis=1, keepdims=True)
     gx, gy = taps[0:1, :], taps[1:2, :]
@@ -135,22 +135,30 @@
 
 
 def forward_kernel(radius, cut, names, info, lengths, est, across, inside, fx, fy, fy_low, *rest):
-    outs, (e_hi, e_lo, lhs, halo, sems) = rest[:-5], rest[-5:]
+    outs, (e_hi, e_lo, lhs) = rest[:-3], rest[-3:]
     slot = pl.program_id(0)
     margin = radius + MAXD
     tile, cols = est.shape
     edge = 2 * margin
+    even = info[names["odd"]] == 0
+
+    def put(piece, at):
+        rows = slice(at, at + piece.shape[0])
+        e_hi[rows, :], e_lo[rows, :] = split(pltpu.roll(piece[...], margin, 1))
 
     @pl.when(slot == 0)
     def _():
-        copies = fetch_sides(info[names["odd"]], inside, across, halo, sems.at[0], sems.at[1])
-        for piece, at in ((est, margin), (halo.at[0], 0), (halo.at[1], margin + tile)):
-            if at == 0:
-                for copy in copies:
-                    copy.wait()
-            top, rest = split(pltpu.roll(piece[...], margin, 1))
-            e_hi[at : at + piece.shape[0], :] = top
-            e_lo[at : at + piece.shape[0], :] = rest
+        put(est, margin)
+
+    @pl.when((slot == 0) & even)
+    def _():
+        put(across, 0)
+        put(inside, margin + tile)
+
+    @pl.when((slot == 0) & jnp.logical_not(even))
+    def _():
+        put(inside, 0)
+        put(across, margin + tile)
 
     live = alive(info, names, lengths, slot, outs[0].shape[0] // 2)
     both = mm(fx[0], e_hi[...])
@@ -196,42 +204,34 @@
     return parts[0] if len(parts) == 1 else jnp.concatenate(parts, axis=1)
 
 
-def fetch_either(flag, source, other, target, sem):
-    @pl.when(flag != 0)
-    def _():
-        fetch(other, target, sem)
-
-    @pl.when(flag == 0)
-    def _():
-        fetch(source, target, sem)
-
-    return pltpu.make_async_copy(source, target, sem)
-
-
 def pair_kernel(half, runs, scal, *refs):
     kept, own, refs = refs[:half], refs[half], refs[half + 1 :]
-    outs, sem = refs[-1 - len(runs) - half : -1], refs[-1]
+    outs, (buffer, sem) = refs[-2 - len(runs) - half : -2], refs[-2:]
     away, inner = scal[half], scal[half + 1]
-    copies = []
-    for out, of_out in zip(outs, runs):
-        at = 0
-        for view, c0, c1 in of_out:
-            cols = slice(c0 * LANES, c1 * LANES)
-            target = out.at[:, at : at + (c1 - c0) * LANES]
-            place = (kept[view].at[away, :, cols], target, sem.at[len(copies)])
-            if view < half - 1:
-                copies.append(fetch(*place))
-            else:
-                copies.append(fetch_either(inner, place[0], own.at[away, :, cols], *place[1:]))
-            at += (c1 - c0) * LANES
-    for s, out in enumerate(outs[len(runs) :]):
-        place = (kept[s].at[1 - away], out, sem.at[len(copies)])
-        if s < half - 1:
-            copies.append(fetch(*place))
-        else:
-            copies.append(fetch_either(inner, place[0], own.at[1 - away], *place[1:]))
-    for copy in copies:
+    last = half - 1
+
+    def part(view, source):
+        for out, of_out in zip(outs, runs):
+            at = 0
+            for which, c0, c1 in of_out:
+                width = (c1 - c0) * LANES
+                if which == view:
+                    out[:, at : at + width] = source[away, :, c0 * LANES : c1 * LANES]
+                at += width
+        outs[len(runs) + view][...] = source[1 - away]
+
+    @pl.when(inner != 0)
+    def _():
+        copy = fetch(own, buffer, sem.at[0])
+        for view in range(last):
+            part(view, kept[view])
         copy.wait()
+        part(last, buffer)
+
+    @pl.when(inner == 0)
+    def _():
+        for view in range(half):
+            part(view, kept[view])
 
 
 def edge_kernel(radius, tile, is_first, is_last, half, runs, names, scal, by, by_low, bx, rim, *rest):
@@ -287,13 +287,7 @@
 def middle_kernel(radius, tile, half, runs, names, scal, by, by_low, bm, rim, *rest):
     mine, rest = rest[:half], rest[half:]
     sib, rest = rest[: len(runs)], rest[len(runs) :]
-    first, second, across, inside, total, lhs, s_hi, s_lo, part, edge, sems = rest
-    width = first.shape[1]
-    late = [
-        fetch(first, part.at[:, :width], sems.at[0]),
-        fetch(second, part.at[:, width:], sems.at[1]),
-        *fetch_sides(scal[names["odd"]], inside, across, edge, sems.at[2], sems.at[3]),
-    ]
+    first, second, across, inside, total, lhs, s_hi, s_lo = rest
     slots = 2 * half
     margin = radius + MAXD
     mid = tile - 2 * margin
@@ -312,11 +306,13 @@
             s_hi[base : base + mid, at] = hi
             s_lo[base : base + mid, at] = lo
     both = mm(band, s_hi[...])
-    for copy in late:
-        copy.wait()
-    total[...] = both[:tile] + both[tile:] + mm(band[:tile], s_lo[...]) + part[...]
-    total[:margin, :width] += edge[0]
-    total[tile - margin :, :width] += edge[1]
+    total[...] = both[:tile] + both[tile:] + mm(band[:tile], s_lo[...])
+    width = first.shape[1]
+    total[:, :width] += first[...]
+    total[:, width:] += second[...]
+    even = scal[names["odd"]] == 0
+    add_rows(total, even, across, margin, 0)
+    add_rows(total, jnp.logical_not(even), inside, margin, 0)
 
 
 def add_rows(total, first, rows, margin, start):
@@ -411,15 +407,15 @@
         grid_spec=pltpu.PrefetchScalarGridSpec(
             num_scalar_prefetch=1,
             grid=(1,),
-            in_specs=[in_hbm()] * (half + 1) + [anywhere()] * len(after),
+            in_specs=[in_vmem()] * half + [in_hbm()] + [anywhere()] * len(after),
             out_specs=[in_vmem()] * len(shapes),
-            scratch_shapes=[pltpu.SemaphoreType.DMA((half + sum(len(of) for of in runs),))],
+            scratch_shapes=[pltpu.VMEM(own.shape, F32), pltpu.SemaphoreType.DMA((1,))],
         ),
         out_shape=[jax.ShapeDtypeStruct(s, F32) for s in shapes],
         compiler_params=params(),
         cost_estimate=light(),
         name="pair",
-    )(scal, *from_hbm([*kept, own]), *after)
+    )(scal, *from_vmem(kept), *from_hbm([own]), *after)
     return out[: len(runs)], out[len(runs) :]
 
 
@@ -480,22 +476,20 @@
         grid_spec=pltpu.PrefetchScalarGridSpec(
             num_scalar_prefetch=2,
             grid=(slots,),
-            in_specs=[in_vmem(), in_hbm(), in_hbm()]
+            in_specs=[in_vmem()] * 3
             + [pl.BlockSpec((1,) + x.shape[1:], lambda i, *_: (i, 0, 0)) for x in (fx, fy, fy_low)],
             out_specs=[in_vmem()] * len(shapes),
             scratch_shapes=[
                 pltpu.VMEM((extended, cols), BF16),
                 pltpu.VMEM((extended, cols), BF16),
                 pltpu.VMEM((2 * margin * cols // LANES, 2 * LANES), BF16),
-                pltpu.VMEM((2, margin, cols), F32),
-                pltpu.SemaphoreType.DMA((2,)),
             ],
         ),
         out_shape=[jax.ShapeDtypeStruct(s, F32) for s in shapes],
         compiler_params=params(),
         cost_estimate=light(),
         name="forward",
-    )(info, lengths, *from_vmem([est]), *from_hbm([across, inside]), fx, fy, fy_low)
+    )(info, lengths, *from_vmem([est, across, inside]), fx, fy, fy_low)
 
 
 def edges(radius, tile, is_first, is_last, runs, names, scal, bands, rim, mine, sib, carries):
@@ -539,23 +533,19 @@
         grid_spec=pltpu.PrefetchScalarGridSpec(
             num_scalar_prefetch=1,
             grid=(1,),
-            in_specs=[in_vmem()] * (4 + half + len(runs))
-            + [anywhere()] * 4,
+            in_specs=[in_vmem()] * (8 + half + len(runs)),
             out_specs=in_vmem(),
             scratch_shapes=[
                 pltpu.VMEM((cols // LANES * mid, 2 * LANES), BF16),
                 pltpu.VMEM((slots * mid, cols), BF16),
                 pltpu.VMEM((slots * mid, cols), BF16),
-                pltpu.VMEM((tile, cols), F32),
-                pltpu.VMEM((2,) + inside.shape, F32),
-                pltpu.SemaphoreType.DMA((4,)),
             ],
         ),
         out_shape=jax.ShapeDtypeStruct((tile, cols), F32),
         compiler_params=params(),
         cost_estimate=light(),
         name="middle",
-    )(scal, *from_vmem([*bands, rim, *mine, *sib]), *mains, across, inside)
+    )(scal, *from_vmem([*bands, rim, *mine, *sib, *mains, across, inside]))
 
 
 def update(radius, slots, names, info, lengths, total, est, inside, across):
@@ -664,7 +654,7 @@
         "pack_second",
     )
     rim_middle, fx, fy, fy_low, by, by_low, bx, bm = prepare(
-        radius, names, away, offsets, lengths, psf, est
+        radius, names, away, offsets.T, lengths.T, psf, est
     )
     packed_b, packed_c = list(packed[:half]), packed[half:]
     fellow = [(p, p ^ 1) for p in range(size)]
@@ -677,7 +667,7 @@
     sib_a = [lax.ppermute(x, "view", fellow) for x in others]
     kept_b = view_send(packed_b)
     kept_c = view_send(packed_c)
-    rims = forward(radius, cut, names, away, lengths, est, across, inside, fx, fy, fy_low)
+    rims = forward(radius, cut, names, away, lengths.T, est, across, inside, fx, fy, fy_low)
     main, across, inside, *carries = edges(
         radius, tile, True, False, runs_a, names, away, (by, by_low, bx), rims[0], mine_a, sib_a, []
     )
@@ -696,7 +686,7 @@
     mains = [chunk[0] for chunk in chunks]
     bands = (by, by_low, bm)
     total = middle(radius, tile, runs, names, away, bands, rim_middle, mine, sib, mains, *chunks[0][1:])
-    out = update(radius, members, names, away, lengths, total, est, *chunks[1][1:])
+    out = update(radius, members, names, away, lengths.T, total, est, *chunks[1][1:])
     return out[None]
 
 

time: 70 us -> 67.9 us (0.970)
  Pallas kernels: 33 us -> 29.5 us
  waiting for transfers between devices: 11 us -> 14.3 us
  local copies, waits for them, and re-layouts: 2.73 us -> 0.12 us
    ppermute x4, starting transfers between devices: 3.13 us -> 5.76 us  [pair_send(): lax.ppermute(x, 'view', [(p, p ^ 1) for p in range(size)])]
    unnamed x24 -> x14, local copies, waits for them, and re-layouts: 2.64 us -> 0.03 us
    ppermute x6, waiting for transfers between devices: 6.82 us -> 9 us  [view_send(): sent.append(lax.ppermute(x, 'view', [(p, q) for p, q in pairs if p != q]))]
    pallas_call x3, Pallas kernels: 7.52 us -> 5.9 us  [pack(): pl.pallas_call(functools.partial(pack_kernel, starts, pieces, len(ins) +...]
    ppermute x2, starting transfers between devices: 1.55 us -> 0.54 us  [per_device(): sib_a = [lax.ppermute(x, 'view', fellow) for x in others]]
    ppermute x1, waiting for transfers between devices: 1.43 us -> 2.19 us  [per_device(): inside = lax.ppermute(slab[0], 'joined', twin)]
    ppermute x6, starting transfers between devices: 7.91 us -> 7.17 us  [view_send(): sent.append(lax.ppermute(x, 'view', [(p, q) for p, q in pairs if p != q]))]
    pallas_call x1, Pallas kernels: 5.74 us -> 5.01 us  [forward(): pl.pallas_call(functools.partial(forward_kernel, radius, cut, names), gri...]
  transfers between devices with their start and end apart: 18 -> 18, of which waited for: 6 -> 6; matrix products, arithmetic and copies ran while one was open for 1% -> 0% of each run, Pallas kernels for 39% -> 35%
where the time goes in v6:
time: 67.9 us; the launch traced here: 67.5 us
  Pallas kernels  29.5 us (43%)
  starting transfers between devices  23.4 us (34%)
  waiting for transfers between devices  14.3 us (21%)
    ppermute x6, waiting for transfers between devices, view_send(): sent.append(lax.ppermute(x, 'view', [(p, q) for p, q in pairs if p != q]))  9 us
    ppermute x6, starting transfers between devices, view_send(): sent.append(lax.ppermute(x, 'view', [(p, q) for p, q in pairs if p != q]))  7.17 us
    pallas_call x3, Pallas kernels, pack(): pl.pallas_call(functools.partial(pack_kernel, starts, pieces, len(ins) +...  5.9 us
    ppermute x4, starting transfers between devices, pair_send(): lax.ppermute(x, 'view', [(p, p ^ 1) for p in range(size)])  5.76 us
    pallas_call x2, Pallas kernels, edges(): pl.pallas_call(functools.partial(edge_kernel, radius, tile, is_first, is_...  5.28 us
    pallas_call x3, Pallas kernels, part_pair(): pl.pallas_call(functools.partial(pair_kernel, half, runs), grid_spec=pltp...  5.11 us
    pallas_call x1, Pallas kernels, forward(): pl.pallas_call(functools.partial(forward_kernel, radius, cut, names), gri...  5.01 us
    ppermute x2, starting transfers between devices, per_device(): across = lax.ppermute(across, 'joined', other)  4.63 us
  transfers between devices with their start and end apart: 18, of which 6 were waited for; matrix products, arithmetic and copies ran while one was open for 0% of the time, Pallas kernels for 35%

profile of v6, /device:TPU:0, one launch (start us, length us, event | category | flops | bytes accessed | tf_op | source)
XLA Modules:
  0.0 67.5 jit_solution(12699581426649148467)
XLA Ops:
  0.0 0.1 stack.47.info.refs_0_.scal
  0.1 1.9 %pack_first.1 = (f32[2,96,1024]{2,1,0:T(8,128)S(1)}, f32[2,96,1024]{2,1,0:T(8,128)S(1)}) custom-call(s32[11]{0:T(128)S(1)} %stack.47.info.refs_0_.scal, f32[4,128,2048]{2,1,0:T(8,128)} %bitcast.24), custom_call_target="tpu_custom_call" | custom-call | bytes 1024 | tf_op jit(solution)/shard_map/pack_first/pallas_call | solution.py:384
  2.0 0.0 copy-start.2
  2.0 3.0 %collective-permute-start.2 = (f32[2,96,1024]{2,1,0:T(8,128)S(1)}, f32[2,96,1024]{2,1,0:T(8,128)S(1)}, u32[]{:S(2)}, u32[]{:S(2)}) collective-permute-start(f32[2,96,1024]{2,1,0:T(8,128)S(1)} %get-tuple-element.51.refs_2_), channel_id=1, source_target_pairs={{0,2},{1,4},{2,0},{3,6},{4,1},{5,7},{6,3},{7,5},{8,10},{9,12},{10,... | collective-permute-start | bytes 2359304 | tf_op jit(solution)/shard_map/ppermute | solution.py:624
  5.0 0.7 %collective-permute-start.3 = (f32[2,96,1024]{2,1,0:T(8,128)S(1)}, f32[2,96,1024]{2,1,0:T(8,128)S(1)}, u32[]{:S(2)}, u32[]{:S(2)}) collective-permute-start(f32[2,96,1024]{2,1,0:T(8,128)S(1)} %get-tuple-element.56.refs_2_), channel_id=1, source_target_pairs={{1,6},{3,4},{4,3},{6,1},{9,14},{11,12},{12,11},{14,9},{17,22},{19,... | collective-permute-start | bytes 2359304 | tf_op jit(solution)/shard_map/ppermute | solution.py:624
  5.8 1.7 %pack_slab.1 = (f32[48,2048]{1,0:T(8,128)S(1)}, f32[48,2048]{1,0:T(8,128)S(1)}) custom-call(s32[11]{0:T(128)S(1)} %stack.47.info.refs_0_.scal, f32[128,2048]{1,0:T(8,128)} %bitcast.16, f32[2,96,1024]{2,1,0:T(8,128)S(1)} %get-tuple-element.51.refs_2_), custom_call_target="tpu_custom_call" | custom-call | bytes 1024 | tf_op jit(solution)/shard_map/pack_slab/pallas_call | solution.py:384
  7.4 3.7 %collective-permute-start.4 = (f32[48,2048]{1,0:T(8,128)S(1)}, f32[48,2048]{1,0:T(8,128)S(1)}, u32[]{:S(2)}, u32[]{:S(2)}) collective-permute-start(f32[48,2048]{1,0:T(8,128)S(1)} %get-tuple-element.59), channel_id=1, source_target_pairs={{0,24},{8,16},{16,8},{24,0},{1,25},{9,17},{17,9},{25,1},{2,26},{10... | collective-permute-start | bytes 1179656 | tf_op jit(solution)/shard_map/ppermute | solution.py:645
  11.1 0.0 copy-start
  11.1 0.0 copy-start.4
  11.1 0.0 copy-start.5
  11.1 0.0 copy-start.6
  11.1 0.1 collective-permute-start.5
  11.2 2.3 %pack_second.1 = (f32[2,96,1024]{2,1,0:T(8,128)S(1)}, f32[2,96,1024]{2,1,0:T(8,128)S(1)}, f32[2,32,2048]{2,1,0:T(8,128)S(1)}, f32[2,32,2048]{2,1,0:T(8,128)S(1)}) custom-call(s32[11]{0:T(128)S(1)} %stack.47.info.refs_0_.scal, f32[4,128,2048]{2,1,0:T(8,128)} %bitcast.25, f32[48,2048]{1,0:T(8,128)S(1)} %get-tuple-element.52.refs_2_), custom_call_target="tpu_custom_call" | custom-call | bytes 1024 | tf_op jit(solution)/shard_map/pack_second/pallas_call | solution.py:384
  13.5 0.0 copy-done.2
  13.5 0.0 copy-start.1
  13.5 0.0 copy-start.3
  13.5 0.6 collective-permute-start.6
  14.1 6.5 %collective-permute-done.2.refs_0_ = f32[2,96,1024]{2,1,0:T(8,128)S(1)} collective-permute-done((f32[2,96,1024]{2,1,0:T(8,128)S(1)}, f32[2,96,1024]{2,1,0:T(8,128)S(1)}, u32[]{:S(2)}, u32[]{:S(2)}) %collective-permute-start.2) | collective-permute-done | bytes 786464 | tf_op jit(solution)/shard_map/ppermute | solution.py:624
  20.6 0.7 %collective-permute-start.7 = (f32[2,96,1024]{2,1,0:T(8,128)S(1)}, f32[2,96,1024]{2,1,0:T(8,128)S(1)}, u32[]{:S(2)}, u32[]{:S(2)}) collective-permute-start(f32[2,96,1024]{2,1,0:T(8,128)S(1)} %get-tuple-element.67.refs_2_), channel_id=1, source_target_pairs={{1,6},{3,4},{4,3},{6,1},{9,14},{11,12},{12,11},{14,9},{17,22},{19,... | collective-permute-start | bytes 2359304 | tf_op jit(solution)/shard_map/ppermute | solution.py:624
  21.3 0.0 copy-done
  21.3 0.0 copy-done.4
  21.4 0.0 copy-done.5
  21.4 0.0 copy-done.6
  21.4 4.4 %prepare.1 = (f32[4,32,2048]{2,1,0:T(8,128)S(1)}, bf16[4,192,224]{2,1,0:T(8,128)(2,1)S(1)}, bf16[4,256,256]{2,1,0:T(8,128)(2,1)S(1)}, bf16[4,128,256]{2,1,0:T(8,...) custom-call(s32[11]{0:T(128)S(1)} %stack.47.info.refs_0_.scal, ...), custom_call_target="tpu_custom_call" | custom-call | bytes 1024 | tf_op jit(solution)/shard_map/prepare/pallas_call | solution.py:446
  25.8 0.0 collective-permute-done.3.refs_1_
  25.8 1.7 %pair.3 = (f32[96,1024]{1,0:T(8,128)S(1)}, f32[96,1024]{1,0:T(8,128)S(1)}, f32[96,1024]{1,0:T(8,128)S(1)}, f32[96,1024]{1,0:T(8,128)S(1)}) custom-call(s32[11]{0:T(128)S(1)} %stack.47.info.refs_0_.scal, f32[2,96,1024]{2,1,0:T(8,128)S(1)} %collective-permute-done.2.refs_0_, f32[2,96,1024]{2,1,0:T(8,128)S(1)} %collective-permute-done.3.refs_1_, ...), custom_call_target="tpu_custom_call" | custom-call | bytes 1024 | tf_op jit(solution)/shard_map/pair/pallas_call | solution.py:405
  27.5 0.0 copy-done.1
  27.5 0.0 collective-permute-done.4.across
  27.5 2.2 %collective-permute-done.5.inside = f32[48,2048]{1,0:T(8,128)S(1)} collective-permute-done((f32[48,2048]{1,0:T(8,128)S(1)}, f32[48,2048]{1,0:T(8,128)S(1)}, u32[]{:S(2)}, u32[]{:S(2)}) %collective-permute-start.5) | collective-permute-done | bytes 393248 | tf_op jit(solution)/shard_map/ppermute | solution.py:646
  29.7 0.5 collective-permute-start.8
  30.2 0.1 collective-permute-start.9
  30.3 5.0 %forward.1 = (f32[4,96,1024]{2,1,0:T(8,128)S(1)}, f32[4,96,1024]{2,1,0:T(8,128)S(1)}) custom-call(s32[11]{0:T(128)S(1)} %stack.47.info.refs_0_.scal, s32[2,4]{1,0:T(2,128)S(1)} %bitcast.21, f32[128,2048]{1,0:T(8,128)S(1)} %bitcast.18, f32[48,2048]{1,0:T(8,128)S(1)} %collective-permute-done.4.across, f32[48,2048]{1,0:T(8,128)S(1)} %collective-permute-done.5.inside, ...), custom_call_target="tpu_custom_call" | custom-call | bytes 1024 | tf_op jit(solution)/shard_map/forward/pallas_call | solution.py:474
  35.3 0.0 collective-permute-done.8.rest_2_
  35.3 0.0 collective-permute-done.9.rest_3_
  35.3 2.5 %edges.2 = (f32[128,896]{1,0:T(8,128)S(1)}, f32[48,896]{1,0:T(8,128)S(1)}, f32[48,896]{1,0:T(8,128)S(1)}, f32[4,96,128]{2,1,0:T(8,128)S(1)}, f32[4,96,128]{2,1,0:T(8,128)S(1)}) custom-call(s32[11]{0:T(128)S(1)} %stack.47.info.refs_0_.scal, bf16[4,256,256]{2,1,0:T(8,128)(2,1)S(1)} %get-tuple-element.47.by, bf16[4,128,256]{2,1,0:T(8,128)(2,1)S(1)} %get-tuple-element.48.by_low, ...), custom_call_target="tpu_custom_call" | custom-call | bytes 1024 | tf_op jit(solution)/shard_map/edges/pallas_call | solution.py:507
  37.9 0.0 collective-permute-done.6.refs_0_
  37.9 0.0 collective-permute-done.7.refs_1_
  37.9 1.7 %pair.4 = (f32[96,2048]{1,0:T(8,128)S(1)}, f32[96,1024]{1,0:T(8,128)S(1)}, f32[96,1024]{1,0:T(8,128)S(1)}) custom-call(s32[11]{0:T(128)S(1)} %stack.47.info.refs_0_.scal, f32[2,96,1024]{2,1,0:T(8,128)S(1)} %collective-permute-done.6.refs_0_, f32[2,96,1024]{2,1,0:T(8,128)S(1)} %collective-permute-done.7.refs_1_, f32[2,96,1024]{2,1,0:T(8,128)} %copy-done.1, ...), custom_call_target="tpu_custom_call" | custom-call | bytes 1024 | tf_op jit(solution)/shard_map/pair/pallas_call | solution.py:405
  39.6 1.6 %collective-permute-start.10 = (f32[96,2048]{1,0:T(8,128)S(1)}, f32[96,2048]{1,0:T(8,128)S(1)}, u32[]{:S(2)}, u32[]{:S(2)}) collective-permute-start(f32[96,2048]{1,0:T(8,128)S(1)} %get-tuple-element.76), channel_id=1, source_target_pairs={{0,1},{1,0},{2,3},{3,2},{4,5},{5,4},{6,7},{7,6},{8,9},{9,8},{10,11... | collective-permute-start | bytes 2359304 | tf_op jit(solution)/shard_map/ppermute | solution.py:629
  41.2 1.5 %collective-permute-start = (f32[2,32,2048]{2,1,0:T(8,128)S(1)}, f32[2,32,2048]{2,1,0:T(8,128)S(1)}, u32[]{:S(2)}, u32[]{:S(2)}) collective-permute-start(f32[2,32,2048]{2,1,0:T(8,128)S(1)} %get-tuple-element.53), channel_id=1, source_target_pairs={{0,2},{1,4},{2,0},{3,6},{4,1},{5,7},{6,3},{7,5},{8,10},{9,12},{10,... | collective-permute-start | bytes 1572872 | tf_op jit(solution)/shard_map/ppermute | solution.py:624
  42.7 0.0 copy-done.3
  42.7 0.7 %collective-permute-start.1 = (f32[2,32,2048]{2,1,0:T(8,128)S(1)}, f32[2,32,2048]{2,1,0:T(8,128)S(1)}, u32[]{:S(2)}, u32[]{:S(2)}) collective-permute-start(f32[2,32,2048]{2,1,0:T(8,128)S(1)} %get-tuple-element.54.refs_2_), channel_id=1, source_target_pairs={{1,6},{3,4},{4,3},{6,1},{9,14},{11,12},{12,11},{14,9},{17,22},{19,... | collective-permute-start | bytes 1572872 | tf_op jit(solution)/shard_map/ppermute | solution.py:624
  43.4 3.7 %collective-permute-start.11 = (f32[48,896]{1,0:T(8,128)S(1)}, f32[48,896]{1,0:T(8,128)S(1)}, u32[]{:S(2)}, u32[]{:S(2)}) collective-permute-start(f32[48,896]{1,0:T(8,128)S(1)} %get-tuple-element.80), channel_id=1, source_target_pairs={{0,24},{8,16},{16,8},{24,0},{1,25},{9,17},{17,9},{25,1},{2,26},{10... | collective-permute-start | bytes 516104 | tf_op jit(solution)/shard_map/ppermute | solution.py:674
  47.1 0.0 collective-permute-start.12
  47.1 0.0 collective-permute-done.10.rest_2_
  47.1 2.7 %edges.3 = (f32[128,1152]{1,0:T(8,128)S(1)}, f32[48,1152]{1,0:T(8,128)S(1)}, f32[48,1152]{1,0:T(8,128)S(1)}) custom-call(s32[11]{0:T(128)S(1)} %stack.47.info.refs_0_.scal, bf16[4,256,256]{2,1,0:T(8,128)(2,1)S(1)} %get-tuple-element.47.by, bf16[4,128,256]{2,1,0:T(8,128)(2,1)S(1)} %get-tuple-element.48.by_low, bf16[448,512]{1,0:T(8,128)(2,1)S(1)} %get-tuple-element.55.bx, ...), custom_call_target="tpu_custom_call" | custom-call | bytes 1024 | tf_op jit(solution)/shard_map/edges/pallas_call | solution.py:507
  49.8 1.0 %collective-permute-start.16 = (f32[48,1152]{1,0:T(8,128)S(1)}, f32[48,1152]{1,0:T(8,128)S(1)}, u32[]{:S(2)}, u32[]{:S(2)}) collective-permute-start(f32[48,1152]{1,0:T(8,128)S(1)} %get-tuple-element.87), channel_id=1, source_target_pairs={{0,24},{8,16},{16,8},{24,0},{1,25},{9,17},{17,9},{25,1},{2,26},{10... | collective-permute-start | bytes 663560 | tf_op jit(solution)/shard_map/ppermute | solution.py:681
  50.8 2.5 %collective-permute-done.refs_0_ = f32[2,32,2048]{2,1,0:T(8,128)S(1)} collective-permute-done((f32[2,32,2048]{2,1,0:T(8,128)S(1)}, f32[2,32,2048]{2,1,0:T(8,128)S(1)}, u32[]{:S(2)}, u32[]{:S(2)}) %collective-permute-start) | collective-permute-done | bytes 524320 | tf_op jit(solution)/shard_map/ppermute | solution.py:624
  53.2 1.6 %collective-permute-start.17 = (f32[48,1152]{1,0:T(8,128)S(1)}, f32[48,1152]{1,0:T(8,128)S(1)}, u32[]{:S(2)}, u32[]{:S(2)}) collective-permute-start(f32[48,1152]{1,0:T(8,128)S(1)} %get-tuple-element.88), channel_id=1, source_target_pairs={{0,8},{8,0},{16,24},{24,16},{1,9},{9,1},{17,25},{25,17},{2,10},{10... | collective-permute-start | bytes 663560 | tf_op jit(solution)/shard_map/ppermute | solution.py:682
  54.8 0.0 collective-permute-done.1.refs_1_
  54.8 0.0 collective-permute-done.11.refs_4_.rest_7_
  54.8 1.1 %collective-permute-done.12.refs_5_.rest_8_ = f32[48,896]{1,0:T(8,128)S(1)} collective-permute-done((f32[48,896]{1,0:T(8,128)S(1)}, f32[48,896]{1,0:T(8,128)S(1)}, u32[]{:S(2)}, u32[]{:S(2)}) %collective-permute-start.12) | collective-permute-done | bytes 172064 | tf_op jit(solution)/shard_map/ppermute | solution.py:675
  55.9 1.6 %pair.5 = (f32[32,1408]{1,0:T(8,128)S(1)}, f32[32,1280]{1,0:T(8,128)S(1)}, f32[32,1408]{1,0:T(8,128)S(1)}, f32[32,2048]{1,0:T(8,128)S(1)}, f32[32,2048]{1,0:T(8,128)S(1)}) custom-call(s32[11]{0:T(128)S(1)} %stack.47.info.refs_0_.scal, f32[2,32,2048]{2,1,0:T(8,128)S(1)} %collective-permute-done.refs_0_, f32[2,32,2048]{2,1,0:T(8,128)S(1)} %collective-permute-done.1.refs_1_, ...), custom_call_target="tpu_custom_call" | custom-call | bytes 1024 | tf_op jit(solution)/shard_map/pair/pallas_call | solution.py:405
  57.6 3.7 %collective-permute-start.13 = (f32[32,1408]{1,0:T(8,128)S(1)}, f32[32,1408]{1,0:T(8,128)S(1)}, u32[]{:S(2)}, u32[]{:S(2)}) collective-permute-start(f32[32,1408]{1,0:T(8,128)S(1)} %get-tuple-element.84), channel_id=1, source_target_pairs={{0,1},{1,0},{2,3},{3,2},{4,5},{5,4},{6,7},{7,6},{8,9},{9,8},{10,11... | collective-permute-start | bytes 540680 | tf_op jit(solution)/shard_map/ppermute | solution.py:629
  61.3 0.1 collective-permute-start.15
  61.3 0.4 collective-permute-start.14
  61.8 1.1 %collective-permute-done.14.rest_3_ = f32[32,1280]{1,0:T(8,128)S(1)} collective-permute-done((f32[32,1280]{1,0:T(8,128)S(1)}, f32[32,1280]{1,0:T(8,128)S(1)}, u32[]{:S(2)}, u32[]{:S(2)}) %collective-permute-start.14) | collective-permute-done | bytes 163872 | tf_op jit(solution)/shard_map/ppermute | solution.py:629
  62.9 0.0 collective-permute-done.13.rest_2_
  62.9 0.0 collective-permute-done.15.rest_4_
  62.9 1.9 %middle.1.total = f32[128,2048]{1,0:T(8,128)S(1)} custom-call(s32[11]{0:T(128)S(1)} %stack.47.info.refs_0_.scal, bf16[4,256,256]{2,1,0:T(8,128)(2,1)S(1)} %get-tuple-element.47.by, bf16[4,128,256]{2,1,0:T(8,128)(2,1)S(1)} %get-tuple-element.48.by_low, bf16[4,256,128]{2,1,0:T(8,128)(2,1)S(1)} %get-tuple-element.49.bm, ...), custom_call_target="tpu_custom_call" | custom-call | bytes 1024 | tf_op jit(solution)/shard_map/middle/pallas_call | solution.py:531
  64.8 0.0 collective-permute-done.16.across
  64.8 0.8 %collective-permute-done.17.inside = f32[48,1152]{1,0:T(8,128)S(1)} collective-permute-done((f32[48,1152]{1,0:T(8,128)S(1)}, f32[48,1152]{1,0:T(8,128)S(1)}, u32[]{:S(2)}, u32[]{:S(2)}) %collective-permute-start.17) | collective-permute-done | bytes 221216 | tf_op jit(solution)/shard_map/ppermute | solution.py:682
  65.6 1.9 %update.1 = f32[128,2048]{1,0:T(8,128)} custom-call(s32[11]{0:T(128)S(1)} %stack.47.info.refs_0_.scal, s32[2,4]{1,0:T(2,128)S(1)} %bitcast.22, f32[128,2048]{1,0:T(8,128)S(1)} %middle.1.total, f32[128,2048]{1,0:T(8,128)S(1)} %bitcast.19, f32[48,1152]{1,0:T(8,128)S(1)} %collective-permute-done.16.across, f32[48,1152]{1,0:T(8,128)S(1)} %collective-permute-done.17.inside), custom_call_target="tpu_custom_call" | custom-call | bytes 1024 | tf_op jit(solution)/shard_map/update/pallas_call | solution.py:553
Async XLA Ops:
  2.0 11.5 %copy-start.2 = (f32[2,96,1024]{2,1,0:T(8,128)}, f32[2,96,1024]{2,1,0:T(8,128)S(1)}, u32[]{:S(2)}) copy-start(f32[2,96,1024]{2,1,0:T(8,128)S(1)} %get-tuple-element.56.refs_2_) | copy-start | bytes 2359300
  2.0 18.6 %collective-permute-start.2 = (f32[2,96,1024]{2,1,0:T(8,128)S(1)}, f32[2,96,1024]{2,1,0:T(8,128)S(1)}, u32[]{:S(2)}, u32[]{:S(2)}) collective-permute-start(f32[2,96,1024]{2,1,0:T(8,128)S(1)} %get-tuple-element.51.refs_2_), channel_id=1, source_target_pairs={{0,2},{1,4},{2,0},{3,6},{4,1},{5,7},{6,3},{7,5},{8,10},{9,12},{10,... | collective-permute-start | bytes 2359304 | tf_op jit(solution)/shard_map/ppermute | solution.py:624
  5.0 20.7 %collective-permute-start.3 = (f32[2,96,1024]{2,1,0:T(8,128)S(1)}, f32[2,96,1024]{2,1,0:T(8,128)S(1)}, u32[]{:S(2)}, u32[]{:S(2)}) collective-permute-start(f32[2,96,1024]{2,1,0:T(8,128)S(1)} %get-tuple-element.56.refs_2_), channel_id=1, source_target_pairs={{1,6},{3,4},{4,3},{6,1},{9,14},{11,12},{12,11},{14,9},{17,22},{19,... | collective-permute-start | bytes 2359304 | tf_op jit(solution)/shard_map/ppermute | solution.py:624
  7.4 20.1 %collective-permute-start.4 = (f32[48,2048]{1,0:T(8,128)S(1)}, f32[48,2048]{1,0:T(8,128)S(1)}, u32[]{:S(2)}, u32[]{:S(2)}) collective-permute-start(f32[48,2048]{1,0:T(8,128)S(1)} %get-tuple-element.59), channel_id=1, source_target_pairs={{0,24},{8,16},{16,8},{24,0},{1,25},{9,17},{17,9},{25,1},{2,26},{10... | collective-permute-start | bytes 1179656 | tf_op jit(solution)/shard_map/ppermute | solution.py:645
  11.1 10.2 %copy-start = (f32[1,128,2048]{2,1,0:T(8,128)S(1)}, f32[1,128,2048]{2,1,0:T(8,128)}, u32[]{:S(2)}) copy-start(f32[1,128,2048]{2,1,0:T(8,128)} %param.5) | copy-start | bytes 3145732
  11.1 10.2 %copy-start.4 = (s32[4,2]{0,1:T(2,128)S(1)}, s32[4,2]{0,1:T(2,128)}, u32[]{:S(2)}) copy-start(s32[4,2]{0,1:T(2,128)} %param.9) | copy-start | bytes 100
  11.1 10.2 %copy-start.5 = (f32[4,2,65]{2,1,0:T(2,128)S(1)}, f32[4,2,65]{2,1,0:T(2,128)}, u32[]{:S(2)}) copy-start(f32[4,2,65]{2,1,0:T(2,128)} %psf.1) | copy-start | bytes 6244
  11.1 10.3 %copy-start.6 = (s32[4,2]{0,1:T(2,128)S(1)}, s32[4,2]{0,1:T(2,128)}, u32[]{:S(2)}) copy-start(s32[4,2]{0,1:T(2,128)} %param.8) | copy-start | bytes 100
  11.1 18.6 %collective-permute-start.5 = (f32[48,2048]{1,0:T(8,128)S(1)}, f32[48,2048]{1,0:T(8,128)S(1)}, u32[]{:S(2)}, u32[]{:S(2)}) collective-permute-start(f32[48,2048]{1,0:T(8,128)S(1)} %get-tuple-element.52.refs_2_), channel_id=1, source_target_pairs={{0,8},{8,0},{16,24},{24,16},{1,9},{9,1},{17,25},{25,17},{2,10},{10... | collective-permute-start | bytes 1179656 | tf_op jit(solution)/shard_map/ppermute | solution.py:646
  13.5 14.0 %copy-start.1 = (f32[2,96,1024]{2,1,0:T(8,128)}, f32[2,96,1024]{2,1,0:T(8,128)S(1)}, u32[]{:S(2)}) copy-start(f32[2,96,1024]{2,1,0:T(8,128)S(1)} %get-tuple-element.67.refs_2_) | copy-start | bytes 2359300
  13.5 29.2 %copy-start.3 = (f32[2,32,2048]{2,1,0:T(8,128)}, f32[2,32,2048]{2,1,0:T(8,128)S(1)}, u32[]{:S(2)}) copy-start(f32[2,32,2048]{2,1,0:T(8,128)S(1)} %get-tuple-element.54.refs_2_) | copy-start | bytes 1572868
  13.5 24.3 %collective-permute-start.6 = (f32[2,96,1024]{2,1,0:T(8,128)S(1)}, f32[2,96,1024]{2,1,0:T(8,128)S(1)}, u32[]{:S(2)}, u32[]{:S(2)}) collective-permute-start(f32[2,96,1024]{2,1,0:T(8,128)S(1)} %get-tuple-element.66), channel_id=1, source_target_pairs={{0,2},{1,4},{2,0},{3,6},{4,1},{5,7},{6,3},{7,5},{8,10},{9,12},{10,... | collective-permute-start | bytes 2359304 | tf_op jit(solution)/shard_map/ppermute | solution.py:624
  20.6 17.2 %collective-permute-start.7 = (f32[2,96,1024]{2,1,0:T(8,128)S(1)}, f32[2,96,1024]{2,1,0:T(8,128)S(1)}, u32[]{:S(2)}, u32[]{:S(2)}) collective-permute-start(f32[2,96,1024]{2,1,0:T(8,128)S(1)} %get-tuple-element.67.refs_2_), channel_id=1, source_target_pairs={{1,6},{3,4},{4,3},{6,1},{9,14},{11,12},{12,11},{14,9},{17,22},{19,... | collective-permute-start | bytes 2359304 | tf_op jit(solution)/shard_map/ppermute | solution.py:624
  29.7 5.6 %collective-permute-start.8 = (f32[96,1024]{1,0:T(8,128)S(1)}, f32[96,1024]{1,0:T(8,128)S(1)}, u32[]{:S(2)}, u32[]{:S(2)}) collective-permute-start(f32[96,1024]{1,0:T(8,128)S(1)} %get-tuple-element.71), channel_id=1, source_target_pairs={{0,1},{1,0},{2,3},{3,2},{4,5},{5,4},{6,7},{7,6},{8,9},{9,8},{10,11... | collective-permute-start | bytes 1179656 | tf_op jit(solution)/shard_map/ppermute | solution.py:667
  30.2 5.1 %collective-permute-start.9 = (f32[96,1024]{1,0:T(8,128)S(1)}, f32[96,1024]{1,0:T(8,128)S(1)}, u32[]{:S(2)}, u32[]{:S(2)}) collective-permute-start(f32[96,1024]{1,0:T(8,128)S(1)} %get-tuple-element.72), channel_id=1, source_target_pairs={{0,1},{1,0},{2,3},{3,2},{4,5},{5,4},{6,7},{7,6},{8,9},{9,8},{10,11... | collective-permute-start | bytes 1179656 | tf_op jit(solution)/shard_map/ppermute | solution.py:667
  39.6 7.4 %collective-permute-start.10 = (f32[96,2048]{1,0:T(8,128)S(1)}, f32[96,2048]{1,0:T(8,128)S(1)}, u32[]{:S(2)}, u32[]{:S(2)}) collective-permute-start(f32[96,2048]{1,0:T(8,128)S(1)} %get-tuple-element.76), channel_id=1, source_target_pairs={{0,1},{1,0},{2,3},{3,2},{4,5},{5,4},{6,7},{7,6},{8,9},{9,8},{10,11... | collective-permute-start | bytes 2359304 | tf_op jit(solution)/shard_map/ppermute | solution.py:629
  41.2 12.0 %collective-permute-start = (f32[2,32,2048]{2,1,0:T(8,128)S(1)}, f32[2,32,2048]{2,1,0:T(8,128)S(1)}, u32[]{:S(2)}, u32[]{:S(2)}) collective-permute-start(f32[2,32,2048]{2,1,0:T(8,128)S(1)} %get-tuple-element.53), channel_id=1, source_target_pairs={{0,2},{1,4},{2,0},{3,6},{4,1},{5,7},{6,3},{7,5},{8,10},{9,12},{10,... | collective-permute-start | bytes 1572872 | tf_op jit(solution)/shard_map/ppermute | solution.py:624
  42.7 12.1 %collective-permute-start.1 = (f32[2,32,2048]{2,1,0:T(8,128)S(1)}, f32[2,32,2048]{2,1,0:T(8,128)S(1)}, u32[]{:S(2)}, u32[]{:S(2)}) collective-permute-start(f32[2,32,2048]{2,1,0:T(8,128)S(1)} %get-tuple-element.54.refs_2_), channel_id=1, source_target_pairs={{1,6},{3,4},{4,3},{6,1},{9,14},{11,12},{12,11},{14,9},{17,22},{19,... | collective-permute-start | bytes 1572872 | tf_op jit(solution)/shard_map/ppermute | solution.py:624
  43.4 11.4 %collective-permute-start.11 = (f32[48,896]{1,0:T(8,128)S(1)}, f32[48,896]{1,0:T(8,128)S(1)}, u32[]{:S(2)}, u32[]{:S(2)}) collective-permute-start(f32[48,896]{1,0:T(8,128)S(1)} %get-tuple-element.80), channel_id=1, source_target_pairs={{0,24},{8,16},{16,8},{24,0},{1,25},{9,17},{17,9},{25,1},{2,26},{10... | collective-permute-start | bytes 516104 | tf_op jit(solution)/shard_map/ppermute | solution.py:674
  47.1 8.9 %collective-permute-start.12 = (f32[48,896]{1,0:T(8,128)S(1)}, f32[48,896]{1,0:T(8,128)S(1)}, u32[]{:S(2)}, u32[]{:S(2)}) collective-permute-start(f32[48,896]{1,0:T(8,128)S(1)} %get-tuple-element.81), channel_id=1, source_target_pairs={{0,8},{8,0},{16,24},{24,16},{1,9},{9,1},{17,25},{25,17},{2,10},{10... | collective-permute-start | bytes 516104 | tf_op jit(solution)/shard_map/ppermute | solution.py:675
  49.8 15.0 %collective-permute-start.16 = (f32[48,1152]{1,0:T(8,128)S(1)}, f32[48,1152]{1,0:T(8,128)S(1)}, u32[]{:S(2)}, u32[]{:S(2)}) collective-permute-start(f32[48,1152]{1,0:T(8,128)S(1)} %get-tuple-element.87), channel_id=1, source_target_pairs={{0,24},{8,16},{16,8},{24,0},{1,25},{9,17},{17,9},{25,1},{2,26},{10... | collective-permute-start | bytes 663560 | tf_op jit(solution)/shard_map/ppermute | solution.py:681
  53.2 12.3 %collective-permute-start.17 = (f32[48,1152]{1,0:T(8,128)S(1)}, f32[48,1152]{1,0:T(8,128)S(1)}, u32[]{:S(2)}, u32[]{:S(2)}) collective-permute-start(f32[48,1152]{1,0:T(8,128)S(1)} %get-tuple-element.88), channel_id=1, source_target_pairs={{0,8},{8,0},{16,24},{24,16},{1,9},{9,1},{17,25},{25,17},{2,10},{10... | collective-permute-start | bytes 663560 | tf_op jit(solution)/shard_map/ppermute | solution.py:682
  57.6 5.3 %collective-permute-start.13 = (f32[32,1408]{1,0:T(8,128)S(1)}, f32[32,1408]{1,0:T(8,128)S(1)}, u32[]{:S(2)}, u32[]{:S(2)}) collective-permute-start(f32[32,1408]{1,0:T(8,128)S(1)} %get-tuple-element.84), channel_id=1, source_target_pairs={{0,1},{1,0},{2,3},{3,2},{4,5},{5,4},{6,7},{7,6},{8,9},{9,8},{10,11... | collective-permute-start | bytes 540680 | tf_op jit(solution)/shard_map/ppermute | solution.py:629
  61.3 1.7 %collective-permute-start.15 = (f32[32,1408]{1,0:T(8,128)S(1)}, f32[32,1408]{1,0:T(8,128)S(1)}, u32[]{:S(2)}, u32[]{:S(2)}) collective-permute-start(f32[32,1408]{1,0:T(8,128)S(1)} %get-tuple-element.86), channel_id=1, source_target_pairs={{0,1},{1,0},{2,3},{3,2},{4,5},{5,4},{6,7},{7,6},{8,9},{9,8},{10,11... | collective-permute-start | bytes 540680 | tf_op jit(solution)/shard_map/ppermute | solution.py:629
  61.3 1.6 %collective-permute-start.14 = (f32[32,1280]{1,0:T(8,128)S(1)}, f32[32,1280]{1,0:T(8,128)S(1)}, u32[]{:S(2)}, u32[]{:S(2)}) collective-permute-start(f32[32,1280]{1,0:T(8,128)S(1)} %get-tuple-element.85), channel_id=1, source_target_pairs={{0,1},{1,0},{2,3},{3,2},{4,5},{5,4},{6,7},{7,6},{8,9},{9,8},{10,11... | collective-permute-start | bytes 491528 | tf_op jit(solution)/shard_map/ppermute | solution.py:629

commit v7 on v6

--- a/solution.py
+++ b/solution.py
@@ -57,13 +57,6 @@
     copy = pltpu.make_async_copy(source, target, sem)
     copy.start()
     return copy
-
-
-def fetch_sides(odd, inside, across, target, first_sem, second_sem):
-    return [
-        fetch(inside, target.at[1 - odd], first_sem),
-        fetch(across, target.at[odd], second_sem),
-    ]
 
 
 def images(lhs, first, second, rows, blocks):
@@ -206,7 +199,7 @@
 
 def pair_kernel(half, runs, scal, *refs):
     kept, own, refs = refs[:half], refs[half], refs[half + 1 :]
-    outs, (buffer, sem) = refs[-2 - len(runs) - half : -2], refs[-2:]
+    outs = refs[-len(runs) - half :]
     away, inner = scal[half], scal[half + 1]
     last = half - 1
 
@@ -222,11 +215,9 @@
 
     @pl.when(inner != 0)
     def _():
-        copy = fetch(own, buffer, sem.at[0])
         for view in range(last):
             part(view, kept[view])
-        copy.wait()
-        part(last, buffer)
+        part(last, own)
 
     @pl.when(inner == 0)
     def _():
@@ -407,15 +398,14 @@
         grid_spec=pltpu.PrefetchScalarGridSpec(
             num_scalar_prefetch=1,
             grid=(1,),
-            in_specs=[in_vmem()] * half + [in_hbm()] + [anywhere()] * len(after),
+            in_specs=[in_vmem()] * (half + 1) + [anywhere()] * len(after),
             out_specs=[in_vmem()] * len(shapes),
-            scratch_shapes=[pltpu.VMEM(own.shape, F32), pltpu.SemaphoreType.DMA((1,))],
         ),
         out_shape=[jax.ShapeDtypeStruct(s, F32) for s in shapes],
         compiler_params=params(),
         cost_estimate=light(),
         name="pair",
-    )(scal, *from_vmem(kept), *from_hbm([own]), *after)
+    )(scal, *from_vmem([*kept, own]), *after)
     return out[: len(runs)], out[len(runs) :]
 
 
@@ -682,7 +672,7 @@
     inside = lax.ppermute(inside, "joined", twin)
     chunks.append((main, inside, across))
     runs = runs_of(3, half, total_blocks)
-    mine, sib = pair_send(runs, kept_c, packed_c[-1], [main, chunks[0][2], chunks[0][1]])
+    mine, sib = pair_send(runs, kept_c, packed_c[-1], [main])
     mains = [chunk[0] for chunk in chunks]
     bands = (by, by_low, bm)
     total = middle(radius, tile, runs, names, away, bands, rim_middle, mine, sib, mains, *chunks[0][1:])

time: 67.9 us -> 67.7 us (level)
  Pallas kernels: 29.5 us -> 26.3 us
  starting transfers between devices: 23.4 us -> 25.4 us
  waiting for transfers between devices: 14.3 us -> 15.5 us
    pallas_call x3, Pallas kernels: 5.11 us -> 1.93 us  [part_pair(): pl.pallas_call(functools.partial(pair_kernel, half, runs), grid_spec=pltp...]
    ppermute x4, starting transfers between devices: 5.76 us -> 7.76 us  [pair_send(): lax.ppermute(x, 'view', [(p, p ^ 1) for p in range(size)])]
    ppermute x1, waiting for transfers between devices: 2.19 us -> 3.28 us  [per_device(): inside = lax.ppermute(slab[0], 'joined', twin)]
  transfers between devices with their start and end apart: 18 -> 18, of which waited for: 6 -> 5; matrix products, arithmetic and copies ran while one was open for 0% -> 0% of each run, Pallas kernels for 35% -> 32%
where the time goes in v7:
time: 67.7 us; the launch traced here: 67.5 us
  Pallas kernels  26.3 us (39%)
  starting transfers between devices  25.4 us (38%)
  waiting for transfers between devices  15.5 us (23%)
    ppermute x6, waiting for transfers between devices, view_send(): sent.append(lax.ppermute(x, 'view', [(p, q) for p, q in pairs if p != q]))  9.03 us
    ppermute x4, starting transfers between devices, pair_send(): lax.ppermute(x, 'view', [(p, p ^ 1) for p in range(size)])  7.76 us
    ppermute x6, starting transfers between devices, view_send(): sent.append(lax.ppermute(x, 'view', [(p, q) for p, q in pairs if p != q]))  7.17 us
    pallas_call x3, Pallas kernels, pack(): pl.pallas_call(functools.partial(pack_kernel, starts, pieces, len(ins) +...  5.9 us
    pallas_call x2, Pallas kernels, edges(): pl.pallas_call(functools.partial(edge_kernel, radius, tile, is_first, is_...  5.28 us
    pallas_call x1, Pallas kernels, forward(): pl.pallas_call(functools.partial(forward_kernel, radius, cut, names), gri...  5.01 us
    ppermute x2, starting transfers between devices, per_device(): across = lax.ppermute(across, 'joined', other)  4.63 us
    pallas_call x1, Pallas kernels, prepare(): pl.pallas_call(functools.partial(prepare_kernel, radius, names), grid_spe...  4.38 us
  transfers between devices with their start and end apart: 18, of which 5 were waited for; matrix products, arithmetic and copies ran while one was open for 0% of the time, Pallas kernels for 32%

profile of v7, /device:TPU:0, one launch (start us, length us, event | category | flops | bytes accessed | tf_op | source)
XLA Modules:
  0.0 67.5 jit_solution(12921690512487355478)
XLA Ops:
  0.0 0.1 stack.47.info.refs_0_.scal
  0.1 1.9 %pack_first.1 = (f32[2,96,1024]{2,1,0:T(8,128)S(1)}, f32[2,96,1024]{2,1,0:T(8,128)S(1)}) custom-call(s32[11]{0:T(128)S(1)} %stack.47.info.refs_0_.scal, f32[4,128,2048]{2,1,0:T(8,128)} %bitcast.24), custom_call_target="tpu_custom_call" | custom-call | bytes 1024 | tf_op jit(solution)/shard_map/pack_first/pallas_call | solution.py:375
  2.0 3.0 %collective-permute-start.2 = (f32[2,96,1024]{2,1,0:T(8,128)S(1)}, f32[2,96,1024]{2,1,0:T(8,128)S(1)}, u32[]{:S(2)}, u32[]{:S(2)}) collective-permute-start(f32[2,96,1024]{2,1,0:T(8,128)S(1)} %get-tuple-element.51.refs_2_), channel_id=1, source_target_pairs={{0,2},{1,4},{2,0},{3,6},{4,1},{5,7},{6,3},{7,5},{8,10},{9,12},{10,... | collective-permute-start | bytes 2359304 | tf_op jit(solution)/shard_map/ppermute | solution.py:614
  5.0 0.7 %collective-permute-start.3 = (f32[2,96,1024]{2,1,0:T(8,128)S(1)}, f32[2,96,1024]{2,1,0:T(8,128)S(1)}, u32[]{:S(2)}, u32[]{:S(2)}) collective-permute-start(f32[2,96,1024]{2,1,0:T(8,128)S(1)} %get-tuple-element.56.refs_2_), channel_id=1, source_target_pairs={{1,6},{3,4},{4,3},{6,1},{9,14},{11,12},{12,11},{14,9},{17,22},{19,... | collective-permute-start | bytes 2359304 | tf_op jit(solution)/shard_map/ppermute | solution.py:614
  5.7 1.7 %pack_slab.1 = (f32[48,2048]{1,0:T(8,128)S(1)}, f32[48,2048]{1,0:T(8,128)S(1)}) custom-call(s32[11]{0:T(128)S(1)} %stack.47.info.refs_0_.scal, f32[128,2048]{1,0:T(8,128)} %bitcast.16, f32[2,96,1024]{2,1,0:T(8,128)S(1)} %get-tuple-element.51.refs_2_), custom_call_target="tpu_custom_call" | custom-call | bytes 1024 | tf_op jit(solution)/shard_map/pack_slab/pallas_call | solution.py:375
  7.4 3.7 %collective-permute-start.4 = (f32[48,2048]{1,0:T(8,128)S(1)}, f32[48,2048]{1,0:T(8,128)S(1)}, u32[]{:S(2)}, u32[]{:S(2)}) collective-permute-start(f32[48,2048]{1,0:T(8,128)S(1)} %get-tuple-element.59), channel_id=1, source_target_pairs={{0,24},{8,16},{16,8},{24,0},{1,25},{9,17},{17,9},{25,1},{2,26},{10... | collective-permute-start | bytes 1179656 | tf_op jit(solution)/shard_map/ppermute | solution.py:635
  11.1 0.0 copy-start
  11.1 0.0 copy-start.1
  11.1 0.0 copy-start.2
  11.1 0.0 copy-start.3
  11.1 0.1 collective-permute-start.5
  11.2 2.3 %pack_second.1 = (f32[2,96,1024]{2,1,0:T(8,128)S(1)}, f32[2,96,1024]{2,1,0:T(8,128)S(1)}, f32[2,32,2048]{2,1,0:T(8,128)S(1)}, f32[2,32,2048]{2,1,0:T(8,128)S(1)}) custom-call(s32[11]{0:T(128)S(1)} %stack.47.info.refs_0_.scal, f32[4,128,2048]{2,1,0:T(8,128)} %bitcast.25, f32[48,2048]{1,0:T(8,128)S(1)} %get-tuple-element.52.refs_2_), custom_call_target="tpu_custom_call" | custom-call | bytes 1024 | tf_op jit(solution)/shard_map/pack_second/pallas_call | solution.py:375
  13.5 0.6 collective-permute-start.6
  14.1 6.5 %collective-permute-done.2.refs_0_ = f32[2,96,1024]{2,1,0:T(8,128)S(1)} collective-permute-done((f32[2,96,1024]{2,1,0:T(8,128)S(1)}, f32[2,96,1024]{2,1,0:T(8,128)S(1)}, u32[]{:S(2)}, u32[]{:S(2)}) %collective-permute-start.2) | collective-permute-done | bytes 786464 | tf_op jit(solution)/shard_map/ppermute | solution.py:614
  20.6 0.7 %collective-permute-start.7 = (f32[2,96,1024]{2,1,0:T(8,128)S(1)}, f32[2,96,1024]{2,1,0:T(8,128)S(1)}, u32[]{:S(2)}, u32[]{:S(2)}) collective-permute-start(f32[2,96,1024]{2,1,0:T(8,128)S(1)} %get-tuple-element.67.refs_2_), channel_id=1, source_target_pairs={{1,6},{3,4},{4,3},{6,1},{9,14},{11,12},{12,11},{14,9},{17,22},{19,... | collective-permute-start | bytes 2359304 | tf_op jit(solution)/shard_map/ppermute | solution.py:614
  21.3 0.0 copy-done
  21.3 0.0 copy-done.1
  21.3 0.0 copy-done.2
  21.4 0.0 copy-done.3
  21.4 4.4 %prepare.1 = (f32[4,32,2048]{2,1,0:T(8,128)S(1)}, bf16[4,192,224]{2,1,0:T(8,128)(2,1)S(1)}, bf16[4,256,256]{2,1,0:T(8,128)(2,1)S(1)}, bf16[4,128,256]{2,1,0:T(8,...) custom-call(s32[11]{0:T(128)S(1)} %stack.47.info.refs_0_.scal, ...), custom_call_target="tpu_custom_call" | custom-call | bytes 1024 | tf_op jit(solution)/shard_map/prepare/pallas_call | solution.py:436
  25.7 0.0 collective-permute-done.3.refs_1_
  25.8 0.7 pair.3
  26.4 0.0 collective-permute-done.4.across
  26.4 3.3 %collective-permute-done.5.inside = f32[48,2048]{1,0:T(8,128)S(1)} collective-permute-done((f32[48,2048]{1,0:T(8,128)S(1)}, f32[48,2048]{1,0:T(8,128)S(1)}, u32[]{:S(2)}, u32[]{:S(2)}) %collective-permute-start.5) | collective-permute-done | bytes 393248 | tf_op jit(solution)/shard_map/ppermute | solution.py:636
  29.7 0.4 collective-permute-start.8
  30.2 0.1 collective-permute-start.9
  30.2 5.0 %forward.1 = (f32[4,96,1024]{2,1,0:T(8,128)S(1)}, f32[4,96,1024]{2,1,0:T(8,128)S(1)}) custom-call(s32[11]{0:T(128)S(1)} %stack.47.info.refs_0_.scal, s32[2,4]{1,0:T(2,128)S(1)} %bitcast.21, f32[128,2048]{1,0:T(8,128)S(1)} %bitcast.18, f32[48,2048]{1,0:T(8,128)S(1)} %collective-permute-done.4.across, f32[48,2048]{1,0:T(8,128)S(1)} %collective-permute-done.5.inside, ...), custom_call_target="tpu_custom_call" | custom-call | bytes 1024 | tf_op jit(solution)/shard_map/forward/pallas_call | solution.py:464
  35.3 0.0 collective-permute-done.8.rest_2_
  35.3 0.0 collective-permute-done.9.rest_3_
  35.3 2.5 %edges.2 = (f32[128,896]{1,0:T(8,128)S(1)}, f32[48,896]{1,0:T(8,128)S(1)}, f32[48,896]{1,0:T(8,128)S(1)}, f32[4,96,128]{2,1,0:T(8,128)S(1)}, f32[4,96,128]{2,1,0:T(8,128)S(1)}) custom-call(s32[11]{0:T(128)S(1)} %stack.47.info.refs_0_.scal, bf16[4,256,256]{2,1,0:T(8,128)(2,1)S(1)} %get-tuple-element.47.by, bf16[4,128,256]{2,1,0:T(8,128)(2,1)S(1)} %get-tuple-element.48.by_low, ...), custom_call_target="tpu_custom_call" | custom-call | bytes 1024 | tf_op jit(solution)/shard_map/edges/pallas_call | solution.py:497
  37.8 0.0 collective-permute-done.6.refs_0_
  37.8 0.0 collective-permute-done.7.refs_1_
  37.8 0.7 pair.4
  38.5 2.7 %collective-permute-start.10 = (f32[96,2048]{1,0:T(8,128)S(1)}, f32[96,2048]{1,0:T(8,128)S(1)}, u32[]{:S(2)}, u32[]{:S(2)}) collective-permute-start(f32[96,2048]{1,0:T(8,128)S(1)} %get-tuple-element.76), channel_id=1, source_target_pairs={{0,1},{1,0},{2,3},{3,2},{4,5},{5,4},{6,7},{7,6},{8,9},{9,8},{10,11... | collective-permute-start | bytes 2359304 | tf_op jit(solution)/shard_map/ppermute | solution.py:619
  41.2 1.5 %collective-permute-start = (f32[2,32,2048]{2,1,0:T(8,128)S(1)}, f32[2,32,2048]{2,1,0:T(8,128)S(1)}, u32[]{:S(2)}, u32[]{:S(2)}) collective-permute-start(f32[2,32,2048]{2,1,0:T(8,128)S(1)} %get-tuple-element.53), channel_id=1, source_target_pairs={{0,2},{1,4},{2,0},{3,6},{4,1},{5,7},{6,3},{7,5},{8,10},{9,12},{10,... | collective-permute-start | bytes 1572872 | tf_op jit(solution)/shard_map/ppermute | solution.py:614
  42.7 0.7 %collective-permute-start.1 = (f32[2,32,2048]{2,1,0:T(8,128)S(1)}, f32[2,32,2048]{2,1,0:T(8,128)S(1)}, u32[]{:S(2)}, u32[]{:S(2)}) collective-permute-start(f32[2,32,2048]{2,1,0:T(8,128)S(1)} %get-tuple-element.54.refs_2_), channel_id=1, source_target_pairs={{1,6},{3,4},{4,3},{6,1},{9,14},{11,12},{12,11},{14,9},{17,22},{19,... | collective-permute-start | bytes 1572872 | tf_op jit(solution)/shard_map/ppermute | solution.py:614
  43.4 3.7 %collective-permute-start.14 = (f32[48,896]{1,0:T(8,128)S(1)}, f32[48,896]{1,0:T(8,128)S(1)}, u32[]{:S(2)}, u32[]{:S(2)}) collective-permute-start(f32[48,896]{1,0:T(8,128)S(1)} %get-tuple-element.85), channel_id=1, source_target_pairs={{0,24},{8,16},{16,8},{24,0},{1,25},{9,17},{17,9},{25,1},{2,26},{10... | collective-permute-start | bytes 516104 | tf_op jit(solution)/shard_map/ppermute | solution.py:664
  47.0 0.0 collective-permute-start.15
  47.0 0.0 collective-permute-done.10.rest_2_
  47.0 2.7 %edges.3 = (f32[128,1152]{1,0:T(8,128)S(1)}, f32[48,1152]{1,0:T(8,128)S(1)}, f32[48,1152]{1,0:T(8,128)S(1)}) custom-call(s32[11]{0:T(128)S(1)} %stack.47.info.refs_0_.scal, bf16[4,256,256]{2,1,0:T(8,128)(2,1)S(1)} %get-tuple-element.47.by, bf16[4,128,256]{2,1,0:T(8,128)(2,1)S(1)} %get-tuple-element.48.by_low, bf16[448,512]{1,0:T(8,128)(2,1)S(1)} %get-tuple-element.55.bx, ...), custom_call_target="tpu_custom_call" | custom-call | bytes 1024 | tf_op jit(solution)/shard_map/edges/pallas_call | solution.py:497
  49.8 1.0 %collective-permute-start.16 = (f32[48,1152]{1,0:T(8,128)S(1)}, f32[48,1152]{1,0:T(8,128)S(1)}, u32[]{:S(2)}, u32[]{:S(2)}) collective-permute-start(f32[48,1152]{1,0:T(8,128)S(1)} %get-tuple-element.87), channel_id=1, source_target_pairs={{0,24},{8,16},{16,8},{24,0},{1,25},{9,17},{17,9},{25,1},{2,26},{10... | collective-permute-start | bytes 663560 | tf_op jit(solution)/shard_map/ppermute | solution.py:671
  50.8 2.5 %collective-permute-done.refs_0_ = f32[2,32,2048]{2,1,0:T(8,128)S(1)} collective-permute-done((f32[2,32,2048]{2,1,0:T(8,128)S(1)}, f32[2,32,2048]{2,1,0:T(8,128)S(1)}, u32[]{:S(2)}, u32[]{:S(2)}) %collective-permute-start) | collective-permute-done | bytes 524320 | tf_op jit(solution)/shard_map/ppermute | solution.py:614
  53.2 1.6 %collective-permute-start.17 = (f32[48,1152]{1,0:T(8,128)S(1)}, f32[48,1152]{1,0:T(8,128)S(1)}, u32[]{:S(2)}, u32[]{:S(2)}) collective-permute-start(f32[48,1152]{1,0:T(8,128)S(1)} %get-tuple-element.88), channel_id=1, source_target_pairs={{0,8},{8,0},{16,24},{24,16},{1,9},{9,1},{17,25},{25,17},{2,10},{10... | collective-permute-start | bytes 663560 | tf_op jit(solution)/shard_map/ppermute | solution.py:672
  54.8 0.0 collective-permute-done.1.refs_1_
  54.8 0.6 pair.5
  55.4 1.9 %collective-permute-start.11 = (f32[32,1408]{1,0:T(8,128)S(1)}, f32[32,1408]{1,0:T(8,128)S(1)}, u32[]{:S(2)}, u32[]{:S(2)}) collective-permute-start(f32[32,1408]{1,0:T(8,128)S(1)} %get-tuple-element.82), channel_id=1, source_target_pairs={{0,1},{1,0},{2,3},{3,2},{4,5},{5,4},{6,7},{7,6},{8,9},{9,8},{10,11... | collective-permute-start | bytes 540680 | tf_op jit(solution)/shard_map/ppermute | solution.py:619
  57.3 0.0 collective-permute-done.14.rest_7_
  57.3 0.1 collective-permute-start.13
  57.4 0.0 collective-permute-done.15.rest_8_
  57.4 3.1 %collective-permute-start.12 = (f32[32,1280]{1,0:T(8,128)S(1)}, f32[32,1280]{1,0:T(8,128)S(1)}, u32[]{:S(2)}, u32[]{:S(2)}) collective-permute-start(f32[32,1280]{1,0:T(8,128)S(1)} %get-tuple-element.83), channel_id=1, source_target_pairs={{0,1},{1,0},{2,3},{3,2},{4,5},{5,4},{6,7},{7,6},{8,9},{9,8},{10,11... | collective-permute-start | bytes 491528 | tf_op jit(solution)/shard_map/ppermute | solution.py:619
  60.5 1.0 %collective-permute-done.12.rest_3_ = f32[32,1280]{1,0:T(8,128)S(1)} collective-permute-done((f32[32,1280]{1,0:T(8,128)S(1)}, f32[32,1280]{1,0:T(8,128)S(1)}, u32[]{:S(2)}, u32[]{:S(2)}) %collective-permute-start.12) | collective-permute-done | bytes 163872 | tf_op jit(solution)/shard_map/ppermute | solution.py:619
  61.6 0.0 collective-permute-done.11.rest_2_
  61.6 0.0 collective-permute-done.13.rest_4_
  61.6 1.9 %middle.1.total = f32[128,2048]{1,0:T(8,128)S(1)} custom-call(s32[11]{0:T(128)S(1)} %stack.47.info.refs_0_.scal, bf16[4,256,256]{2,1,0:T(8,128)(2,1)S(1)} %get-tuple-element.47.by, bf16[4,128,256]{2,1,0:T(8,128)(2,1)S(1)} %get-tuple-element.48.by_low, bf16[4,256,128]{2,1,0:T(8,128)(2,1)S(1)} %get-tuple-element.49.bm, ...), custom_call_target="tpu_custom_call" | custom-call | bytes 1024 | tf_op jit(solution)/shard_map/middle/pallas_call | solution.py:521
  63.4 0.0 collective-permute-done.16.across
  63.5 2.1 %collective-permute-done.17.inside = f32[48,1152]{1,0:T(8,128)S(1)} collective-permute-done((f32[48,1152]{1,0:T(8,128)S(1)}, f32[48,1152]{1,0:T(8,128)S(1)}, u32[]{:S(2)}, u32[]{:S(2)}) %collective-permute-start.17) | collective-permute-done | bytes 221216 | tf_op jit(solution)/shard_map/ppermute | solution.py:672
  65.6 1.9 %update.1 = f32[128,2048]{1,0:T(8,128)} custom-call(s32[11]{0:T(128)S(1)} %stack.47.info.refs_0_.scal, s32[2,4]{1,0:T(2,128)S(1)} %bitcast.22, f32[128,2048]{1,0:T(8,128)S(1)} %middle.1.total, f32[128,2048]{1,0:T(8,128)S(1)} %bitcast.19, f32[48,1152]{1,0:T(8,128)S(1)} %collective-permute-done.16.across, f32[48,1152]{1,0:T(8,128)S(1)} %collective-permute-done.17.inside), custom_call_target="tpu_custom_call" | custom-call | bytes 1024 | tf_op jit(solution)/shard_map/update/pallas_call | solution.py:543
Async XLA Ops:
  2.0 18.6 %collective-permute-start.2 = (f32[2,96,1024]{2,1,0:T(8,128)S(1)}, f32[2,96,1024]{2,1,0:T(8,128)S(1)}, u32[]{:S(2)}, u32[]{:S(2)}) collective-permute-start(f32[2,96,1024]{2,1,0:T(8,128)S(1)} %get-tuple-element.51.refs_2_), channel_id=1, source_target_pairs={{0,2},{1,4},{2,0},{3,6},{4,1},{5,7},{6,3},{7,5},{8,10},{9,12},{10,... | collective-permute-start | bytes 2359304 | tf_op jit(solution)/shard_map/ppermute | solution.py:614
  5.0 20.7 %collective-permute-start.3 = (f32[2,96,1024]{2,1,0:T(8,128)S(1)}, f32[2,96,1024]{2,1,0:T(8,128)S(1)}, u32[]{:S(2)}, u32[]{:S(2)}) collective-permute-start(f32[2,96,1024]{2,1,0:T(8,128)S(1)} %get-tuple-element.56.refs_2_), channel_id=1, source_target_pairs={{1,6},{3,4},{4,3},{6,1},{9,14},{11,12},{12,11},{14,9},{17,22},{19,... | collective-permute-start | bytes 2359304 | tf_op jit(solution)/shard_map/ppermute | solution.py:614
  7.4 19.0 %collective-permute-start.4 = (f32[48,2048]{1,0:T(8,128)S(1)}, f32[48,2048]{1,0:T(8,128)S(1)}, u32[]{:S(2)}, u32[]{:S(2)}) collective-permute-start(f32[48,2048]{1,0:T(8,128)S(1)} %get-tuple-element.59), channel_id=1, source_target_pairs={{0,24},{8,16},{16,8},{24,0},{1,25},{9,17},{17,9},{25,1},{2,26},{10... | collective-permute-start | bytes 1179656 | tf_op jit(solution)/shard_map/ppermute | solution.py:635
  11.1 10.2 %copy-start = (f32[1,128,2048]{2,1,0:T(8,128)S(1)}, f32[1,128,2048]{2,1,0:T(8,128)}, u32[]{:S(2)}) copy-start(f32[1,128,2048]{2,1,0:T(8,128)} %param.5) | copy-start | bytes 3145732
  11.1 10.2 %copy-start.1 = (s32[4,2]{0,1:T(2,128)S(1)}, s32[4,2]{0,1:T(2,128)}, u32[]{:S(2)}) copy-start(s32[4,2]{0,1:T(2,128)} %param.9) | copy-start | bytes 100
  11.1 10.2 %copy-start.2 = (f32[4,2,65]{2,1,0:T(2,128)S(1)}, f32[4,2,65]{2,1,0:T(2,128)}, u32[]{:S(2)}) copy-start(f32[4,2,65]{2,1,0:T(2,128)} %psf.1) | copy-start | bytes 6244
  11.1 10.3 %copy-start.3 = (s32[4,2]{0,1:T(2,128)S(1)}, s32[4,2]{0,1:T(2,128)}, u32[]{:S(2)}) copy-start(s32[4,2]{0,1:T(2,128)} %param.8) | copy-start | bytes 100
  11.1 18.6 %collective-permute-start.5 = (f32[48,2048]{1,0:T(8,128)S(1)}, f32[48,2048]{1,0:T(8,128)S(1)}, u32[]{:S(2)}, u32[]{:S(2)}) collective-permute-start(f32[48,2048]{1,0:T(8,128)S(1)} %get-tuple-element.52.refs_2_), channel_id=1, source_target_pairs={{0,8},{8,0},{16,24},{24,16},{1,9},{9,1},{17,25},{25,17},{2,10},{10... | collective-permute-start | bytes 1179656 | tf_op jit(solution)/shard_map/ppermute | solution.py:636
  13.5 24.3 %collective-permute-start.6 = (f32[2,96,1024]{2,1,0:T(8,128)S(1)}, f32[2,96,1024]{2,1,0:T(8,128)S(1)}, u32[]{:S(2)}, u32[]{:S(2)}) collective-permute-start(f32[2,96,1024]{2,1,0:T(8,128)S(1)} %get-tuple-element.66), channel_id=1, source_target_pairs={{0,2},{1,4},{2,0},{3,6},{4,1},{5,7},{6,3},{7,5},{8,10},{9,12},{10,... | collective-permute-start | bytes 2359304 | tf_op jit(solution)/shard_map/ppermute | solution.py:614
  20.6 17.2 %collective-permute-start.7 = (f32[2,96,1024]{2,1,0:T(8,128)S(1)}, f32[2,96,1024]{2,1,0:T(8,128)S(1)}, u32[]{:S(2)}, u32[]{:S(2)}) collective-permute-start(f32[2,96,1024]{2,1,0:T(8,128)S(1)} %get-tuple-element.67.refs_2_), channel_id=1, source_target_pairs={{1,6},{3,4},{4,3},{6,1},{9,14},{11,12},{12,11},{14,9},{17,22},{19,... | collective-permute-start | bytes 2359304 | tf_op jit(solution)/shard_map/ppermute | solution.py:614
  29.7 5.5 %collective-permute-start.8 = (f32[96,1024]{1,0:T(8,128)S(1)}, f32[96,1024]{1,0:T(8,128)S(1)}, u32[]{:S(2)}, u32[]{:S(2)}) collective-permute-start(f32[96,1024]{1,0:T(8,128)S(1)} %get-tuple-element.71), channel_id=1, source_target_pairs={{0,1},{1,0},{2,3},{3,2},{4,5},{5,4},{6,7},{7,6},{8,9},{9,8},{10,11... | collective-permute-start | bytes 1179656 | tf_op jit(solution)/shard_map/ppermute | solution.py:657
  30.2 5.1 %collective-permute-start.9 = (f32[96,1024]{1,0:T(8,128)S(1)}, f32[96,1024]{1,0:T(8,128)S(1)}, u32[]{:S(2)}, u32[]{:S(2)}) collective-permute-start(f32[96,1024]{1,0:T(8,128)S(1)} %get-tuple-element.72), channel_id=1, source_target_pairs={{0,1},{1,0},{2,3},{3,2},{4,5},{5,4},{6,7},{7,6},{8,9},{9,8},{10,11... | collective-permute-start | bytes 1179656 | tf_op jit(solution)/shard_map/ppermute | solution.py:657
  38.5 8.5 %collective-permute-start.10 = (f32[96,2048]{1,0:T(8,128)S(1)}, f32[96,2048]{1,0:T(8,128)S(1)}, u32[]{:S(2)}, u32[]{:S(2)}) collective-permute-start(f32[96,2048]{1,0:T(8,128)S(1)} %get-tuple-element.76), channel_id=1, source_target_pairs={{0,1},{1,0},{2,3},{3,2},{4,5},{5,4},{6,7},{7,6},{8,9},{9,8},{10,11... | collective-permute-start | bytes 2359304 | tf_op jit(solution)/shard_map/ppermute | solution.py:619
  41.2 12.0 %collective-permute-start = (f32[2,32,2048]{2,1,0:T(8,128)S(1)}, f32[2,32,2048]{2,1,0:T(8,128)S(1)}, u32[]{:S(2)}, u32[]{:S(2)}) collective-permute-start(f32[2,32,2048]{2,1,0:T(8,128)S(1)} %get-tuple-element.53), channel_id=1, source_target_pairs={{0,2},{1,4},{2,0},{3,6},{4,1},{5,7},{6,3},{7,5},{8,10},{9,12},{10,... | collective-permute-start | bytes 1572872 | tf_op jit(solution)/shard_map/ppermute | solution.py:614
  42.7 12.1 %collective-permute-start.1 = (f32[2,32,2048]{2,1,0:T(8,128)S(1)}, f32[2,32,2048]{2,1,0:T(8,128)S(1)}, u32[]{:S(2)}, u32[]{:S(2)}) collective-permute-start(f32[2,32,2048]{2,1,0:T(8,128)S(1)} %get-tuple-element.54.refs_2_), channel_id=1, source_target_pairs={{1,6},{3,4},{4,3},{6,1},{9,14},{11,12},{12,11},{14,9},{17,22},{19,... | collective-permute-start | bytes 1572872 | tf_op jit(solution)/shard_map/ppermute | solution.py:614
  43.4 14.0 %collective-permute-start.14 = (f32[48,896]{1,0:T(8,128)S(1)}, f32[48,896]{1,0:T(8,128)S(1)}, u32[]{:S(2)}, u32[]{:S(2)}) collective-permute-start(f32[48,896]{1,0:T(8,128)S(1)} %get-tuple-element.85), channel_id=1, source_target_pairs={{0,24},{8,16},{16,8},{24,0},{1,25},{9,17},{17,9},{25,1},{2,26},{10... | collective-permute-start | bytes 516104 | tf_op jit(solution)/shard_map/ppermute | solution.py:664
  47.0 10.4 %collective-permute-start.15 = (f32[48,896]{1,0:T(8,128)S(1)}, f32[48,896]{1,0:T(8,128)S(1)}, u32[]{:S(2)}, u32[]{:S(2)}) collective-permute-start(f32[48,896]{1,0:T(8,128)S(1)} %get-tuple-element.86), channel_id=1, source_target_pairs={{0,8},{8,0},{16,24},{24,16},{1,9},{9,1},{17,25},{25,17},{2,10},{10... | collective-permute-start | bytes 516104 | tf_op jit(solution)/shard_map/ppermute | solution.py:665
  49.8 13.7 %collective-permute-start.16 = (f32[48,1152]{1,0:T(8,128)S(1)}, f32[48,1152]{1,0:T(8,128)S(1)}, u32[]{:S(2)}, u32[]{:S(2)}) collective-permute-start(f32[48,1152]{1,0:T(8,128)S(1)} %get-tuple-element.87), channel_id=1, source_target_pairs={{0,24},{8,16},{16,8},{24,0},{1,25},{9,17},{17,9},{25,1},{2,26},{10... | collective-permute-start | bytes 663560 | tf_op jit(solution)/shard_map/ppermute | solution.py:671
  53.2 12.3 %collective-permute-start.17 = (f32[48,1152]{1,0:T(8,128)S(1)}, f32[48,1152]{1,0:T(8,128)S(1)}, u32[]{:S(2)}, u32[]{:S(2)}) collective-permute-start(f32[48,1152]{1,0:T(8,128)S(1)} %get-tuple-element.88), channel_id=1, source_target_pairs={{0,8},{8,0},{16,24},{24,16},{1,9},{9,1},{17,25},{25,17},{2,10},{10... | collective-permute-start | bytes 663560 | tf_op jit(solution)/shard_map/ppermute | solution.py:672
  55.4 6.1 %collective-permute-start.11 = (f32[32,1408]{1,0:T(8,128)S(1)}, f32[32,1408]{1,0:T(8,128)S(1)}, u32[]{:S(2)}, u32[]{:S(2)}) collective-permute-start(f32[32,1408]{1,0:T(8,128)S(1)} %get-tuple-element.82), channel_id=1, source_target_pairs={{0,1},{1,0},{2,3},{3,2},{4,5},{5,4},{6,7},{7,6},{8,9},{9,8},{10,11... | collective-permute-start | bytes 540680 | tf_op jit(solution)/shard_map/ppermute | solution.py:619
  57.3 4.2 %collective-permute-start.13 = (f32[32,1408]{1,0:T(8,128)S(1)}, f32[32,1408]{1,0:T(8,128)S(1)}, u32[]{:S(2)}, u32[]{:S(2)}) collective-permute-start(f32[32,1408]{1,0:T(8,128)S(1)} %get-tuple-element.84), channel_id=1, source_target_pairs={{0,1},{1,0},{2,3},{3,2},{4,5},{5,4},{6,7},{7,6},{8,9},{9,8},{10,11... | collective-permute-start | bytes 540680 | tf_op jit(solution)/shard_map/ppermute | solution.py:619
  57.4 4.1 %collective-permute-start.12 = (f32[32,1280]{1,0:T(8,128)S(1)}, f32[32,1280]{1,0:T(8,128)S(1)}, u32[]{:S(2)}, u32[]{:S(2)}) collective-permute-start(f32[32,1280]{1,0:T(8,128)S(1)} %get-tuple-element.83), channel_id=1, source_target_pairs={{0,1},{1,0},{2,3},{3,2},{4,5},{5,4},{6,7},{7,6},{8,9},{9,8},{10,11... | collective-permute-start | bytes 491528 | tf_op jit(solution)/shard_map/ppermute | solution.py:619
